TPU v7x, 1024 devices: a whole 4x8x16 slice. The times are simulated.
1024 devices in a mesh: dp: 128 (over x, z, core), tensor: 8 (over y).
Axes of the slice: x: 4, y: 8, z: 16, core: 2. Of those that a mesh axis runs over, the one named last changes fastest.
Arguments:
- q_ctx: bfloat16 [16384, 4096], P('dp', 'tensor'), may hold values from -0.119628906 to 0.119628906
- p_ctx: bfloat16 [2048, 4096], P('dp', 'tensor'), may hold values from -0.119628906 to 0.119628906
- out_weight: bfloat16 [4096, 4096], P('tensor'), may hold values from -0.09375 to 0.09375
- neighbours: int32 [128, 8], P('dp'), may hold values from 0 to 127, as said below
- positive: int32 [16384], P('dp'), may hold values from 0 to 127
Outputs:
- q_grad: bfloat16 [16384, 4096], P('dp', 'tensor')
- p_grad: bfloat16 [2048, 4096], P('dp', 'tensor')
- losses: float32 [16384], P('dp')
Inputs may be any that keep to these rules, and one draw needn't show every extreme that they name: `neighbours`: row i lists 8 different blocks: first i itself, then blocks (i + o) mod 128 with 1 <= o <= 14; some row lists the block at distance 14.
All inputs are finite; a program needn't handle non-finite values.
Results may differ from a plain program's by a relative error of at most 0.012.
Values may be sent and summed in bfloat16 or wider, within the bound.
No kernel may reach another device: no remote copies, remote signals or barrier semaphores. Data moves between devices by JAX's collectives and lax.ppermute only.
A program may use at most 32 MiB of HBM per device.

v0:
```python
import jax
import jax.numpy as jnp
from jax import lax
from jax.sharding import PartitionSpec as P

SCALE = 50.0
EPS = 1e-06


def shifted(value, axis, by):
    peers = lax.axis_size(axis)
    return lax.ppermute(value, axis, [(i, (i + by) % peers) for i in range(peers)])


def on_device(q_ctx, p_ctx, out_weight, neighbours, positive):
    q_rows = q_ctx.shape[0]
    p_rows = p_ctx.shape[0]
    width = out_weight.shape[1]
    slice_width = width // lax.axis_size("tensor")
    offset = lax.axis_index("tensor") * slice_width
    ctx = jnp.concatenate([q_ctx, p_ctx], axis=0)
    partial_pre = jnp.dot(ctx, out_weight, preferred_element_type=jnp.float32)
    pre = lax.psum(partial_pre, "tensor")
    norm = jnp.sqrt(jnp.sum(pre * pre, axis=-1, keepdims=True) + EPS)
    emb_full = pre / norm
    emb_slice = lax.dynamic_slice_in_dim(emb_full, offset, slice_width, 1)
    emb_b = emb_slice.astype(jnp.bfloat16)
    q_emb = emb_b[:q_rows]
    p_emb = emb_b[q_rows:]
    listed = neighbours[0]
    count_listed = listed.shape[0]
    dp_count = lax.axis_size("dp")
    reach_most = min(dp_count - 1, 2 * count_listed - 2)
    distance = (listed - lax.axis_index("dp")) % dp_count
    ahead = [p_emb]
    for step in range(1, reach_most + 1):
        ahead.append(shifted(p_emb, "dp", -step))
    stacked = jnp.stack(ahead, axis=0)
    cand = stacked[distance].reshape(count_listed * p_rows, slice_width)
    partial_scores = lax.dot_general(
        q_emb, cand, (((1,), (1,)), ((), ())), preferred_element_type=jnp.float32
    )
    scores = lax.psum(partial_scores, "tensor") * SCALE
    lse = jnp.log(jnp.sum(jnp.exp(scores), axis=-1))
    slots = jnp.arange(count_listed * p_rows, dtype=jnp.int32)
    onehot = (slots[None, :] == positive[:, None]).astype(jnp.float32)
    losses = lse - jnp.sum(scores * onehot, axis=-1)
    dscore = (jnp.exp(scores - lse[:, None]) - onehot).astype(jnp.bfloat16)
    dq = jnp.dot(dscore, cand, preferred_element_type=jnp.float32) * SCALE
    dcand = (
        lax.dot_general(dscore, q_emb, (((0,), (0,)), ((), ())), preferred_element_type=jnp.float32)
        * SCALE
    )
    dcand_blocks = dcand.reshape(count_listed, p_rows, slice_width)
    steps_all = jnp.arange(reach_most + 1, dtype=jnp.int32)
    matches = (steps_all[:, None] == distance[None, :]).astype(jnp.float32)
    outgoing = jnp.einsum("sk,kpf->spf", matches, dcand_blocks, precision=lax.Precision.HIGHEST)
    dpass = outgoing[0]
    for step in range(1, reach_most + 1):
        dpass = dpass + shifted(outgoing[step].astype(jnp.bfloat16), "dp", step).astype(jnp.float32)
    demb = jnp.concatenate([dq, dpass], axis=0).astype(jnp.bfloat16)
    demb_full = lax.all_gather(demb, "tensor", axis=1, tiled=True).astype(jnp.float32)
    inner = jnp.sum(emb_full * demb_full, axis=-1, keepdims=True)
    dpre = ((demb_full - emb_full * inner) / norm).astype(jnp.bfloat16)
    grads = lax.dot_general(
        dpre, out_weight, (((1,), (1,)), ((), ())), preferred_element_type=jnp.float32
    ).astype(jnp.bfloat16)
    return (grads[:q_rows], grads[q_rows:], losses)


def solution(mesh):
    placed = (P("dp", "tensor"), P("dp", "tensor"), P("tensor", None), P("dp", None), P("dp"))
    return jax.shard_map(
        on_device,
        mesh=mesh,
        in_specs=placed,
        out_specs=(P("dp", "tensor"), P("dp", "tensor"), P("dp")),
        check_vma=False,
    )
```

profile of v0, /device:TPU:1, one launch (start us, length us, event | category | flops | bytes accessed | tf_op | source)
XLA Modules:
  0.0 414.5 jit_solution(16882607743942076186)
XLA Ops:
  7.2 4.5 %fusion.11 = f32[144,4096]{1,0:T(8,128)} fusion(bf16[512,4096]{1,0:T(8,128)(2,1)} %param.7, bf16[16,512]{1,0:T(8,128)(2,1)} %param.6, bf16[128,512]{1,0:T(8,128)(2,1)} %param.5), kind=kOutput, calls=%fused_computation.16 | convolution fusion | flops 604274688 | bytes 6701056 | tf_op jit(solution)/shard_map/dot_general | solution.py:22
  11.8 0.6 copy-done.4
  12.4 105.0 %all-reduce.3.cloned.1.call-done = f32[144,4096]{1,0:T(8,128)} async-done(((f32[144,4096]{1,0:T(8,128)}), f32[144,4096]{1,0:T(8,128)}) %all-reduce.3.cloned.1.call-update) | async-done | bytes 2359312 | tf_op jit(solution)/shard_map/psum | solution.py:23
  117.4 2.1 multiply_reduce_fusion
  120.1 6.1 %collective-permute-start = (bf16[16,512]{1,0:T(8,128)(2,1)S(1)}, bf16[16,512]{1,0:T(8,128)(2,1)S(1)}, u32[]{:S(2)}, u32[]{:S(2)}) collective-permute-start(bf16[16,512]{1,0:T(8,128)(2,1)S(1)} %slice.93), channel_id=1, source_target_pairs={{0,1016},{8,0},{16,8},{24,16},{32,24},{40,32},{48,40},{56,48},{64,... | collective-permute-start | bytes 49160 | tf_op jit(solution)/shard_map/ppermute | solution.py:12
  126.3 8.8 %collective-permute-start.1 = (bf16[16,512]{1,0:T(8,128)(2,1)S(1)}, bf16[16,512]{1,0:T(8,128)(2,1)S(1)}, u32[]{:S(2)}, u32[]{:S(2)}) collective-permute-start(bf16[16,512]{1,0:T(8,128)(2,1)S(1)} %slice.93), channel_id=1, source_target_pairs={{0,1008},{8,1016},{16,0},{24,8},{32,16},{40,24},{48,32},{56,40},{6... | collective-permute-start | bytes 49160 | tf_op jit(solution)/shard_map/ppermute | solution.py:12
  135.1 3.2 collective-permute-start.2
  138.2 3.6 collective-permute-start.3
  141.9 5.9 %collective-permute-start.4 = (bf16[16,512]{1,0:T(8,128)(2,1)S(1)}, bf16[16,512]{1,0:T(8,128)(2,1)S(1)}, u32[]{:S(2)}, u32[]{:S(2)}) collective-permute-start(bf16[16,512]{1,0:T(8,128)(2,1)S(1)} %slice.93), channel_id=1, source_target_pairs={{0,984},{8,992},{16,1000},{24,1008},{32,1016},{40,0},{48,8},{56,16... | collective-permute-start | bytes 49160 | tf_op jit(solution)/shard_map/ppermute | solution.py:12
  147.8 2.5 collective-permute-start.5
  150.3 2.1 collective-permute-start.6
  152.5 6.5 %collective-permute-start.7 = (bf16[16,512]{1,0:T(8,128)(2,1)S(1)}, bf16[16,512]{1,0:T(8,128)(2,1)S(1)}, u32[]{:S(2)}, u32[]{:S(2)}) collective-permute-start(bf16[16,512]{1,0:T(8,128)(2,1)S(1)} %slice.93), channel_id=1, source_target_pairs={{0,960},{8,968},{16,976},{24,984},{32,992},{40,1000},{48,1008},{56... | collective-permute-start | bytes 49160 | tf_op jit(solution)/shard_map/ppermute | solution.py:12
  159.0 7.4 %collective-permute-start.8 = (bf16[16,512]{1,0:T(8,128)(2,1)S(1)}, bf16[16,512]{1,0:T(8,128)(2,1)S(1)}, u32[]{:S(2)}, u32[]{:S(2)}) collective-permute-start(bf16[16,512]{1,0:T(8,128)(2,1)S(1)} %slice.93), channel_id=1, source_target_pairs={{0,952},{8,960},{16,968},{24,976},{32,984},{40,992},{48,1000},{56,... | collective-permute-start | bytes 49160 | tf_op jit(solution)/shard_map/ppermute | solution.py:12
  166.4 3.4 collective-permute-start.9
  169.8 2.9 collective-permute-start.10
  172.7 10.1 %collective-permute-start.11 = (bf16[16,512]{1,0:T(8,128)(2,1)S(1)}, bf16[16,512]{1,0:T(8,128)(2,1)S(1)}, u32[]{:S(2)}, u32[]{:S(2)}) collective-permute-start(bf16[16,512]{1,0:T(8,128)(2,1)S(1)} %slice.93), channel_id=1, source_target_pairs={{0,928},{8,936},{16,944},{24,952},{32,960},{40,968},{48,976},{56,9... | collective-permute-start | bytes 49160 | tf_op jit(solution)/shard_map/ppermute | solution.py:12
  182.8 3.8 collective-permute-start.12
  186.7 7.9 %collective-permute-start.13 = (bf16[16,512]{1,0:T(8,128)(2,1)S(1)}, bf16[16,512]{1,0:T(8,128)(2,1)S(1)}, u32[]{:S(2)}, u32[]{:S(2)}) collective-permute-start(bf16[16,512]{1,0:T(8,128)(2,1)S(1)} %slice.93), channel_id=1, source_target_pairs={{0,912},{8,920},{16,928},{24,936},{32,944},{40,952},{48,960},{56,9... | collective-permute-start | bytes 49160 | tf_op jit(solution)/shard_map/ppermute | solution.py:12
  194.8 3.0 collective-permute-done.13
  197.8 0.6 gather_fusion
  198.4 0.8 fusion.16
  199.3 80.0 %all-reduce.5.cloned.1.call-done = f32[128,128]{1,0:T(8,128)} async-done(((f32[128,128]{1,0:T(8,128)}), f32[128,128]{1,0:T(8,128)}) %all-reduce.5.cloned.1.call-update) | async-done | bytes 65552 | tf_op jit(solution)/shard_map/psum | solution.py:43
  279.3 1.1 select_reduce_fusion
  280.4 0.5 log_subtract_fusion
  280.9 1.1 convolution_multiply_fusion
  282.0 0.5 fusion.9
  282.9 8.3 %collective-permute-start.14 = (bf16[16,512]{1,0:T(8,128)(2,1)S(1)}, bf16[16,512]{1,0:T(8,128)(2,1)S(1)}, u32[]{:S(2)}, u32[]{:S(2)}) collective-permute-start(bf16[16,512]{1,0:T(8,128)(2,1)S(1)} %get-tuple-element.7), channel_id=1, source_target_pairs={{0,8},{8,16},{16,24},{24,32},{32,40},{40,48},{48,56},{56,64},{64,7... | collective-permute-start | bytes 49160 | tf_op jit(solution)/shard_map/ppermute | solution.py:12
  291.2 3.3 collective-permute-start.15
  294.5 3.3 collective-permute-start.16
  297.8 5.6 %collective-permute-start.17 = (bf16[16,512]{1,0:T(8,128)(2,1)S(1)}, bf16[16,512]{1,0:T(8,128)(2,1)S(1)}, u32[]{:S(2)}, u32[]{:S(2)}) collective-permute-start(bf16[16,512]{1,0:T(8,128)(2,1)S(1)} %get-tuple-element.18), channel_id=1, source_target_pairs={{0,32},{8,40},{16,48},{24,56},{32,64},{40,72},{48,80},{56,88},{64,... | collective-permute-start | bytes 49160 | tf_op jit(solution)/shard_map/ppermute | solution.py:12
  303.4 7.2 %collective-permute-start.18 = (bf16[16,512]{1,0:T(8,128)(2,1)S(1)}, bf16[16,512]{1,0:T(8,128)(2,1)S(1)}, u32[]{:S(2)}, u32[]{:S(2)}) collective-permute-start(bf16[16,512]{1,0:T(8,128)(2,1)S(1)} %get-tuple-element.17), channel_id=1, source_target_pairs={{0,40},{8,48},{16,56},{24,64},{32,72},{40,80},{48,88},{56,96},{64,... | collective-permute-start | bytes 49160 | tf_op jit(solution)/shard_map/ppermute | solution.py:12
  310.6 2.7 collective-permute-start.19
  313.4 2.7 collective-permute-start.20
  316.1 2.7 collective-permute-start.21
  318.9 9.4 %collective-permute-start.22 = (bf16[16,512]{1,0:T(8,128)(2,1)S(1)}, bf16[16,512]{1,0:T(8,128)(2,1)S(1)}, u32[]{:S(2)}, u32[]{:S(2)}) collective-permute-start(bf16[16,512]{1,0:T(8,128)(2,1)S(1)} %get-tuple-element.13), channel_id=1, source_target_pairs={{0,72},{8,80},{16,88},{24,96},{32,104},{40,112},{48,120},{56,128},... | collective-permute-start | bytes 49160 | tf_op jit(solution)/shard_map/ppermute | solution.py:12
  328.2 5.2 %collective-permute-start.23 = (bf16[16,512]{1,0:T(8,128)(2,1)S(1)}, bf16[16,512]{1,0:T(8,128)(2,1)S(1)}, u32[]{:S(2)}, u32[]{:S(2)}) collective-permute-start(bf16[16,512]{1,0:T(8,128)(2,1)S(1)} %get-tuple-element.12), channel_id=1, source_target_pairs={{0,80},{8,88},{16,96},{24,104},{32,112},{40,120},{48,128},{56,136}... | collective-permute-start | bytes 49160 | tf_op jit(solution)/shard_map/ppermute | solution.py:12
  333.5 2.7 collective-permute-start.24
  336.2 9.1 %collective-permute-start.25 = (bf16[16,512]{1,0:T(8,128)(2,1)S(1)}, bf16[16,512]{1,0:T(8,128)(2,1)S(1)}, u32[]{:S(2)}, u32[]{:S(2)}) collective-permute-start(bf16[16,512]{1,0:T(8,128)(2,1)S(1)} %get-tuple-element.10), channel_id=1, source_target_pairs={{0,96},{8,104},{16,112},{24,120},{32,128},{40,136},{48,144},{56,15... | collective-permute-start | bytes 49160 | tf_op jit(solution)/shard_map/ppermute | solution.py:12
  345.4 6.1 %collective-permute-start.26 = (bf16[16,512]{1,0:T(8,128)(2,1)S(1)}, bf16[16,512]{1,0:T(8,128)(2,1)S(1)}, u32[]{:S(2)}, u32[]{:S(2)}) collective-permute-start(bf16[16,512]{1,0:T(8,128)(2,1)S(1)} %get-tuple-element.9), channel_id=1, source_target_pairs={{0,104},{8,112},{16,120},{24,128},{32,136},{40,144},{48,152},{56,1... | collective-permute-start | bytes 49160 | tf_op jit(solution)/shard_map/ppermute | solution.py:12
  351.5 6.9 %collective-permute-start.27 = (bf16[16,512]{1,0:T(8,128)(2,1)S(1)}, bf16[16,512]{1,0:T(8,128)(2,1)S(1)}, u32[]{:S(2)}, u32[]{:S(2)}) collective-permute-start(bf16[16,512]{1,0:T(8,128)(2,1)S(1)} %get-tuple-element.8), channel_id=1, source_target_pairs={{0,112},{8,120},{16,128},{24,136},{32,144},{40,152},{48,160},{56,1... | collective-permute-start | bytes 49160 | tf_op jit(solution)/shard_map/ppermute | solution.py:12
  358.7 2.1 collective-permute-done.26
  360.8 5.5 %collective-permute-done.27 = bf16[16,512]{1,0:T(8,128)(2,1)S(1)} collective-permute-done((bf16[16,512]{1,0:T(8,128)(2,1)S(1)}, bf16[16,512]{1,0:T(8,128)(2,1)S(1)}, u32[]{:S(2)}, u32[]{:S(2)}) %collective-permute-start.27) | collective-permute-done | bytes 16416 | tf_op jit(solution)/shard_map/ppermute | solution.py:12
  366.3 0.7 pad_maximum_fusion
  367.0 34.1 %all-gather.2.cloned.1.call-done = bf16[144,4096]{1,0:T(8,128)(2,1)} async-done(((bf16[144,512]{1,0:T(8,128)(2,1)}), bf16[144,4096]{1,0:T(8,128)(2,1)}) %all-gather.2.cloned.1.call-update) | async-done | bytes 1179664 | tf_op jit(solution)/shard_map/all_gather | solution.py:62
  401.1 1.8 fusion
  403.0 3.7 fusion.5
  406.7 0.7 slice.109
  407.4 0.6 slice.110
  (66 shorter events, 1.8 us)
Async XLA Ops:
  7.2 110.2 %all-reduce.3.cloned.1.call-start = ((), (), s32[]{:S(2)}) async-start(), calls=%async_computation | async-start | bytes 4718592 | tf_op jit(solution)/shard_map/psum | solution.py:23
  11.7 0.7 copy-start.4
  11.8 267.5 %all-reduce.5.cloned.1.call-start = ((), (), s32[]{:S(2)}) async-start(), calls=%async_computation.1 | async-start | bytes 131072 | tf_op jit(solution)/shard_map/psum | solution.py:43
  117.4 2.4 copy-start
  119.7 159.5 %copy-start.3 = (s32[128]{0:T(128)S(1)}, s32[128]{0:T(128)}, u32[]{:S(2)}) copy-start(s32[128]{0:T(128)} %param.9) | copy-start | bytes 1540
  120.1 27.7 %collective-permute-start = (bf16[16,512]{1,0:T(8,128)(2,1)S(1)}, bf16[16,512]{1,0:T(8,128)(2,1)S(1)}, u32[]{:S(2)}, u32[]{:S(2)}) collective-permute-start(bf16[16,512]{1,0:T(8,128)(2,1)S(1)} %slice.93), channel_id=1, source_target_pairs={{0,1016},{8,0},{16,8},{24,16},{32,24},{40,32},{48,40},{56,48},{64,... | collective-permute-start | bytes 49160 | tf_op jit(solution)/shard_map/ppermute | solution.py:12
  126.3 24.0 %collective-permute-start.1 = (bf16[16,512]{1,0:T(8,128)(2,1)S(1)}, bf16[16,512]{1,0:T(8,128)(2,1)S(1)}, u32[]{:S(2)}, u32[]{:S(2)}) collective-permute-start(bf16[16,512]{1,0:T(8,128)(2,1)S(1)} %slice.93), channel_id=1, source_target_pairs={{0,1008},{8,1016},{16,0},{24,8},{32,16},{40,24},{48,32},{56,40},{6... | collective-permute-start | bytes 49160 | tf_op jit(solution)/shard_map/ppermute | solution.py:12
  135.1 17.4 %collective-permute-start.2 = (bf16[16,512]{1,0:T(8,128)(2,1)S(1)}, bf16[16,512]{1,0:T(8,128)(2,1)S(1)}, u32[]{:S(2)}, u32[]{:S(2)}) collective-permute-start(bf16[16,512]{1,0:T(8,128)(2,1)S(1)} %slice.93), channel_id=1, source_target_pairs={{0,1000},{8,1008},{16,1016},{24,0},{32,8},{40,16},{48,24},{56,32},... | collective-permute-start | bytes 49160 | tf_op jit(solution)/shard_map/ppermute | solution.py:12
  138.2 20.7 %collective-permute-start.3 = (bf16[16,512]{1,0:T(8,128)(2,1)S(1)}, bf16[16,512]{1,0:T(8,128)(2,1)S(1)}, u32[]{:S(2)}, u32[]{:S(2)}) collective-permute-start(bf16[16,512]{1,0:T(8,128)(2,1)S(1)} %slice.93), channel_id=1, source_target_pairs={{0,992},{8,1000},{16,1008},{24,1016},{32,0},{40,8},{48,16},{56,24}... | collective-permute-start | bytes 49160 | tf_op jit(solution)/shard_map/ppermute | solution.py:12
  141.9 24.5 %collective-permute-start.4 = (bf16[16,512]{1,0:T(8,128)(2,1)S(1)}, bf16[16,512]{1,0:T(8,128)(2,1)S(1)}, u32[]{:S(2)}, u32[]{:S(2)}) collective-permute-start(bf16[16,512]{1,0:T(8,128)(2,1)S(1)} %slice.93), channel_id=1, source_target_pairs={{0,984},{8,992},{16,1000},{24,1008},{32,1016},{40,0},{48,8},{56,16... | collective-permute-start | bytes 49160 | tf_op jit(solution)/shard_map/ppermute | solution.py:12
  147.8 21.9 %collective-permute-start.5 = (bf16[16,512]{1,0:T(8,128)(2,1)S(1)}, bf16[16,512]{1,0:T(8,128)(2,1)S(1)}, u32[]{:S(2)}, u32[]{:S(2)}) collective-permute-start(bf16[16,512]{1,0:T(8,128)(2,1)S(1)} %slice.93), channel_id=1, source_target_pairs={{0,976},{8,984},{16,992},{24,1000},{32,1008},{40,1016},{48,0},{56,... | collective-permute-start | bytes 49160 | tf_op jit(solution)/shard_map/ppermute | solution.py:12
  150.3 22.3 %collective-permute-start.6 = (bf16[16,512]{1,0:T(8,128)(2,1)S(1)}, bf16[16,512]{1,0:T(8,128)(2,1)S(1)}, u32[]{:S(2)}, u32[]{:S(2)}) collective-permute-start(bf16[16,512]{1,0:T(8,128)(2,1)S(1)} %slice.93), channel_id=1, source_target_pairs={{0,968},{8,976},{16,984},{24,992},{32,1000},{40,1008},{48,1016},{5... | collective-permute-start | bytes 49160 | tf_op jit(solution)/shard_map/ppermute | solution.py:12
  152.5 30.3 %collective-permute-start.7 = (bf16[16,512]{1,0:T(8,128)(2,1)S(1)}, bf16[16,512]{1,0:T(8,128)(2,1)S(1)}, u32[]{:S(2)}, u32[]{:S(2)}) collective-permute-start(bf16[16,512]{1,0:T(8,128)(2,1)S(1)} %slice.93), channel_id=1, source_target_pairs={{0,960},{8,968},{16,976},{24,984},{32,992},{40,1000},{48,1008},{56... | collective-permute-start | bytes 49160 | tf_op jit(solution)/shard_map/ppermute | solution.py:12
  159.0 27.7 %collective-permute-start.8 = (bf16[16,512]{1,0:T(8,128)(2,1)S(1)}, bf16[16,512]{1,0:T(8,128)(2,1)S(1)}, u32[]{:S(2)}, u32[]{:S(2)}) collective-permute-start(bf16[16,512]{1,0:T(8,128)(2,1)S(1)} %slice.93), channel_id=1, source_target_pairs={{0,952},{8,960},{16,968},{24,976},{32,984},{40,992},{48,1000},{56,... | collective-permute-start | bytes 49160 | tf_op jit(solution)/shard_map/ppermute | solution.py:12
  166.4 28.2 %collective-permute-start.9 = (bf16[16,512]{1,0:T(8,128)(2,1)S(1)}, bf16[16,512]{1,0:T(8,128)(2,1)S(1)}, u32[]{:S(2)}, u32[]{:S(2)}) collective-permute-start(bf16[16,512]{1,0:T(8,128)(2,1)S(1)} %slice.93), channel_id=1, source_target_pairs={{0,944},{8,952},{16,960},{24,968},{32,976},{40,984},{48,992},{56,1... | collective-permute-start | bytes 49160 | tf_op jit(solution)/shard_map/ppermute | solution.py:12
  169.8 24.9 %collective-permute-start.10 = (bf16[16,512]{1,0:T(8,128)(2,1)S(1)}, bf16[16,512]{1,0:T(8,128)(2,1)S(1)}, u32[]{:S(2)}, u32[]{:S(2)}) collective-permute-start(bf16[16,512]{1,0:T(8,128)(2,1)S(1)} %slice.93), channel_id=1, source_target_pairs={{0,936},{8,944},{16,952},{24,960},{32,968},{40,976},{48,984},{56,9... | collective-permute-start | bytes 49160 | tf_op jit(solution)/shard_map/ppermute | solution.py:12
  172.7 22.0 %collective-permute-start.11 = (bf16[16,512]{1,0:T(8,128)(2,1)S(1)}, bf16[16,512]{1,0:T(8,128)(2,1)S(1)}, u32[]{:S(2)}, u32[]{:S(2)}) collective-permute-start(bf16[16,512]{1,0:T(8,128)(2,1)S(1)} %slice.93), channel_id=1, source_target_pairs={{0,928},{8,936},{16,944},{24,952},{32,960},{40,968},{48,976},{56,9... | collective-permute-start | bytes 49160 | tf_op jit(solution)/shard_map/ppermute | solution.py:12
  182.8 12.0 %collective-permute-start.12 = (bf16[16,512]{1,0:T(8,128)(2,1)S(1)}, bf16[16,512]{1,0:T(8,128)(2,1)S(1)}, u32[]{:S(2)}, u32[]{:S(2)}) collective-permute-start(bf16[16,512]{1,0:T(8,128)(2,1)S(1)} %slice.93), channel_id=1, source_target_pairs={{0,920},{8,928},{16,936},{24,944},{32,952},{40,960},{48,968},{56,9... | collective-permute-start | bytes 49160 | tf_op jit(solution)/shard_map/ppermute | solution.py:12
  186.7 11.1 %collective-permute-start.13 = (bf16[16,512]{1,0:T(8,128)(2,1)S(1)}, bf16[16,512]{1,0:T(8,128)(2,1)S(1)}, u32[]{:S(2)}, u32[]{:S(2)}) collective-permute-start(bf16[16,512]{1,0:T(8,128)(2,1)S(1)} %slice.93), channel_id=1, source_target_pairs={{0,912},{8,920},{16,928},{24,936},{32,944},{40,952},{48,960},{56,9... | collective-permute-start | bytes 49160 | tf_op jit(solution)/shard_map/ppermute | solution.py:12
  199.2 201.9 %all-gather.2.cloned.1.call-start = ((), (), s32[]{:S(2)}) async-start(), calls=%async_computation.2 | async-start | bytes 1327104 | tf_op jit(solution)/shard_map/all_gather | solution.py:62
  279.3 79.1 %copy-start.2 = (f32[128,128]{1,0:T(8,128)S(1)}, f32[128,128]{1,0:T(8,128)}, u32[]{:S(2)}) copy-start(f32[128,128]{1,0:T(8,128)} %all-reduce.5.cloned.1.call-done) | copy-start | bytes 196612
  282.9 27.7 %collective-permute-start.14 = (bf16[16,512]{1,0:T(8,128)(2,1)S(1)}, bf16[16,512]{1,0:T(8,128)(2,1)S(1)}, u32[]{:S(2)}, u32[]{:S(2)}) collective-permute-start(bf16[16,512]{1,0:T(8,128)(2,1)S(1)} %get-tuple-element.7), channel_id=1, source_target_pairs={{0,8},{8,16},{16,24},{24,32},{32,40},{40,48},{48,56},{56,64},{64,7... | collective-permute-start | bytes 49160 | tf_op jit(solution)/shard_map/ppermute | solution.py:12
  291.2 22.1 %collective-permute-start.15 = (bf16[16,512]{1,0:T(8,128)(2,1)S(1)}, bf16[16,512]{1,0:T(8,128)(2,1)S(1)}, u32[]{:S(2)}, u32[]{:S(2)}) collective-permute-start(bf16[16,512]{1,0:T(8,128)(2,1)S(1)} %get-tuple-element.20), channel_id=1, source_target_pairs={{0,16},{8,24},{16,32},{24,40},{32,48},{40,56},{48,64},{56,72},{64,... | collective-permute-start | bytes 49160 | tf_op jit(solution)/shard_map/ppermute | solution.py:12
  294.5 21.6 %collective-permute-start.16 = (bf16[16,512]{1,0:T(8,128)(2,1)S(1)}, bf16[16,512]{1,0:T(8,128)(2,1)S(1)}, u32[]{:S(2)}, u32[]{:S(2)}) collective-permute-start(bf16[16,512]{1,0:T(8,128)(2,1)S(1)} %get-tuple-element.19), channel_id=1, source_target_pairs={{0,24},{8,32},{16,40},{24,48},{32,56},{40,64},{48,72},{56,80},{64,... | collective-permute-start | bytes 49160 | tf_op jit(solution)/shard_map/ppermute | solution.py:12
  297.8 21.0 %collective-permute-start.17 = (bf16[16,512]{1,0:T(8,128)(2,1)S(1)}, bf16[16,512]{1,0:T(8,128)(2,1)S(1)}, u32[]{:S(2)}, u32[]{:S(2)}) collective-permute-start(bf16[16,512]{1,0:T(8,128)(2,1)S(1)} %get-tuple-element.18), channel_id=1, source_target_pairs={{0,32},{8,40},{16,48},{24,56},{32,64},{40,72},{48,80},{56,88},{64,... | collective-permute-start | bytes 49160 | tf_op jit(solution)/shard_map/ppermute | solution.py:12
  303.4 24.8 %collective-permute-start.18 = (bf16[16,512]{1,0:T(8,128)(2,1)S(1)}, bf16[16,512]{1,0:T(8,128)(2,1)S(1)}, u32[]{:S(2)}, u32[]{:S(2)}) collective-permute-start(bf16[16,512]{1,0:T(8,128)(2,1)S(1)} %get-tuple-element.17), channel_id=1, source_target_pairs={{0,40},{8,48},{16,56},{24,64},{32,72},{40,80},{48,88},{56,96},{64,... | collective-permute-start | bytes 49160 | tf_op jit(solution)/shard_map/ppermute | solution.py:12
  310.6 22.9 %collective-permute-start.19 = (bf16[16,512]{1,0:T(8,128)(2,1)S(1)}, bf16[16,512]{1,0:T(8,128)(2,1)S(1)}, u32[]{:S(2)}, u32[]{:S(2)}) collective-permute-start(bf16[16,512]{1,0:T(8,128)(2,1)S(1)} %get-tuple-element.16), channel_id=1, source_target_pairs={{0,48},{8,56},{16,64},{24,72},{32,80},{40,88},{48,96},{56,104},{64... | collective-permute-start | bytes 49160 | tf_op jit(solution)/shard_map/ppermute | solution.py:12
  313.4 22.9 %collective-permute-start.20 = (bf16[16,512]{1,0:T(8,128)(2,1)S(1)}, bf16[16,512]{1,0:T(8,128)(2,1)S(1)}, u32[]{:S(2)}, u32[]{:S(2)}) collective-permute-start(bf16[16,512]{1,0:T(8,128)(2,1)S(1)} %get-tuple-element.15), channel_id=1, source_target_pairs={{0,56},{8,64},{16,72},{24,80},{32,88},{40,96},{48,104},{56,112},{6... | collective-permute-start | bytes 49160 | tf_op jit(solution)/shard_map/ppermute | solution.py:12
  316.1 29.2 %collective-permute-start.21 = (bf16[16,512]{1,0:T(8,128)(2,1)S(1)}, bf16[16,512]{1,0:T(8,128)(2,1)S(1)}, u32[]{:S(2)}, u32[]{:S(2)}) collective-permute-start(bf16[16,512]{1,0:T(8,128)(2,1)S(1)} %get-tuple-element.14), channel_id=1, source_target_pairs={{0,64},{8,72},{16,80},{24,88},{32,96},{40,104},{48,112},{56,120},{... | collective-permute-start | bytes 49160 | tf_op jit(solution)/shard_map/ppermute | solution.py:12
  318.9 32.7 %collective-permute-start.22 = (bf16[16,512]{1,0:T(8,128)(2,1)S(1)}, bf16[16,512]{1,0:T(8,128)(2,1)S(1)}, u32[]{:S(2)}, u32[]{:S(2)}) collective-permute-start(bf16[16,512]{1,0:T(8,128)(2,1)S(1)} %get-tuple-element.13), channel_id=1, source_target_pairs={{0,72},{8,80},{16,88},{24,96},{32,104},{40,112},{48,120},{56,128},... | collective-permute-start | bytes 49160 | tf_op jit(solution)/shard_map/ppermute | solution.py:12
  328.2 30.4 %collective-permute-start.23 = (bf16[16,512]{1,0:T(8,128)(2,1)S(1)}, bf16[16,512]{1,0:T(8,128)(2,1)S(1)}, u32[]{:S(2)}, u32[]{:S(2)}) collective-permute-start(bf16[16,512]{1,0:T(8,128)(2,1)S(1)} %get-tuple-element.12), channel_id=1, source_target_pairs={{0,80},{8,88},{16,96},{24,104},{32,112},{40,120},{48,128},{56,136}... | collective-permute-start | bytes 49160 | tf_op jit(solution)/shard_map/ppermute | solution.py:12
  333.5 25.2 %collective-permute-start.24 = (bf16[16,512]{1,0:T(8,128)(2,1)S(1)}, bf16[16,512]{1,0:T(8,128)(2,1)S(1)}, u32[]{:S(2)}, u32[]{:S(2)}) collective-permute-start(bf16[16,512]{1,0:T(8,128)(2,1)S(1)} %get-tuple-element.11), channel_id=1, source_target_pairs={{0,88},{8,96},{16,104},{24,112},{32,120},{40,128},{48,136},{56,144... | collective-permute-start | bytes 49160 | tf_op jit(solution)/shard_map/ppermute | solution.py:12
  336.2 22.4 %collective-permute-start.25 = (bf16[16,512]{1,0:T(8,128)(2,1)S(1)}, bf16[16,512]{1,0:T(8,128)(2,1)S(1)}, u32[]{:S(2)}, u32[]{:S(2)}) collective-permute-start(bf16[16,512]{1,0:T(8,128)(2,1)S(1)} %get-tuple-element.10), channel_id=1, source_target_pairs={{0,96},{8,104},{16,112},{24,120},{32,128},{40,136},{48,144},{56,15... | collective-permute-start | bytes 49160 | tf_op jit(solution)/shard_map/ppermute | solution.py:12
  345.4 15.4 %collective-permute-start.26 = (bf16[16,512]{1,0:T(8,128)(2,1)S(1)}, bf16[16,512]{1,0:T(8,128)(2,1)S(1)}, u32[]{:S(2)}, u32[]{:S(2)}) collective-permute-start(bf16[16,512]{1,0:T(8,128)(2,1)S(1)} %get-tuple-element.9), channel_id=1, source_target_pairs={{0,104},{8,112},{16,120},{24,128},{32,136},{40,144},{48,152},{56,1... | collective-permute-start | bytes 49160 | tf_op jit(solution)/shard_map/ppermute | solution.py:12
  351.5 14.8 %collective-permute-start.27 = (bf16[16,512]{1,0:T(8,128)(2,1)S(1)}, bf16[16,512]{1,0:T(8,128)(2,1)S(1)}, u32[]{:S(2)}, u32[]{:S(2)}) collective-permute-start(bf16[16,512]{1,0:T(8,128)(2,1)S(1)} %get-tuple-element.8), channel_id=1, source_target_pairs={{0,112},{8,120},{16,128},{24,136},{32,144},{40,152},{48,160},{56,1... | collective-permute-start | bytes 49160 | tf_op jit(solution)/shard_map/ppermute | solution.py:12
  401.1 1.8 copy-start.1
Sparse Core Ops, SparseCore 0:
  11.9 105.4 all-reduce.2
  199.4 79.8 all-reduce.4
  367.2 33.9 all-gather.1
where the time goes:
time: 419 us; the launch traced here: 415 us
  waiting for transfers between devices  230 us (55%)
  starting transfers between devices  150 us (36%)
  between operations  14.4 us (3%)
  matrix products  11 us (3%)
  other arithmetic  6.91 us (2%)
    ppermute x28, starting transfers between devices, shifted(): lax.ppermute(value, axis, [(i, (i + by) % peers) for i in range(peers)])  149 us
    psum x1, waiting for transfers between devices, on_device(): pre = lax.psum(partial_pre, 'tensor')  105 us
    psum x1, waiting for transfers between devices, on_device(): scores = lax.psum(partial_scores, 'tensor') * SCALE  80 us
    all_gather x1, waiting for transfers between devices, on_device(): lax.all_gather(demb, 'tensor', axis=1, tiled=True).astype(jnp.float32)  34.1 us
    ppermute x28, waiting for transfers between devices, shifted(): lax.ppermute(value, axis, [(i, (i + by) % peers) for i in range(peers)])  10.8 us
  transfers between devices with their start and end apart: 31, of which 7 were waited for; matrix products, arithmetic and copies ran while one was open for 0% of the time, Pallas kernels for 0%

commit v1 on v0

v1 whole, which is shorter than its diff:
```python
import jax
import jax.numpy as jnp
from jax import lax
from jax.sharding import Mesh
from jax.sharding import PartitionSpec as P

SCALE = 50.0
EPS = 1e-06
WINDOW = 8
CORES = 2
MEMBERS = ("core", "tensor")
CHIPS = ("w", "zlo")


def shift_chips(value, by):
    chips = lax.axis_size(CHIPS)
    return lax.ppermute(value, CHIPS, [(i, (i + by) % chips) for i in range(chips)])


def halves(value, parts):
    out = []
    for _ in range(parts):
        top = lax.reduce_precision(value, 8, 7)
        out.append(top.astype(jnp.bfloat16))
        value = value - top
    return out


def on_device(q_ctx, p_ctx, out_weight, neighbours, positive):
    f32, bf16 = jnp.float32, jnp.bfloat16
    q_rows, p_rows = q_ctx.shape[0], p_ctx.shape[0]
    listed = neighbours.shape[1]
    slots = listed * p_rows
    tensors = lax.axis_size("tensor")
    members = CORES * tensors
    feats = out_weight.shape[1] // members
    q_part = q_rows // tensors
    core, place = lax.axis_index("core"), lax.axis_index("zlo")

    far_ctx = shift_chips(p_ctx, -WINDOW)
    other = lax.ppermute(neighbours, "core", [(0, 1), (1, 0)])
    lists = jnp.concatenate([neighbours, other], axis=0)
    lists = jnp.where(core == 0, lists, lists[::-1])

    def project(rows):
        part = jnp.dot(rows, out_weight, preferred_element_type=f32).astype(bf16)
        return part.reshape(rows.shape[0], members, feats).transpose(1, 0, 2)

    def reduce_over_tensor(part):
        got = lax.all_to_all(part, MEMBERS, 0, 0)
        got = got.reshape(CORES, tensors, part.shape[1], feats).astype(f32)
        return jnp.sum(got, axis=1).astype(bf16)

    p_pre = reduce_over_tensor(project(jnp.concatenate([p_ctx, far_ctx], axis=0)))
    q_pre = reduce_over_tensor(project(q_ctx))
    near, far = p_pre[:, :p_rows], p_pre[:, p_rows:]

    ids = jnp.arange(WINDOW, dtype=jnp.int32)
    outgoing = jnp.where((ids <= place)[:, None, None, None], near[None], far[None])
    window = lax.all_to_all(outgoing, "zlo", 0, 0).reshape(WINDOW * CORES, p_rows, feats)
    spots = lists % (WINDOW * CORES)
    cand = window[spots].reshape(CORES, slots, feats)

    raw = jnp.einsum("kqf,kcf->kqc", q_pre, cand, preferred_element_type=f32)
    q_sq = jnp.sum(jnp.square(q_pre.astype(f32)), axis=-1)
    c_sq = jnp.sum(jnp.square(cand.astype(f32)), axis=-1)
    q_sq = jnp.pad(q_sq.reshape(CORES, tensors, 1, q_part), ((0, 0), (0, 0), (0, 0), (0, slots - q_part)))
    c_sq = jnp.broadcast_to(c_sq[:, None, None, :], (CORES, tensors, 1, slots))
    extra = jnp.zeros((CORES, tensors, 6, slots), f32)
    sums = jnp.concatenate([raw.reshape(CORES, tensors, q_part, slots), q_sq, c_sq, extra], axis=2)
    sums = lax.all_to_all(sums.reshape(members, q_part + 8, slots), MEMBERS, 0, 0)
    sums = jnp.sum(sums, axis=0)
    raw = sums[:q_part]
    inv_q = lax.rsqrt(sums[q_part, :q_part] + EPS)
    inv_c = lax.rsqrt(sums[q_part + 1] + EPS)

    scores = raw * (SCALE * inv_q)[:, None] * inv_c[None, :]
    lse = jnp.log(jnp.sum(jnp.exp(scores), axis=-1))
    pos = lax.dynamic_slice_in_dim(positive, lax.axis_index("tensor") * q_part, q_part)
    onehot = (jnp.arange(slots, dtype=jnp.int32)[None, :] == pos[:, None]).astype(f32)
    loss = lse - jnp.sum(scores * onehot, axis=-1)
    dscore = jnp.exp(scores - lse[:, None]) - onehot
    coef = lax.reduce_precision(dscore * (SCALE * inv_q)[:, None] * inv_c[None, :], 8, 7)
    weighted = coef * raw
    q_inner = jnp.square(inv_q) * jnp.sum(weighted, axis=-1)
    c_inner = jnp.square(inv_c) * jnp.sum(weighted, axis=0)

    row = jnp.concatenate(halves(q_inner, 2) + halves(loss, 3))
    row = jnp.pad(row, (0, slots - row.shape[0]))
    c_rows = jnp.stack([row] + halves(c_inner, 2) + [jnp.zeros((slots,), bf16)] * 5)
    told = jnp.concatenate([coef.astype(bf16), c_rows], axis=0)
    told = lax.all_to_all(jnp.broadcast_to(told[None], (members,) + told.shape), MEMBERS, 0, 0)
    told = told.reshape(CORES, tensors, q_part + 8, slots)
    coef = told[:, :, :q_part].reshape(CORES, q_rows, slots)
    row = told[:, :, q_part].astype(f32)
    q_inner = (row[..., :q_part] + row[..., q_part : 2 * q_part]).reshape(CORES, q_rows, 1)
    loss = row[..., 2 * q_part : 3 * q_part] + row[..., 3 * q_part : 4 * q_part] + row[..., 4 * q_part : 5 * q_part]
    losses = jnp.where(core == 0, loss[0], loss[1]).reshape(q_rows)
    c_inner = jnp.sum(told[:, :, q_part + 1 : q_part + 3].astype(f32), axis=(1, 2))[..., None]

    dq = jnp.einsum("kqc,kcf->kqf", coef, cand, preferred_element_type=f32)
    dq = (dq - q_inner * q_pre.astype(f32)).astype(bf16)
    dc = jnp.einsum("kqc,kqf->kcf", coef, q_pre, preferred_element_type=f32)
    dc = (dc - c_inner * cand.astype(f32)).astype(bf16)
    match = (jnp.arange(WINDOW * CORES, dtype=jnp.int32)[:, None, None] == spots[None]).astype(bf16)
    dwin = jnp.einsum("wks,kspf->wpf", match, dc.reshape(CORES, listed, p_rows, feats), preferred_element_type=f32)

    back = lax.all_to_all(dwin.astype(bf16).reshape(WINDOW, CORES, p_rows, feats), "zlo", 0, 0).astype(f32)
    mine = (ids <= place)[:, None, None, None]
    near = jnp.sum(jnp.where(mine, back, 0.0), axis=0)
    far = jnp.sum(jnp.where(mine, 0.0, back), axis=0).astype(bf16)
    dp = (near + shift_chips(far, WINDOW).astype(f32)).astype(bf16)

    def gather_features(part):
        part = jnp.broadcast_to(part[:, None], (CORES, tensors) + part.shape[1:])
        return lax.all_to_all(part.reshape((members,) + part.shape[2:]), MEMBERS, 0, 0)

    def unproject(part):
        weight = out_weight.reshape(out_weight.shape[0], members, feats)
        return jnp.einsum("mrf,hmf->rh", part, weight, preferred_element_type=f32).astype(bf16)

    q_grad = unproject(gather_features(dq))
    p_grad = unproject(gather_features(dp))
    return q_grad, p_grad, losses


def solution(mesh):
    dp, tensors = mesh.shape["dp"], mesh.shape["tensor"]
    fine = Mesh(
        mesh.devices.reshape(dp // (WINDOW * CORES), WINDOW, CORES, tensors), ("w", "zlo", "core", "tensor")
    )
    rows = ("w", "zlo", "core")
    placed = (P(rows, "tensor"), P(rows, "tensor"), P("tensor", None), P(rows, None), P(rows))
    return jax.shard_map(
        on_device,
        mesh=fine,
        in_specs=placed,
        out_specs=(P(rows, "tensor"), P(rows, "tensor"), P(rows)),
        check_vma=False,
    )
```

time: 419 us -> 211 us (0.50)
  waiting for transfers between devices: 230 us -> 92.3 us
  starting transfers between devices: 150 us -> 79.9 us
  between operations: 14.4 us -> 0.91 us
  blocking collectives: 0 us -> 12.1 us
  matrix products: 11 us -> 15.2 us
    psum x2 -> x0, waiting for transfers between devices: 185 us -> none  [the longest x1 105 us: on_device(): pre = lax.psum(partial_pre, 'tensor')]
    ppermute x28 -> x3, starting transfers between devices: 149 us -> 35.6 us  [the longest x2 33.6 us: shift_chips(): lax.ppermute(value, CHIPS, [(i, (i + by) % chips) for i in range(chips)])]
    all_to_all x0 -> x7, waiting for transfers between devices: none -> 85.8 us  [the longest x2 32.1 us: reduce_over_tensor(): got = lax.all_to_all(part, MEMBERS, 0, 0)]
    all_to_all x0 -> x7, starting transfers between devices: none -> 44.3 us  [the longest x2 16.2 us: reduce_over_tensor(): got = lax.all_to_all(part, MEMBERS, 0, 0)]
    all_gather x1 -> x0, waiting for transfers between devices: 34.1 us -> none  [on_device(): lax.all_gather(demb, 'tensor', axis=1, tiled=True).astype(jnp.float32)]
    all_to_all x0 -> x1, blocking collectives: none -> 12.1 us  [on_device(): lax.all_to_all(jnp.broadcast_to(told[None], (members,) + told.shape), MEM...]
    ppermute x28 -> x3, waiting for transfers between devices: 10.8 us -> 6.47 us  [the longest x2 5.57 us: shift_chips(): lax.ppermute(value, CHIPS, [(i, (i + by) % chips) for i in range(chips)])]
    dot_general x6 -> x8, matrix products: 11 us -> 15.2 us  [the longest x2 8.36 us: unproject(): jnp.einsum('mrf,hmf->rh', part, weight, preferred_element_type=f32)]
  transfers between devices with their start and end apart: 31 -> 10, of which waited for: 7 -> 10; matrix products, arithmetic and copies ran while one was open for 0% -> 5% of each run, Pallas kernels for 0% -> 0%
where the time goes in v1:
time: 211 us; the launch traced here: 210 us
  waiting for transfers between devices  92.3 us (44%)
  starting transfers between devices  79.9 us (38%)
  matrix products  15.2 us (7%)
  blocking collectives  12.1 us (6%)
  local copies, waits for them, and re-layouts  6.33 us (3%)
  other arithmetic  2.93 us (1%)
    ppermute x2, starting transfers between devices, shift_chips(): lax.ppermute(value, CHIPS, [(i, (i + by) % chips) for i in range(chips)])  33.6 us
    all_to_all x2, waiting for transfers between devices, reduce_over_tensor(): got = lax.all_to_all(part, MEMBERS, 0, 0)  32.1 us
    all_to_all x2, waiting for transfers between devices, gather_features(): lax.all_to_all(part.reshape((members,) + part.shape[2:]), MEMBERS, 0, 0)  29 us
    all_to_all x2, starting transfers between devices, reduce_over_tensor(): got = lax.all_to_all(part, MEMBERS, 0, 0)  16.2 us
    all_to_all x1, blocking collectives, on_device(): lax.all_to_all(jnp.broadcast_to(told[None], (members,) + told.shape), MEM...  12.1 us
    all_to_all x2, starting transfers between devices, gather_features(): lax.all_to_all(part.reshape((members,) + part.shape[2:]), MEMBERS, 0, 0)  11.6 us
    all_to_all x1, waiting for transfers between devices, on_device(): lax.all_to_all(dwin.astype(bf16).reshape(WINDOW, CORES, p_rows, feats), '...  10.3 us
    dot_general x2, matrix products, unproject(): jnp.einsum('mrf,hmf->rh', part, weight, preferred_element_type=f32)  8.36 us
  transfers between devices with their start and end apart: 10, of which 10 were waited for; matrix products, arithmetic and copies ran while one was open for 5% of the time, Pallas kernels for 0%

profile of v1, /device:TPU:1, one launch (start us, length us, event | category | flops | bytes accessed | tf_op | source)
XLA Modules:
  0.0 209.6 jit_solution(10802344221641524238)
XLA Ops:
  0.6 22.2 %collective-permute-start = (bf16[16,512]{1,0:T(8,128)(2,1)}, bf16[16,512]{1,0:T(8,128)(2,1)S(1)}, u32[]{:S(2)}, u32[]{:S(2)}) collective-permute-start(bf16[16,512]{1,0:T(8,128)(2,1)} %param.6), channel_id=1, source_target_pairs={{0,896},{16,912},{32,928},{48,944},{64,960},{80,976},{96,992},{112... | collective-permute-start | bytes 49160 | tf_op jit(solution)/shard_map/ppermute | solution.py:17
  22.9 1.1 collective-permute-done
  23.9 3.0 %convolution_convert_fusion.1 = bf16[32,4096]{1,0:T(8,128)(2,1)S(1)} fusion(bf16[512,4096]{1,0:T(8,128)(2,1)} %param.7, bf16[16,512]{1,0:T(8,128)(2,1)S(1)} %collective-permute-done, bf16[16,512]{1,0:T(8,128)(2,1)} %param.6), kind=kOutput, calls=%fused_computation.2 | convolution fusion | flops 134414336 | bytes 4489216 | tf_op jit(solution)/shard_map/dot_general | solution.py:46
  27.0 0.7 copy.110
  27.7 8.9 %all-to-all-start.1 = ((bf16[16,32,256]{2,1,0:T(8,128)(2,1)}), bf16[16,32,256]{2,1,0:T(8,128)(2,1)S(1)}, u32[]{:S(2)}, u32[]{:S(2)}) async-start(bf16[16,32,256]{2,1,0:T(8,128)(2,1)} %bitcast.87), calls=%async_computation.1 | async-start | bytes 524288 | tf_op jit(solution)/shard_map/all_to_all | solution.py:50
  36.6 9.4 %all-to-all-done.1 = bf16[16,32,256]{2,1,0:T(8,128)(2,1)S(1)} async-done(((bf16[16,32,256]{2,1,0:T(8,128)(2,1)}), bf16[16,32,256]{2,1,0:T(8,128)(2,1)S(1)}, u32[]{:S(2)}, u32[]{:S(2)}) %all-to-all-start.1) | async-done | bytes 262176 | tf_op jit(solution)/shard_map/all_to_all | solution.py:50
  46.1 0.8 broadcast_select_fusion
  46.9 7.7 %all-to-all-start.2 = ((bf16[8,2,16,256]{3,1,2,0:T(2,128)(2,1)}), bf16[8,2,16,256]{3,1,2,0:T(2,128)(2,1)S(1)}, u32[]{:S(2)}, u32[]{:S(2)}) async-start(bf16[8,2,16,256]{3,1,2,0:T(2,128)(2,1)} %broadcast_select_fusion), calls=%async_computation.2 | async-start | bytes 262144 | tf_op jit(solution)/shard_map/all_to_all | solution.py:60
  54.6 2.9 %convolution_convert_fusion = bf16[128,4096]{1,0:T(8,128)(2,1)S(1)} fusion(bf16[128,512]{1,0:T(8,128)(2,1)S(1)} %copy-done, bf16[512,4096]{1,0:T(8,128)(2,1)} %param.7), kind=kOutput, calls=%fused_computation.1 | convolution fusion | flops 537395200 | bytes 5373952 | tf_op jit(solution)/shard_map/dot_general | solution.py:46
  57.5 1.1 copy.109
  58.6 6.2 %all-to-all-done.2 = bf16[8,2,16,256]{3,1,2,0:T(2,128)(2,1)S(1)} async-done(((bf16[8,2,16,256]{3,1,2,0:T(2,128)(2,1)}), bf16[8,2,16,256]{3,1,2,0:T(2,128)(2,1)S(1)}, u32[]{:S(2)}, u32[]{:S(2)}) %all-to-all-start.2) | async-done | bytes 131104 | tf_op jit(solution)/shard_map/all_to_all | solution.py:60
  64.9 7.3 %all-to-all-start = ((bf16[16,128,256]{2,1,0:T(8,128)(2,1)}), bf16[16,128,256]{2,1,0:T(8,128)(2,1)S(1)}, u32[]{:S(2)}, u32[]{:S(2)}) async-start(bf16[16,128,256]{2,1,0:T(8,128)(2,1)} %bitcast.85), calls=%async_computation | async-start | bytes 2097152 | tf_op jit(solution)/shard_map/all_to_all | solution.py:50
  72.2 2.0 collective-permute-start.1
  74.3 0.9 collective-permute-done.1
  75.3 0.1 reshape.120
  75.4 0.6 gather_fusion
  76.0 0.1 multiply_reduce_fusion
  76.1 0.1 broadcast_in_dim.62
  76.2 22.7 %all-to-all-done = bf16[16,128,256]{2,1,0:T(8,128)(2,1)S(1)} async-done(((bf16[16,128,256]{2,1,0:T(8,128)(2,1)}), bf16[16,128,256]{2,1,0:T(8,128)(2,1)S(1)}, u32[]{:S(2)}, u32[]{:S(2)}) %all-to-all-start) | async-done | bytes 1048608 | tf_op jit(solution)/shard_map/all_to_all | solution.py:50
  98.8 0.1 bitcast_reduce_fusion
  99.0 0.1 fusion.21
  99.1 0.2 fusion.47
  99.4 0.8 maximum_maximum_fusion
  100.1 4.8 %all-to-all-start.3 = ((f32[16,24,128]{2,1,0:T(8,128)}), f32[16,24,128]{2,1,0:T(8,128)S(1)}, u32[]{:S(2)}, u32[]{:S(2)}) async-start(f32[16,24,128]{2,1,0:T(8,128)} %maximum_maximum_fusion), calls=%async_computation.3 | async-start | bytes 393216 | tf_op jit(solution)/shard_map/all_to_all | solution.py:71
  105.0 8.2 %all-to-all-done.3 = f32[16,24,128]{2,1,0:T(8,128)S(1)} async-done(((f32[16,24,128]{2,1,0:T(8,128)}), f32[16,24,128]{2,1,0:T(8,128)S(1)}, u32[]{:S(2)}, u32[]{:S(2)}) %all-to-all-start.3) | async-done | bytes 196640 | tf_op jit(solution)/shard_map/all_to_all | solution.py:71
  113.3 0.2 select_reduce_fusion
  113.5 0.2 fusion.33
  113.7 0.1 concatenate.28
  113.9 12.1 %all_to_all.40 = bf16[16,24,128]{2,1,0:T(8,128)(2,1)S(1)} all-to-all(bf16[16,24,128]{2,1,0:T(8,128)(2,1)S(1)} %broadcast_in_dim.98), channel_id=1, replica_groups=mesh['w'=8,'zlo'=8,'core'=2,'tensor'=8] {'core','tensor'}, dimensions={0} | all-to-all | bytes 196608 | tf_op jit(solution)/shard_map/all_to_all | solution.py:92
  126.0 0.2 fusion.11
  126.3 0.3 fusion.9
  126.6 0.8 copy.66
  127.4 4.0 %all-to-all-start.6 = ((bf16[8,2,16,256]{3,1,2,0:T(2,128)(2,1)}), bf16[8,2,16,256]{3,1,2,0:T(2,128)(2,1)S(1)}, u32[]{:S(2)}, u32[]{:S(2)}) async-start(bf16[8,2,16,256]{3,1,2,0:T(2,128)(2,1)} %copy.66), calls=%async_computation.6 | async-start | bytes 262144 | tf_op jit(solution)/shard_map/all_to_all | solution.py:108
  131.4 10.3 %all-to-all-done.6 = bf16[8,2,16,256]{3,1,2,0:T(2,128)(2,1)S(1)} async-done(((bf16[8,2,16,256]{3,1,2,0:T(2,128)(2,1)}), bf16[8,2,16,256]{3,1,2,0:T(2,128)(2,1)S(1)}, u32[]{:S(2)}, u32[]{:S(2)}) %all-to-all-start.6) | async-done | bytes 131104 | tf_op jit(solution)/shard_map/all_to_all | solution.py:108
  141.7 0.4 fusion.23
  142.1 11.3 %collective-permute-start.2 = (bf16[2,16,256]{2,1,0:T(8,128)(2,1)S(1)}, bf16[2,16,256]{2,1,0:T(8,128)(2,1)S(1)}, u32[]{:S(2)}, u32[]{:S(2)}) collective-permute-start(bf16[2,16,256]{2,1,0:T(8,128)(2,1)S(1)} %copy.108), channel_id=1, source_target_pairs={{0,128},{16,144},{32,160},{48,176},{64,192},{80,208},{96,224},{112... | collective-permute-start | bytes 49160 | tf_op jit(solution)/shard_map/ppermute | solution.py:17
  153.4 4.5 %collective-permute-done.2 = bf16[2,16,256]{2,1,0:T(8,128)(2,1)S(1)} collective-permute-done((bf16[2,16,256]{2,1,0:T(8,128)(2,1)S(1)}, bf16[2,16,256]{2,1,0:T(8,128)(2,1)S(1)}, u32[]{:S(2)}, u32[]{:S(2)}) %collective-permute-start.2) | collective-permute-done | bytes 16416 | tf_op jit(solution)/shard_map/ppermute | solution.py:17
  157.9 0.7 broadcast_in_dim.101
  158.6 6.8 %all-to-all-start.7 = ((bf16[16,16,256]{2,1,0:T(8,128)(2,1)}), bf16[16,16,256]{2,1,0:T(8,128)(2,1)S(1)}, u32[]{:S(2)}, u32[]{:S(2)}) async-start(bf16[16,16,256]{2,1,0:T(8,128)(2,1)} %bitcast.24), calls=%async_computation.7 | async-start | bytes 262144 | tf_op jit(solution)/shard_map/all_to_all | solution.py:116
  165.5 0.1 mul.90
  165.6 0.2 fusion.10
  165.8 7.0 %all-to-all-done.7 = bf16[16,16,256]{2,1,0:T(8,128)(2,1)S(1)} async-done(((bf16[16,16,256]{2,1,0:T(8,128)(2,1)}), bf16[16,16,256]{2,1,0:T(8,128)(2,1)S(1)}, u32[]{:S(2)}, u32[]{:S(2)}) %all-to-all-start.7) | async-done | bytes 131104 | tf_op jit(solution)/shard_map/all_to_all | solution.py:116
  172.8 1.1 broadcast_in_dim.99
  173.9 4.7 %all-to-all-start.5 = ((bf16[16,128,256]{2,1,0:T(8,128)(2,1)}), bf16[16,128,256]{2,1,0:T(8,128)(2,1)S(1)}, u32[]{:S(2)}, u32[]{:S(2)}) async-start(bf16[16,128,256]{2,1,0:T(8,128)(2,1)} %bitcast.18), calls=%async_computation.5 | async-start | bytes 2097152 | tf_op jit(solution)/shard_map/all_to_all | solution.py:116
  178.6 0.6 select_n.55
  179.2 4.0 %fusion.18 = bf16[16,512]{1,0:T(8,128)(2,1)} fusion(bf16[16,16,256]{2,1,0:T(8,128)(2,1)S(1)} %all-to-all-done.7, bf16[64,16,8,256]{3,2,1,0:T(8,128)(2,1)} %bitcast.88), kind=kOutput, calls=%fused_computation.18 | convolution fusion | flops 67117056 | bytes 4341760 | tf_op jit(solution)/shard_map/mrf,hmf->rh/dot_general | solution.py:120
  183.2 22.0 %all-to-all-done.5 = bf16[16,128,256]{2,1,0:T(8,128)(2,1)S(1)} async-done(((bf16[16,128,256]{2,1,0:T(8,128)(2,1)}), bf16[16,128,256]{2,1,0:T(8,128)(2,1)S(1)}, u32[]{:S(2)}, u32[]{:S(2)}) %all-to-all-start.5) | async-done | bytes 1048608 | tf_op jit(solution)/shard_map/all_to_all | solution.py:116
  205.2 4.4 %fusion.12 = bf16[128,512]{1,0:T(8,128)(2,1)} fusion(bf16[16,128,256]{2,1,0:T(8,128)(2,1)S(1)} %all-to-all-done.5, bf16[64,16,8,256]{3,2,1,0:T(8,128)(2,1)} %bitcast.89), kind=kOutput, calls=%fused_computation.16 | convolution fusion | flops 536936448 | bytes 5373952 | tf_op jit(solution)/shard_map/mrf,hmf->rh/dot_general | solution.py:120
  (44 shorter events, 0.8 us)
Async XLA Ops:
  0.6 54.0 %copy-start = (bf16[128,512]{1,0:T(8,128)(2,1)S(1)}, bf16[128,512]{1,0:T(8,128)(2,1)}, u32[]{:S(2)}) copy-start(bf16[128,512]{1,0:T(8,128)(2,1)} %param.5) | copy-start | bytes 393220
  0.6 23.3 %collective-permute-start = (bf16[16,512]{1,0:T(8,128)(2,1)}, bf16[16,512]{1,0:T(8,128)(2,1)S(1)}, u32[]{:S(2)}, u32[]{:S(2)}) collective-permute-start(bf16[16,512]{1,0:T(8,128)(2,1)} %param.6), channel_id=1, source_target_pairs={{0,896},{16,912},{32,928},{48,944},{64,960},{80,976},{96,992},{112... | collective-permute-start | bytes 49160 | tf_op jit(solution)/shard_map/ppermute | solution.py:17
  27.7 18.3 %all-to-all-start.1 = ((bf16[16,32,256]{2,1,0:T(8,128)(2,1)}), bf16[16,32,256]{2,1,0:T(8,128)(2,1)S(1)}, u32[]{:S(2)}, u32[]{:S(2)}) async-start(bf16[16,32,256]{2,1,0:T(8,128)(2,1)} %bitcast.87), calls=%async_computation.1 | async-start | bytes 524288 | tf_op jit(solution)/shard_map/all_to_all | solution.py:50
  46.9 17.9 %all-to-all-start.2 = ((bf16[8,2,16,256]{3,1,2,0:T(2,128)(2,1)}), bf16[8,2,16,256]{3,1,2,0:T(2,128)(2,1)S(1)}, u32[]{:S(2)}, u32[]{:S(2)}) async-start(bf16[8,2,16,256]{3,1,2,0:T(2,128)(2,1)} %broadcast_select_fusion), calls=%async_computation.2 | async-start | bytes 262144 | tf_op jit(solution)/shard_map/all_to_all | solution.py:60
  54.6 17.6 %copy-start.1 = (s32[1,8]{1,0:T(1,128)S(1)}, s32[1,8]{1,0:T(1,128)}, u32[]{:S(2)}) copy-start(s32[1,8]{1,0:T(1,128)} %param.8) | copy-start | bytes 100
  57.5 47.4 %copy-start.2 = (s32[128]{0:T(128)S(1)}, s32[128]{0:T(128)}, u32[]{:S(2)}) copy-start(s32[128]{0:T(128)} %param.9) | copy-start | bytes 1540
  64.9 34.0 %all-to-all-start = ((bf16[16,128,256]{2,1,0:T(8,128)(2,1)}), bf16[16,128,256]{2,1,0:T(8,128)(2,1)S(1)}, u32[]{:S(2)}, u32[]{:S(2)}) async-start(bf16[16,128,256]{2,1,0:T(8,128)(2,1)} %bitcast.85), calls=%async_computation | async-start | bytes 2097152 | tf_op jit(solution)/shard_map/all_to_all | solution.py:50
  72.2 3.0 %collective-permute-start.1 = (s32[1,8]{1,0:T(1,128)S(1)}, s32[1,8]{1,0:T(1,128)S(1)}, u32[]{:S(2)}, u32[]{:S(2)}) collective-permute-start(s32[1,8]{1,0:T(1,128)S(1)} %copy-done.1), channel_id=1, source_target_pairs={{0,8},{8,0},{1,9},{9,1},{2,10},{10,2},{3,11},{11,3},{4,12},{12,4},... | collective-permute-start | bytes 104 | tf_op jit(solution)/shard_map/ppermute | solution.py:41
  100.1 13.1 %all-to-all-start.3 = ((f32[16,24,128]{2,1,0:T(8,128)}), f32[16,24,128]{2,1,0:T(8,128)S(1)}, u32[]{:S(2)}, u32[]{:S(2)}) async-start(f32[16,24,128]{2,1,0:T(8,128)} %maximum_maximum_fusion), calls=%async_computation.3 | async-start | bytes 393216 | tf_op jit(solution)/shard_map/all_to_all | solution.py:71
  127.4 14.3 %all-to-all-start.6 = ((bf16[8,2,16,256]{3,1,2,0:T(2,128)(2,1)}), bf16[8,2,16,256]{3,1,2,0:T(2,128)(2,1)S(1)}, u32[]{:S(2)}, u32[]{:S(2)}) async-start(bf16[8,2,16,256]{3,1,2,0:T(2,128)(2,1)} %copy.66), calls=%async_computation.6 | async-start | bytes 262144 | tf_op jit(solution)/shard_map/all_to_all | solution.py:108
  142.1 15.9 %collective-permute-start.2 = (bf16[2,16,256]{2,1,0:T(8,128)(2,1)S(1)}, bf16[2,16,256]{2,1,0:T(8,128)(2,1)S(1)}, u32[]{:S(2)}, u32[]{:S(2)}) collective-permute-start(bf16[2,16,256]{2,1,0:T(8,128)(2,1)S(1)} %copy.108), channel_id=1, source_target_pairs={{0,128},{16,144},{32,160},{48,176},{64,192},{80,208},{96,224},{112... | collective-permute-start | bytes 49160 | tf_op jit(solution)/shard_map/ppermute | solution.py:17
  158.6 14.2 %all-to-all-start.7 = ((bf16[16,16,256]{2,1,0:T(8,128)(2,1)}), bf16[16,16,256]{2,1,0:T(8,128)(2,1)S(1)}, u32[]{:S(2)}, u32[]{:S(2)}) async-start(bf16[16,16,256]{2,1,0:T(8,128)(2,1)} %bitcast.24), calls=%async_computation.7 | async-start | bytes 262144 | tf_op jit(solution)/shard_map/all_to_all | solution.py:116
  173.9 31.4 %all-to-all-start.5 = ((bf16[16,128,256]{2,1,0:T(8,128)(2,1)}), bf16[16,128,256]{2,1,0:T(8,128)(2,1)S(1)}, u32[]{:S(2)}, u32[]{:S(2)}) async-start(bf16[16,128,256]{2,1,0:T(8,128)(2,1)} %bitcast.18), calls=%async_computation.5 | async-start | bytes 2097152 | tf_op jit(solution)/shard_map/all_to_all | solution.py:116

commit v2 on v1

--- a/solution.py
+++ b/solution.py
@@ -9,12 +9,11 @@
 WINDOW = 8
 CORES = 2
 MEMBERS = ("core", "tensor")
-CHIPS = ("w", "zlo")
 
 
 def shift_chips(value, by):
-    chips = lax.axis_size(CHIPS)
-    return lax.ppermute(value, CHIPS, [(i, (i + by) % chips) for i in range(chips)])
+    chips = lax.axis_size("chip")
+    return lax.ppermute(value, "chip", [(i, (i + by) % chips) for i in range(chips)])
 
 
 def halves(value, parts):
@@ -35,9 +34,8 @@
     members = CORES * tensors
     feats = out_weight.shape[1] // members
     q_part = q_rows // tensors
-    core, place = lax.axis_index("core"), lax.axis_index("zlo")
+    core, chip = lax.axis_index("core"), lax.axis_index("chip")
 
-    far_ctx = shift_chips(p_ctx, -WINDOW)
     other = lax.ppermute(neighbours, "core", [(0, 1), (1, 0)])
     lists = jnp.concatenate([neighbours, other], axis=0)
     lists = jnp.where(core == 0, lists, lists[::-1])
@@ -51,14 +49,16 @@
         got = got.reshape(CORES, tensors, part.shape[1], feats).astype(f32)
         return jnp.sum(got, axis=1).astype(bf16)
 
-    p_pre = reduce_over_tensor(project(jnp.concatenate([p_ctx, far_ctx], axis=0)))
+    p_part = project(p_ctx)
+    q_ctx, p_part = lax.optimization_barrier((q_ctx, p_part))
+    window = reduce_over_tensor(p_part)
     q_pre = reduce_over_tensor(project(q_ctx))
-    near, far = p_pre[:, :p_rows], p_pre[:, p_rows:]
 
-    ids = jnp.arange(WINDOW, dtype=jnp.int32)
-    outgoing = jnp.where((ids <= place)[:, None, None, None], near[None], far[None])
-    window = lax.all_to_all(outgoing, "zlo", 0, 0).reshape(WINDOW * CORES, p_rows, feats)
-    spots = lists % (WINDOW * CORES)
+    reach = 1
+    while reach < WINDOW:
+        window = jnp.concatenate([window, shift_chips(window, -reach)], axis=0)
+        reach *= 2
+    spots = (lists - CORES * chip) % (CORES * lax.axis_size("chip"))
     cand = window[spots].reshape(CORES, slots, feats)
 
     raw = jnp.einsum("kqf,kcf->kqc", q_pre, cand, preferred_element_type=f32)
@@ -105,11 +105,11 @@
     match = (jnp.arange(WINDOW * CORES, dtype=jnp.int32)[:, None, None] == spots[None]).astype(bf16)
     dwin = jnp.einsum("wks,kspf->wpf", match, dc.reshape(CORES, listed, p_rows, feats), preferred_element_type=f32)
 
-    back = lax.all_to_all(dwin.astype(bf16).reshape(WINDOW, CORES, p_rows, feats), "zlo", 0, 0).astype(f32)
-    mine = (ids <= place)[:, None, None, None]
-    near = jnp.sum(jnp.where(mine, back, 0.0), axis=0)
-    far = jnp.sum(jnp.where(mine, 0.0, back), axis=0).astype(bf16)
-    dp = (near + shift_chips(far, WINDOW).astype(f32)).astype(bf16)
+    while reach > 1:
+        reach //= 2
+        away = shift_chips(dwin[CORES * reach :].astype(bf16), reach)
+        dwin = dwin[: CORES * reach] + away.astype(f32)
+    dp = dwin.astype(bf16)
 
     def gather_features(part):
         part = jnp.broadcast_to(part[:, None], (CORES, tensors) + part.shape[1:])
@@ -119,17 +119,16 @@
         weight = out_weight.reshape(out_weight.shape[0], members, feats)
         return jnp.einsum("mrf,hmf->rh", part, weight, preferred_element_type=f32).astype(bf16)
 
-    q_grad = unproject(gather_features(dq))
+    q_all = gather_features(dq)
+    q_all, dp = lax.optimization_barrier((q_all, dp))
     p_grad = unproject(gather_features(dp))
-    return q_grad, p_grad, losses
+    return unproject(q_all), p_grad, losses
 
 
 def solution(mesh):
     dp, tensors = mesh.shape["dp"], mesh.shape["tensor"]
-    fine = Mesh(
-        mesh.devices.reshape(dp // (WINDOW * CORES), WINDOW, CORES, tensors), ("w", "zlo", "core", "tensor")
-    )
-    rows = ("w", "zlo", "core")
+    fine = Mesh(mesh.devices.reshape(dp // CORES, CORES, tensors), ("chip", "core", "tensor"))
+    rows = ("chip", "core")
     placed = (P(rows, "tensor"), P(rows, "tensor"), P("tensor", None), P(rows, None), P(rows))
     return jax.shard_map(
         on_device,

time: 211 us -> 156 us (0.74)
  waiting for transfers between devices: 92.3 us -> 39.7 us
    all_to_all x2, waiting for transfers between devices: 32.1 us -> 3.32 us  [reduce_over_tensor(): got = lax.all_to_all(part, MEMBERS, 0, 0)]
    all_to_all x2, waiting for transfers between devices: 29 us -> 2.92 us  [gather_features(): lax.all_to_all(part.reshape((members,) + part.shape[2:]), MEMBERS, 0, 0)]
    ppermute x2 -> x6, waiting for transfers between devices: 5.57 us -> 25.3 us  [shift_chips(): lax.ppermute(value, 'chip', [(i, (i + by) % chips) for i in range(chips)])]
    all_to_all x2 -> x0, waiting for transfers between devices: 16.5 us -> none  [the longest x1 10.3 us: on_device(): lax.all_to_all(dwin.astype(bf16).reshape(WINDOW, CORES, p_rows, feats), '...]
    all_to_all x2 -> x0, starting transfers between devices: 11.7 us -> none  [the longest x1 7.66 us: on_device(): lax.all_to_all(outgoing, 'zlo', 0, 0).reshape(WINDOW * CORES, p_rows, feats)]
    all_to_all x2, starting transfers between devices: 16.2 us -> 22.2 us  [reduce_over_tensor(): got = lax.all_to_all(part, MEMBERS, 0, 0)]
    all_to_all x1, starting transfers between devices: 4.83 us -> 10.1 us  [on_device(): lax.all_to_all(sums.reshape(members, q_part + 8, slots), MEMBERS, 0, 0)]
    all_to_all x2, starting transfers between devices: 11.6 us -> 14.1 us  [gather_features(): lax.all_to_all(part.reshape((members,) + part.shape[2:]), MEMBERS, 0, 0)]
  transfers between devices with their start and end apart: 10 -> 12, of which waited for: 10 -> 9; matrix products, arithmetic and copies ran while one was open for 5% -> 7% of each run, Pallas kernels for 0% -> 0%
where the time goes in v2:
time: 156 us; the launch traced here: 155 us
  starting transfers between devices  79.9 us (51%)
  waiting for transfers between devices  39.7 us (25%)
  matrix products  15 us (10%)
  blocking collectives  12.1 us (8%)
  local copies, waits for them, and re-layouts  5.44 us (3%)
  other arithmetic  1.83 us (1%)
    ppermute x6, starting transfers between devices, shift_chips(): lax.ppermute(value, 'chip', [(i, (i + by) % chips) for i in range(chips)])  31.4 us
    ppermute x6, waiting for transfers between devices, shift_chips(): lax.ppermute(value, 'chip', [(i, (i + by) % chips) for i in range(chips)])  25.3 us
    all_to_all x2, starting transfers between devices, reduce_over_tensor(): got = lax.all_to_all(part, MEMBERS, 0, 0)  22.2 us
    all_to_all x2, starting transfers between devices, gather_features(): lax.all_to_all(part.reshape((members,) + part.shape[2:]), MEMBERS, 0, 0)  14.1 us
    all_to_all x1, blocking collectives, on_device(): lax.all_to_all(jnp.broadcast_to(told[None], (members,) + told.shape), MEM...  12.1 us
    all_to_all x1, starting transfers between devices, on_device(): lax.all_to_all(sums.reshape(members, q_part + 8, slots), MEMBERS, 0, 0)  10.1 us
    dot_general x2, matrix products, unproject(): jnp.einsum('mrf,hmf->rh', part, weight, preferred_element_type=f32)  8.36 us
    all_to_all x1, waiting for transfers between devices, on_device(): lax.all_to_all(sums.reshape(members, q_part + 8, slots), MEMBERS, 0, 0)  8.2 us
  transfers between devices with their start and end apart: 12, of which 9 were waited for; matrix products, arithmetic and copies ran while one was open for 7% of the time, Pallas kernels for 0%

profile of v2, /device:TPU:1, one launch (start us, length us, event | category | flops | bytes accessed | tf_op | source)
XLA Modules:
  0.0 155.0 jit_solution(9496142214655839059)
XLA Ops:
  0.6 2.9 %convolution_convert_fusion.1 = bf16[16,4096]{1,0:T(8,128)(2,1)S(1)} fusion(bf16[16,512]{1,0:T(8,128)(2,1)} %param.6, bf16[512,4096]{1,0:T(8,128)(2,1)} %param.7), kind=kOutput, calls=%fused_computation.2 | convolution fusion | flops 67174400 | bytes 4341760 | tf_op jit(solution)/shard_map/dot_general | solution.py:44
  3.5 0.7 copy.77
  4.2 17.5 %all-to-all-start.1 = ((bf16[16,16,256]{2,1,0:T(8,128)(2,1)}), bf16[16,16,256]{2,1,0:T(8,128)(2,1)S(1)}, u32[]{:S(2)}, u32[]{:S(2)}) async-start(bf16[16,16,256]{2,1,0:T(8,128)(2,1)} %bitcast.83), calls=%async_computation.1 | async-start | bytes 262144 | tf_op jit(solution)/shard_map/all_to_all | solution.py:48
  21.7 2.9 %convolution_convert_fusion = bf16[128,4096]{1,0:T(8,128)(2,1)S(1)} fusion(bf16[128,512]{1,0:T(8,128)(2,1)S(1)} %copy-done, bf16[512,4096]{1,0:T(8,128)(2,1)} %param.7), kind=kOutput, calls=%fused_computation.1 | convolution fusion | flops 537395200 | bytes 5373952 | tf_op jit(solution)/shard_map/dot_general | solution.py:44
  24.7 1.1 copy.76
  25.8 3.3 %all-to-all-done.1 = bf16[16,16,256]{2,1,0:T(8,128)(2,1)S(1)} async-done(((bf16[16,16,256]{2,1,0:T(8,128)(2,1)}), bf16[16,16,256]{2,1,0:T(8,128)(2,1)S(1)}, u32[]{:S(2)}, u32[]{:S(2)}) %all-to-all-start.1) | async-done | bytes 131104 | tf_op jit(solution)/shard_map/all_to_all | solution.py:48
  29.1 4.7 %all-to-all-start = ((bf16[16,128,256]{2,1,0:T(8,128)(2,1)}), bf16[16,128,256]{2,1,0:T(8,128)(2,1)S(1)}, u32[]{:S(2)}, u32[]{:S(2)}) async-start(bf16[16,128,256]{2,1,0:T(8,128)(2,1)} %bitcast.81), calls=%async_computation | async-start | bytes 2097152 | tf_op jit(solution)/shard_map/all_to_all | solution.py:48
  33.8 2.1 %collective-permute-start.3 = (s32[1,8]{1,0:T(1,128)S(1)}, s32[1,8]{1,0:T(1,128)S(1)}, u32[]{:S(2)}, u32[]{:S(2)}) collective-permute-start(s32[1,8]{1,0:T(1,128)S(1)} %copy-done.1), channel_id=1, source_target_pairs={{0,8},{8,0},{1,9},{9,1},{2,10},{10,2},{3,11},{11,3},{4,12},{12,4},... | collective-permute-start | bytes 104 | tf_op jit(solution)/shard_map/ppermute | solution.py:39
  36.0 11.2 %collective-permute-start = (bf16[2,16,256]{2,1,0:T(8,128)(2,1)S(1)}, bf16[2,16,256]{2,1,0:T(8,128)(2,1)S(1)}, u32[]{:S(2)}, u32[]{:S(2)}) collective-permute-start(bf16[2,16,256]{2,1,0:T(8,128)(2,1)S(1)} %bitcast_reduce_fusion.1), channel_id=1, source_target_pairs={{0,1008},{16,0},{32,16},{48,32},{64,48},{80,64},{96,80},{112,96},{... | collective-permute-start | bytes 49160 | tf_op jit(solution)/shard_map/ppermute | solution.py:16
  47.3 0.8 collective-permute-done
  48.1 3.9 %collective-permute-start.1 = (bf16[4,16,256]{2,1,0:T(8,128)(2,1)S(1)}, bf16[4,16,256]{2,1,0:T(8,128)(2,1)S(1)}, u32[]{:S(2)}, u32[]{:S(2)}) collective-permute-start(bf16[4,16,256]{2,1,0:T(8,128)(2,1)S(1)} %pad_maximum_fusion.2), channel_id=1, source_target_pairs={{0,992},{16,1008},{32,0},{48,16},{64,32},{80,48},{96,64},{112,80},... | collective-permute-start | bytes 98312 | tf_op jit(solution)/shard_map/ppermute | solution.py:16
  52.0 0.1 reshape.106
  52.1 1.8 %collective-permute-done.1 = bf16[4,16,256]{2,1,0:T(8,128)(2,1)S(1)} collective-permute-done((bf16[4,16,256]{2,1,0:T(8,128)(2,1)S(1)}, bf16[4,16,256]{2,1,0:T(8,128)(2,1)S(1)}, u32[]{:S(2)}, u32[]{:S(2)}) %collective-permute-start.1) | collective-permute-done | bytes 32800 | tf_op jit(solution)/shard_map/ppermute | solution.py:16
  54.0 3.9 %collective-permute-start.2 = (bf16[8,16,256]{2,1,0:T(8,128)(2,1)S(1)}, bf16[8,16,256]{2,1,0:T(8,128)(2,1)S(1)}, u32[]{:S(2)}, u32[]{:S(2)}) collective-permute-start(bf16[8,16,256]{2,1,0:T(8,128)(2,1)S(1)} %pad_maximum_fusion.1), channel_id=1, source_target_pairs={{0,960},{16,976},{32,992},{48,1008},{64,0},{80,16},{96,32},{112,48... | collective-permute-start | bytes 196616 | tf_op jit(solution)/shard_map/ppermute | solution.py:16
  57.9 5.8 %collective-permute-done.2 = bf16[8,16,256]{2,1,0:T(8,128)(2,1)S(1)} collective-permute-done((bf16[8,16,256]{2,1,0:T(8,128)(2,1)S(1)}, bf16[8,16,256]{2,1,0:T(8,128)(2,1)S(1)}, u32[]{:S(2)}, u32[]{:S(2)}) %collective-permute-start.2) | collective-permute-done | bytes 65568 | tf_op jit(solution)/shard_map/ppermute | solution.py:16
  63.7 0.6 gather_fusion
  64.2 0.1 multiply_reduce_fusion
  64.3 0.1 broadcast_in_dim.17
  64.4 0.1 bitcast_reduce_fusion
  64.6 0.1 fusion.20
  64.7 0.2 fusion.39
  64.9 0.1 reshape.96
  65.0 0.8 maximum_maximum_fusion
  65.7 10.1 %all-to-all-start.2 = ((f32[16,24,128]{2,1,0:T(8,128)}), f32[16,24,128]{2,1,0:T(8,128)S(1)}, u32[]{:S(2)}, u32[]{:S(2)}) async-start(f32[16,24,128]{2,1,0:T(8,128)} %maximum_maximum_fusion), calls=%async_computation.2 | async-start | bytes 393216 | tf_op jit(solution)/shard_map/all_to_all | solution.py:71
  75.8 0.1 dynamic_slice.3
  75.9 8.2 %all-to-all-done.2 = f32[16,24,128]{2,1,0:T(8,128)S(1)} async-done(((f32[16,24,128]{2,1,0:T(8,128)}), f32[16,24,128]{2,1,0:T(8,128)S(1)}, u32[]{:S(2)}, u32[]{:S(2)}) %all-to-all-start.2) | async-done | bytes 196640 | tf_op jit(solution)/shard_map/all_to_all | solution.py:71
  84.1 0.2 select_reduce_fusion
  84.3 0.2 fusion.27
  84.6 0.1 concatenate.38
  84.8 12.1 %all_to_all.30 = bf16[16,24,128]{2,1,0:T(8,128)(2,1)S(1)} all-to-all(bf16[16,24,128]{2,1,0:T(8,128)(2,1)S(1)} %broadcast_in_dim.21), channel_id=1, replica_groups=mesh['chip'=64,'core'=2,'tensor'=8] {'core','tensor'}, dimensions={0} | all-to-all | bytes 196608 | tf_op jit(solution)/shard_map/all_to_all | solution.py:92
  97.0 0.1 mul.90
  97.0 0.2 fusion.9
  97.2 1.1 broadcast_in_dim.22
  98.3 4.6 %all-to-all-start.4 = ((bf16[16,128,256]{2,1,0:T(8,128)(2,1)}), bf16[16,128,256]{2,1,0:T(8,128)(2,1)S(1)}, u32[]{:S(2)}, u32[]{:S(2)}) async-start(bf16[16,128,256]{2,1,0:T(8,128)(2,1)} %bitcast.17), calls=%async_computation.4 | async-start | bytes 2097152 | tf_op jit(solution)/shard_map/all_to_all | solution.py:116
  102.9 0.2 fusion.10
  103.2 0.3 convolution_bitcast_fusion
  103.5 1.9 %collective-permute-start.4 = (bf16[8,16,256]{2,0,1:T(8,128)(2,1)S(1)}, bf16[8,16,256]{2,0,1:T(8,128)(2,1)S(1)}, u32[]{:S(2)}, u32[]{:S(2)}) collective-permute-start(bf16[8,16,256]{2,0,1:T(8,128)(2,1)S(1)} %slice.144), channel_id=1, source_target_pairs={{0,64},{16,80},{32,96},{48,112},{64,128},{80,144},{96,160},{112,17... | collective-permute-start | bytes 196616 | tf_op jit(solution)/shard_map/ppermute | solution.py:16
  105.4 9.5 %collective-permute-done.4 = bf16[8,16,256]{2,0,1:T(8,128)(2,1)S(1)} collective-permute-done((bf16[8,16,256]{2,0,1:T(8,128)(2,1)S(1)}, bf16[8,16,256]{2,0,1:T(8,128)(2,1)S(1)}, u32[]{:S(2)}, u32[]{:S(2)}) %collective-permute-start.4) | collective-permute-done | bytes 65568 | tf_op jit(solution)/shard_map/ppermute | solution.py:16
  115.0 6.3 %collective-permute-start.5 = (bf16[4,16,256]{2,0,1:T(4,128)(2,1)S(1)}, bf16[4,16,256]{2,0,1:T(4,128)(2,1)S(1)}, u32[]{:S(2)}, u32[]{:S(2)}) collective-permute-start(bf16[4,16,256]{2,0,1:T(4,128)(2,1)S(1)} %slice.145), channel_id=1, source_target_pairs={{0,32},{16,48},{32,64},{48,80},{64,96},{80,112},{96,128},{112,144}... | collective-permute-start | bytes 98312 | tf_op jit(solution)/shard_map/ppermute | solution.py:16
  121.3 4.4 %collective-permute-done.5 = bf16[4,16,256]{2,0,1:T(4,128)(2,1)S(1)} collective-permute-done((bf16[4,16,256]{2,0,1:T(4,128)(2,1)S(1)}, bf16[4,16,256]{2,0,1:T(4,128)(2,1)S(1)}, u32[]{:S(2)}, u32[]{:S(2)}) %collective-permute-start.5) | collective-permute-done | bytes 32800 | tf_op jit(solution)/shard_map/ppermute | solution.py:16
  125.7 4.2 %collective-permute-start.6 = (bf16[2,16,256]{2,0,1:T(2,128)(2,1)S(1)}, bf16[2,16,256]{2,0,1:T(2,128)(2,1)S(1)}, u32[]{:S(2)}, u32[]{:S(2)}) collective-permute-start(bf16[2,16,256]{2,0,1:T(2,128)(2,1)S(1)} %slice.146), channel_id=1, source_target_pairs={{0,16},{16,32},{32,48},{48,64},{64,80},{80,96},{96,112},{112,128},... | collective-permute-start | bytes 49160 | tf_op jit(solution)/shard_map/ppermute | solution.py:16
  129.9 0.6 select_n.40
  130.5 3.0 %collective-permute-done.6 = bf16[2,16,256]{2,0,1:T(2,128)(2,1)S(1)} collective-permute-done((bf16[2,16,256]{2,0,1:T(2,128)(2,1)S(1)}, bf16[2,16,256]{2,0,1:T(2,128)(2,1)S(1)}, u32[]{:S(2)}, u32[]{:S(2)}) %collective-permute-start.6) | collective-permute-done | bytes 16416 | tf_op jit(solution)/shard_map/ppermute | solution.py:16
  133.6 0.6 broadcast_in_dim.23
  134.2 9.5 %all-to-all-start.5 = ((bf16[16,16,256]{2,1,0:T(8,128)(2,1)}), bf16[16,16,256]{2,1,0:T(8,128)(2,1)S(1)}, u32[]{:S(2)}, u32[]{:S(2)}) async-start(bf16[16,16,256]{2,1,0:T(8,128)(2,1)} %bitcast.23), calls=%async_computation.5 | async-start | bytes 262144 | tf_op jit(solution)/shard_map/all_to_all | solution.py:116
  143.7 4.4 %fusion.11 = bf16[128,512]{1,0:T(8,128)(2,1)} fusion(bf16[16,128,256]{2,1,0:T(8,128)(2,1)S(1)} %all-to-all-done.4, bf16[64,16,8,256]{3,2,1,0:T(8,128)(2,1)} %bitcast.84), kind=kOutput, calls=%fused_computation.15 | convolution fusion | flops 536936448 | bytes 5373952 | tf_op jit(solution)/shard_map/mrf,hmf->rh/dot_general | solution.py:120
  148.1 2.9 %all-to-all-done.5 = bf16[16,16,256]{2,1,0:T(8,128)(2,1)S(1)} async-done(((bf16[16,16,256]{2,1,0:T(8,128)(2,1)}), bf16[16,16,256]{2,1,0:T(8,128)(2,1)S(1)}, u32[]{:S(2)}, u32[]{:S(2)}) %all-to-all-start.5) | async-done | bytes 131104 | tf_op jit(solution)/shard_map/all_to_all | solution.py:116
  151.0 4.0 %fusion.17 = bf16[16,512]{1,0:T(8,128)(2,1)} fusion(bf16[16,16,256]{2,1,0:T(8,128)(2,1)S(1)} %all-to-all-done.5, bf16[64,16,8,256]{3,2,1,0:T(8,128)(2,1)} %bitcast.85), kind=kOutput, calls=%fused_computation.17 | convolution fusion | flops 67117056 | bytes 4341760 | tf_op jit(solution)/shard_map/mrf,hmf->rh/dot_general | solution.py:120
  (47 shorter events, 0.6 us)
Async XLA Ops:
  0.6 21.1 %copy-start = (bf16[128,512]{1,0:T(8,128)(2,1)S(1)}, bf16[128,512]{1,0:T(8,128)(2,1)}, u32[]{:S(2)}) copy-start(bf16[128,512]{1,0:T(8,128)(2,1)} %param.5) | copy-start | bytes 393220
  4.2 24.9 %all-to-all-start.1 = ((bf16[16,16,256]{2,1,0:T(8,128)(2,1)}), bf16[16,16,256]{2,1,0:T(8,128)(2,1)S(1)}, u32[]{:S(2)}, u32[]{:S(2)}) async-start(bf16[16,16,256]{2,1,0:T(8,128)(2,1)} %bitcast.83), calls=%async_computation.1 | async-start | bytes 262144 | tf_op jit(solution)/shard_map/all_to_all | solution.py:48
  21.7 12.1 %copy-start.1 = (s32[1,8]{1,0:T(1,128)S(1)}, s32[1,8]{1,0:T(1,128)}, u32[]{:S(2)}) copy-start(s32[1,8]{1,0:T(1,128)} %param.8) | copy-start | bytes 100
  24.7 51.2 %copy-start.2 = (s32[128]{0:T(128)S(1)}, s32[128]{0:T(128)}, u32[]{:S(2)}) copy-start(s32[128]{0:T(128)} %param.9) | copy-start | bytes 1540
  29.1 35.4 %all-to-all-start = ((bf16[16,128,256]{2,1,0:T(8,128)(2,1)}), bf16[16,128,256]{2,1,0:T(8,128)(2,1)S(1)}, u32[]{:S(2)}, u32[]{:S(2)}) async-start(bf16[16,128,256]{2,1,0:T(8,128)(2,1)} %bitcast.81), calls=%async_computation | async-start | bytes 2097152 | tf_op jit(solution)/shard_map/all_to_all | solution.py:48
  33.8 13.4 %collective-permute-start.3 = (s32[1,8]{1,0:T(1,128)S(1)}, s32[1,8]{1,0:T(1,128)S(1)}, u32[]{:S(2)}, u32[]{:S(2)}) collective-permute-start(s32[1,8]{1,0:T(1,128)S(1)} %copy-done.1), channel_id=1, source_target_pairs={{0,8},{8,0},{1,9},{9,1},{2,10},{10,2},{3,11},{11,3},{4,12},{12,4},... | collective-permute-start | bytes 104 | tf_op jit(solution)/shard_map/ppermute | solution.py:39
  36.0 12.1 %collective-permute-start = (bf16[2,16,256]{2,1,0:T(8,128)(2,1)S(1)}, bf16[2,16,256]{2,1,0:T(8,128)(2,1)S(1)}, u32[]{:S(2)}, u32[]{:S(2)}) collective-permute-start(bf16[2,16,256]{2,1,0:T(8,128)(2,1)S(1)} %bitcast_reduce_fusion.1), channel_id=1, source_target_pairs={{0,1008},{16,0},{32,16},{48,32},{64,48},{80,64},{96,80},{112,96},{... | collective-permute-start | bytes 49160 | tf_op jit(solution)/shard_map/ppermute | solution.py:16
  48.1 5.8 %collective-permute-start.1 = (bf16[4,16,256]{2,1,0:T(8,128)(2,1)S(1)}, bf16[4,16,256]{2,1,0:T(8,128)(2,1)S(1)}, u32[]{:S(2)}, u32[]{:S(2)}) collective-permute-start(bf16[4,16,256]{2,1,0:T(8,128)(2,1)S(1)} %pad_maximum_fusion.2), channel_id=1, source_target_pairs={{0,992},{16,1008},{32,0},{48,16},{64,32},{80,48},{96,64},{112,80},... | collective-permute-start | bytes 98312 | tf_op jit(solution)/shard_map/ppermute | solution.py:16
  54.0 9.7 %collective-permute-start.2 = (bf16[8,16,256]{2,1,0:T(8,128)(2,1)S(1)}, bf16[8,16,256]{2,1,0:T(8,128)(2,1)S(1)}, u32[]{:S(2)}, u32[]{:S(2)}) collective-permute-start(bf16[8,16,256]{2,1,0:T(8,128)(2,1)S(1)} %pad_maximum_fusion.1), channel_id=1, source_target_pairs={{0,960},{16,976},{32,992},{48,1008},{64,0},{80,16},{96,32},{112,48... | collective-permute-start | bytes 196616 | tf_op jit(solution)/shard_map/ppermute | solution.py:16
  65.7 18.4 %all-to-all-start.2 = ((f32[16,24,128]{2,1,0:T(8,128)}), f32[16,24,128]{2,1,0:T(8,128)S(1)}, u32[]{:S(2)}, u32[]{:S(2)}) async-start(f32[16,24,128]{2,1,0:T(8,128)} %maximum_maximum_fusion), calls=%async_computation.2 | async-start | bytes 393216 | tf_op jit(solution)/shard_map/all_to_all | solution.py:71
  98.3 35.2 %all-to-all-start.4 = ((bf16[16,128,256]{2,1,0:T(8,128)(2,1)}), bf16[16,128,256]{2,1,0:T(8,128)(2,1)S(1)}, u32[]{:S(2)}, u32[]{:S(2)}) async-start(bf16[16,128,256]{2,1,0:T(8,128)(2,1)} %bitcast.17), calls=%async_computation.4 | async-start | bytes 2097152 | tf_op jit(solution)/shard_map/all_to_all | solution.py:116
  103.5 11.4 %collective-permute-start.4 = (bf16[8,16,256]{2,0,1:T(8,128)(2,1)S(1)}, bf16[8,16,256]{2,0,1:T(8,128)(2,1)S(1)}, u32[]{:S(2)}, u32[]{:S(2)}) collective-permute-start(bf16[8,16,256]{2,0,1:T(8,128)(2,1)S(1)} %slice.144), channel_id=1, source_target_pairs={{0,64},{16,80},{32,96},{48,112},{64,128},{80,144},{96,160},{112,17... | collective-permute-start | bytes 196616 | tf_op jit(solution)/shard_map/ppermute | solution.py:16
  115.0 10.7 %collective-permute-start.5 = (bf16[4,16,256]{2,0,1:T(4,128)(2,1)S(1)}, bf16[4,16,256]{2,0,1:T(4,128)(2,1)S(1)}, u32[]{:S(2)}, u32[]{:S(2)}) collective-permute-start(bf16[4,16,256]{2,0,1:T(4,128)(2,1)S(1)} %slice.145), channel_id=1, source_target_pairs={{0,32},{16,48},{32,64},{48,80},{64,96},{80,112},{96,128},{112,144}... | collective-permute-start | bytes 98312 | tf_op jit(solution)/shard_map/ppermute | solution.py:16
  125.7 7.8 %collective-permute-start.6 = (bf16[2,16,256]{2,0,1:T(2,128)(2,1)S(1)}, bf16[2,16,256]{2,0,1:T(2,128)(2,1)S(1)}, u32[]{:S(2)}, u32[]{:S(2)}) collective-permute-start(bf16[2,16,256]{2,0,1:T(2,128)(2,1)S(1)} %slice.146), channel_id=1, source_target_pairs={{0,16},{16,32},{32,48},{48,64},{64,80},{80,96},{96,112},{112,128},... | collective-permute-start | bytes 49160 | tf_op jit(solution)/shard_map/ppermute | solution.py:16
  134.2 16.8 %all-to-all-start.5 = ((bf16[16,16,256]{2,1,0:T(8,128)(2,1)}), bf16[16,16,256]{2,1,0:T(8,128)(2,1)S(1)}, u32[]{:S(2)}, u32[]{:S(2)}) async-start(bf16[16,16,256]{2,1,0:T(8,128)(2,1)} %bitcast.23), calls=%async_computation.5 | async-start | bytes 262144 | tf_op jit(solution)/shard_map/all_to_all | solution.py:116

commit v3 on v2

v3 whole, which is shorter than its diff:
```python
import jax
import jax.numpy as jnp
from jax import lax
from jax.sharding import Mesh
from jax.sharding import PartitionSpec as P

SCALE = 50.0
EPS = 1e-06
WINDOW = 8
CORES = 2
TENSOR = ("u", "par")
MEMBERS = ("core",) + TENSOR
ALIKE = ("core", "u")


def shift_chips(value, by):
    chips = lax.axis_size("chip")
    return lax.ppermute(value, "chip", [(i, (i + by) % chips) for i in range(chips)])


def swap(value, odd):
    peers = lax.axis_size(TENSOR)
    return lax.ppermute(value, TENSOR, [(t, (t + (1 if t % 2 == odd else -1)) % peers) for t in range(peers)])


def halves(value, parts):
    out = []
    for _ in range(parts):
        top = lax.reduce_precision(value, 8, 7)
        out.append(top.astype(jnp.bfloat16))
        value = value - top
    return out


def on_device(q_ctx, p_ctx, out_weight, neighbours, positive):
    f32, bf16 = jnp.float32, jnp.bfloat16
    q_rows, p_rows = q_ctx.shape[0], p_ctx.shape[0]
    listed = neighbours.shape[1]
    slots = listed * p_rows
    tensors = lax.axis_size(TENSOR)
    members = CORES * tensors
    feats = out_weight.shape[1] // members
    q_share = q_rows // tensors
    core, chip = lax.axis_index("core"), lax.axis_index("chip")

    other = lax.ppermute(neighbours, "core", [(0, 1), (1, 0)])
    lists = jnp.concatenate([neighbours, other], axis=0)
    lists = jnp.where(core == 0, lists, lists[::-1])

    def project(rows):
        part = jnp.dot(rows, out_weight, preferred_element_type=f32).astype(bf16)
        return part.reshape(rows.shape[0], members, feats).transpose(1, 0, 2)

    def reduce_over_tensor(part):
        got = lax.all_to_all(part, MEMBERS, 0, 0)
        got = got.reshape(CORES, tensors, part.shape[1], feats).astype(f32)
        return jnp.sum(got, axis=1).astype(bf16)

    p_part = project(p_ctx)
    q_ctx, p_part = lax.optimization_barrier((q_ctx, p_part))
    window = reduce_over_tensor(p_part)
    parity = lax.axis_index("par")
    q_part = project(q_ctx).reshape(CORES, tensors // 2, 2, q_rows, feats)
    keep = jnp.where(parity == 0, q_part[:, :, 0], q_part[:, :, 1])
    send = jnp.where(parity == 0, q_part[:, :, 1], q_part[:, :, 0])
    got = jnp.stack([swap(send[0], 0), swap(send[1], 1)])
    q_pair = (keep.astype(f32) + got.astype(f32)).astype(bf16)
    q_pair = lax.all_to_all(q_pair.reshape(members // 2, q_rows, feats), ALIKE, 0, 0)
    q_pre = jnp.sum(q_pair.reshape(CORES, tensors // 2, q_rows, feats).astype(f32), axis=1).astype(bf16)

    window = jnp.concatenate([window] + [shift_chips(window, -by) for by in range(1, WINDOW // 2)], axis=0)
    window = jnp.concatenate([window, shift_chips(window, -(WINDOW // 2))], axis=0)
    spots = (lists - CORES * chip) % (CORES * lax.axis_size("chip"))
    cand = window[spots].reshape(CORES, slots, feats)

    raw = jnp.einsum("kqf,kcf->kqc", q_pre, cand, preferred_element_type=f32)
    q_sq = jnp.sum(jnp.square(q_pre.astype(f32)), axis=-1)
    c_sq = jnp.sum(jnp.square(cand.astype(f32)), axis=-1)
    q_sq = jnp.pad(q_sq.reshape(CORES, tensors, 1, q_share), ((0, 0), (0, 0), (0, 0), (0, slots - q_share)))
    c_sq = jnp.broadcast_to(c_sq[:, None, None, :], (CORES, tensors, 1, slots))
    extra = jnp.zeros((CORES, tensors, 6, slots), f32)
    sums = jnp.concatenate([raw.reshape(CORES, tensors, q_share, slots), q_sq, c_sq, extra], axis=2)
    sums = lax.all_to_all(sums.reshape(members, q_share + 8, slots), MEMBERS, 0, 0)
    sums = jnp.sum(sums, axis=0)
    raw = sums[:q_share]
    inv_q = lax.rsqrt(sums[q_share, :q_share] + EPS)
    inv_c = lax.rsqrt(sums[q_share + 1] + EPS)

    scores = raw * (SCALE * inv_q)[:, None] * inv_c[None, :]
    lse = jnp.log(jnp.sum(jnp.exp(scores), axis=-1))
    pos = lax.dynamic_slice_in_dim(positive, lax.axis_index(TENSOR) * q_share, q_share)
    onehot = (jnp.arange(slots, dtype=jnp.int32)[None, :] == pos[:, None]).astype(f32)
    loss = lse - jnp.sum(scores * onehot, axis=-1)
    dscore = jnp.exp(scores - lse[:, None]) - onehot
    coef = lax.reduce_precision(dscore * (SCALE * inv_q)[:, None] * inv_c[None, :], 8, 7)
    weighted = coef * raw
    q_inner = jnp.square(inv_q) * jnp.sum(weighted, axis=-1)
    c_inner = jnp.square(inv_c) * jnp.sum(weighted, axis=0)

    row = jnp.concatenate(halves(q_inner, 2) + halves(loss, 3))
    row = jnp.pad(row, (0, slots - row.shape[0]))
    c_rows = jnp.stack([row] + halves(c_inner, 2) + [jnp.zeros((slots,), bf16)] * 5)
    told = jnp.concatenate([coef.astype(bf16), c_rows], axis=0)
    told = lax.all_to_all(jnp.broadcast_to(told[None], (members,) + told.shape), MEMBERS, 0, 0)
    told = told.reshape(CORES, tensors, q_share + 8, slots)
    coef = told[:, :, :q_share].reshape(CORES, q_rows, slots)
    row = told[:, :, q_share].astype(f32)
    q_inner = (row[..., :q_share] + row[..., q_share : 2 * q_share]).reshape(CORES, q_rows, 1)
    loss = row[..., 2 * q_share : 3 * q_share] + row[..., 3 * q_share : 4 * q_share] + row[..., 4 * q_share : 5 * q_share]
    losses = jnp.where(core == 0, loss[0], loss[1]).reshape(q_rows)
    c_inner = jnp.sum(told[:, :, q_share + 1 : q_share + 3].astype(f32), axis=(1, 2))[..., None]

    dq = jnp.einsum("kqc,kcf->kqf", coef, cand, preferred_element_type=f32)
    dq = (dq - q_inner * q_pre.astype(f32)).astype(bf16)
    dc = jnp.einsum("kqc,kqf->kcf", coef, q_pre, preferred_element_type=f32)
    dc = (dc - c_inner * cand.astype(f32)).astype(bf16)
    match = (jnp.arange(WINDOW * CORES, dtype=jnp.int32)[:, None, None] == spots[None]).astype(bf16)
    dwin = jnp.einsum("wks,kspf->wpf", match, dc.reshape(CORES, listed, p_rows, feats), preferred_element_type=f32)

    half = dwin.shape[0] // 2
    dwin = dwin[:half] + shift_chips(dwin[half:].astype(bf16), WINDOW // 2).astype(f32)
    dwin = dwin.reshape(WINDOW // 2, CORES, p_rows, feats)
    away = [shift_chips(dwin[by].astype(bf16), by) for by in range(1, WINDOW // 2)]
    dp = sum([part.astype(f32) for part in away], dwin[0]).astype(bf16)

    def unproject(part):
        weight = out_weight.reshape(out_weight.shape[0], members, feats)
        return jnp.einsum("mrf,hmf->rh", part, weight, preferred_element_type=f32).astype(bf16)

    dq = jnp.broadcast_to(dq[:, None], (CORES, tensors // 2, q_rows, feats))
    dq = lax.all_to_all(dq.reshape(members // 2, q_rows, feats), ALIKE, 0, 0)
    dq, dp = lax.optimization_barrier((dq, dp))
    dp = jnp.broadcast_to(dp[:, None], (CORES, tensors, p_rows, feats))
    dp = lax.all_to_all(dp.reshape(members, p_rows, feats), MEMBERS, 0, 0)
    dq = dq.reshape(CORES, tensors // 2, q_rows, feats)
    got = jnp.stack([swap(dq[0], 0), swap(dq[1], 1)])
    dq = jnp.where(parity == 0, jnp.stack([dq, got], axis=2), jnp.stack([got, dq], axis=2))
    q_grad = unproject(dq.reshape(members, q_rows, feats))
    return q_grad, unproject(dp), losses


def solution(mesh):
    dp, tensors = mesh.shape["dp"], mesh.shape["tensor"]
    fine = Mesh(mesh.devices.reshape(dp // CORES, CORES, tensors // 2, 2), ("chip",) + MEMBERS)
    rows = ("chip", "core")
    placed = (P(rows, TENSOR), P(rows, TENSOR), P(TENSOR, None), P(rows, None), P(rows))
    return jax.shard_map(
        on_device,
        mesh=fine,
        in_specs=placed,
        out_specs=(P(rows, TENSOR), P(rows, TENSOR), P(rows)),
        check_vma=False,
    )
```

time: 156 us -> 177 us (1.13)
  starting transfers between devices: 79.9 us -> 102 us
  matrix products: 15 us -> 13 us
    ppermute x0 -> x4, starting transfers between devices: none -> 15.4 us  [swap(): lax.ppermute(value, TENSOR, [(t, (t + (1 if t % 2 == odd else -1)) % peer...]
    ppermute x0 -> x4, waiting for transfers between devices: none -> 7.79 us  [swap(): lax.ppermute(value, TENSOR, [(t, (t + (1 if t % 2 == odd else -1)) % peer...]
    all_to_all x3 -> x4, starting transfers between devices: 24.2 us -> 31.8 us  [the longest x1 11.2 us: on_device(): lax.all_to_all(sums.reshape(members, q_share + 8, slots), MEMBERS, 0, 0)]
    all_to_all x2 -> x1, starting transfers between devices: 22.2 us -> 17.5 us  [reduce_over_tensor(): got = lax.all_to_all(part, MEMBERS, 0, 0)]
    ppermute x6 -> x8, starting transfers between devices: 31.4 us -> 35.5 us  [shift_chips(): lax.ppermute(value, 'chip', [(i, (i + by) % chips) for i in range(chips)])]
    all_to_all x2 -> x1, waiting for transfers between devices: 3.32 us -> 0.01 us  [reduce_over_tensor(): got = lax.all_to_all(part, MEMBERS, 0, 0)]
    all_to_all x3 -> x4, waiting for transfers between devices: 11.1 us -> 8.2 us  [the longest x1 8.2 us: on_device(): lax.all_to_all(sums.reshape(members, q_share + 8, slots), MEMBERS, 0, 0)]
    dot_general x2, matrix products: 8.36 us -> 6.33 us  [unproject(): jnp.einsum('mrf,hmf->rh', part, weight, preferred_element_type=f32)]
  transfers between devices with their start and end apart: 12 -> 18, of which waited for: 9 -> 9; matrix products, arithmetic and copies ran while one was open for 7% -> 6% of each run, Pallas kernels for 0% -> 0%
where the time goes in v3:
time: 177 us; the launch traced here: 176 us
  starting transfers between devices  102 us (58%)
  waiting for transfers between devices  40.3 us (23%)
  matrix products  13 us (7%)
  blocking collectives  12.1 us (7%)
  local copies, waits for them, and re-layouts  4.3 us (2%)
  other arithmetic  3.1 us (2%)
    ppermute x8, starting transfers between devices, shift_chips(): lax.ppermute(value, 'chip', [(i, (i + by) % chips) for i in range(chips)])  35.5 us
    ppermute x8, waiting for transfers between devices, shift_chips(): lax.ppermute(value, 'chip', [(i, (i + by) % chips) for i in range(chips)])  24.3 us
    all_to_all x1, starting transfers between devices, reduce_over_tensor(): got = lax.all_to_all(part, MEMBERS, 0, 0)  17.5 us
    ppermute x4, starting transfers between devices, swap(): lax.ppermute(value, TENSOR, [(t, (t + (1 if t % 2 == odd else -1)) % peer...  15.4 us
    all_to_all x1, blocking collectives, on_device(): lax.all_to_all(jnp.broadcast_to(told[None], (members,) + told.shape), MEM...  12.1 us
    all_to_all x1, starting transfers between devices, on_device(): lax.all_to_all(sums.reshape(members, q_share + 8, slots), MEMBERS, 0, 0)  11.2 us
    all_to_all x1, starting transfers between devices, on_device(): dp = lax.all_to_all(dp.reshape(members, p_rows, feats), MEMBERS, 0, 0)  9.06 us
    all_to_all x1, waiting for transfers between devices, on_device(): lax.all_to_all(sums.reshape(members, q_share + 8, slots), MEMBERS, 0, 0)  8.2 us
  transfers between devices with their start and end apart: 18, of which 9 were waited for; matrix products, arithmetic and copies ran while one was open for 6% of the time, Pallas kernels for 0%

profile of v3, /device:TPU:1, one launch (start us, length us, event | category | flops | bytes accessed | tf_op | source)
XLA Modules:
  0.0 176.2 jit_solution(8883946592019771427)
XLA Ops:
  0.7 2.9 %convolution_convert_fusion.1 = bf16[16,4096]{1,0:T(8,128)(2,1)S(1)} fusion(bf16[16,512]{1,0:T(8,128)(2,1)} %param.6, bf16[512,4096]{1,0:T(8,128)(2,1)} %param.7), kind=kOutput, calls=%fused_computation.2 | convolution fusion | flops 67174400 | bytes 4341760 | tf_op jit(solution)/shard_map/dot_general | solution.py:51
  3.6 0.7 copy.83
  4.2 17.5 %all-to-all-start.1 = ((bf16[16,16,256]{2,1,0:T(8,128)(2,1)}), bf16[16,16,256]{2,1,0:T(8,128)(2,1)S(1)}, u32[]{:S(2)}, u32[]{:S(2)}) async-start(bf16[16,16,256]{2,1,0:T(8,128)(2,1)} %bitcast.102), calls=%async_computation.1 | async-start | bytes 262144 | tf_op jit(solution)/shard_map/all_to_all | solution.py:55
  21.7 2.1 %collective-permute-start.6 = (s32[1,8]{1,0:T(1,128)S(1)}, s32[1,8]{1,0:T(1,128)S(1)}, u32[]{:S(2)}, u32[]{:S(2)}) collective-permute-start(s32[1,8]{1,0:T(1,128)S(1)} %copy-done.2), channel_id=1, source_target_pairs={{0,8},{8,0},{1,9},{9,1},{2,10},{10,2},{3,11},{11,3},{4,12},{12,4},... | collective-permute-start | bytes 104 | tf_op jit(solution)/shard_map/ppermute | solution.py:46
  23.8 2.9 %convolution_convert_fusion = bf16[128,4096]{1,0:T(8,128)(2,1)S(1)} fusion(bf16[128,512]{1,0:T(8,128)(2,1)S(1)} %copy-done, bf16[512,4096]{1,0:T(8,128)(2,1)} %param.7), kind=kOutput, calls=%fused_computation.1 | convolution fusion | flops 537395200 | bytes 5373952 | tf_op jit(solution)/shard_map/dot_general | solution.py:51
  27.0 3.4 %collective-permute-start = (bf16[4,128,256]{2,1,0:T(8,128)(2,1)S(1)}, bf16[4,128,256]{2,1,0:T(8,128)(2,1)S(1)}, u32[]{:S(2)}, u32[]{:S(2)}) collective-permute-start(bf16[4,128,256]{2,1,0:T(8,128)(2,1)S(1)} %get-tuple-element.28), channel_id=1, source_target_pairs={{0,1},{1,0},{2,3},{3,2},{4,5},{5,4},{6,7},{7,6},{8,9},{9,8},{10,11... | collective-permute-start | bytes 786440 | tf_op jit(solution)/shard_map/ppermute | solution.py:23
  30.4 4.3 %collective-permute-start.1 = (bf16[4,128,256]{2,1,0:T(8,128)(2,1)S(1)}, bf16[4,128,256]{2,1,0:T(8,128)(2,1)S(1)}, u32[]{:S(2)}, u32[]{:S(2)}) collective-permute-start(bf16[4,128,256]{2,1,0:T(8,128)(2,1)S(1)} %get-tuple-element.29), channel_id=1, source_target_pairs={{0,7},{1,2},{2,1},{3,4},{4,3},{5,6},{6,5},{7,0},{8,15},{9,10},{10,... | collective-permute-start | bytes 786440 | tf_op jit(solution)/shard_map/ppermute | solution.py:23
  35.0 1.6 collective-permute-done
  36.6 4.4 %collective-permute-done.1 = bf16[4,128,256]{2,1,0:T(8,128)(2,1)S(1)} collective-permute-done((bf16[4,128,256]{2,1,0:T(8,128)(2,1)S(1)}, bf16[4,128,256]{2,1,0:T(8,128)(2,1)S(1)}, u32[]{:S(2)}, u32[]{:S(2)}) %collective-permute-start.1) | collective-permute-done | bytes 262176 | tf_op jit(solution)/shard_map/ppermute | solution.py:23
  41.0 1.0 fusion.19
  42.0 7.1 %all-to-all-start = ((bf16[8,128,256]{2,1,0:T(8,128)(2,1)}), bf16[8,128,256]{2,1,0:T(8,128)(2,1)S(1)}, u32[]{:S(2)}, u32[]{:S(2)}) async-start(bf16[8,128,256]{2,1,0:T(8,128)(2,1)} %fusion.19), calls=%async_computation | async-start | bytes 1048576 | tf_op jit(solution)/shard_map/all_to_all | solution.py:68
  49.1 11.3 %collective-permute-start.2 = (bf16[2,16,256]{2,1,0:T(8,128)(2,1)S(1)}, bf16[2,16,256]{2,1,0:T(8,128)(2,1)S(1)}, u32[]{:S(2)}, u32[]{:S(2)}) collective-permute-start(bf16[2,16,256]{2,1,0:T(8,128)(2,1)S(1)} %bitcast_reduce_fusion.1), channel_id=1, source_target_pairs={{0,1008},{16,0},{32,16},{48,32},{64,48},{80,64},{96,80},{112,96},{... | collective-permute-start | bytes 49160 | tf_op jit(solution)/shard_map/ppermute | solution.py:18
  60.4 2.2 %collective-permute-start.3 = (bf16[2,16,256]{2,1,0:T(8,128)(2,1)S(1)}, bf16[2,16,256]{2,1,0:T(8,128)(2,1)S(1)}, u32[]{:S(2)}, u32[]{:S(2)}) collective-permute-start(bf16[2,16,256]{2,1,0:T(8,128)(2,1)S(1)} %bitcast_reduce_fusion.1), channel_id=1, source_target_pairs={{0,992},{16,1008},{32,0},{48,16},{64,32},{80,48},{96,64},{112,80},... | collective-permute-start | bytes 49160 | tf_op jit(solution)/shard_map/ppermute | solution.py:18
  62.6 3.4 %collective-permute-start.4 = (bf16[2,16,256]{2,1,0:T(8,128)(2,1)S(1)}, bf16[2,16,256]{2,1,0:T(8,128)(2,1)S(1)}, u32[]{:S(2)}, u32[]{:S(2)}) collective-permute-start(bf16[2,16,256]{2,1,0:T(8,128)(2,1)S(1)} %bitcast_reduce_fusion.1), channel_id=1, source_target_pairs={{0,976},{16,992},{32,1008},{48,0},{64,16},{80,32},{96,48},{112,64}... | collective-permute-start | bytes 49160 | tf_op jit(solution)/shard_map/ppermute | solution.py:18
  66.0 2.9 %collective-permute-done.4 = bf16[2,16,256]{2,1,0:T(8,128)(2,1)S(1)} collective-permute-done((bf16[2,16,256]{2,1,0:T(8,128)(2,1)S(1)}, bf16[2,16,256]{2,1,0:T(8,128)(2,1)S(1)}, u32[]{:S(2)}, u32[]{:S(2)}) %collective-permute-start.4) | collective-permute-done | bytes 16416 | tf_op jit(solution)/shard_map/ppermute | solution.py:18
  68.9 3.6 %collective-permute-start.5 = (bf16[8,16,256]{2,1,0:T(8,128)(2,1)S(1)}, bf16[8,16,256]{2,1,0:T(8,128)(2,1)S(1)}, u32[]{:S(2)}, u32[]{:S(2)}) collective-permute-start(bf16[8,16,256]{2,1,0:T(8,128)(2,1)S(1)} %pad_maximum_fusion.1), channel_id=1, source_target_pairs={{0,960},{16,976},{32,992},{48,1008},{64,0},{80,16},{96,32},{112,48... | collective-permute-start | bytes 196616 | tf_op jit(solution)/shard_map/ppermute | solution.py:18
  72.6 5.5 %collective-permute-done.5 = bf16[8,16,256]{2,1,0:T(8,128)(2,1)S(1)} collective-permute-done((bf16[8,16,256]{2,1,0:T(8,128)(2,1)S(1)}, bf16[8,16,256]{2,1,0:T(8,128)(2,1)S(1)}, u32[]{:S(2)}, u32[]{:S(2)}) %collective-permute-start.5) | collective-permute-done | bytes 65568 | tf_op jit(solution)/shard_map/ppermute | solution.py:18
  78.1 0.6 gather_fusion
  78.6 0.1 multiply_reduce_fusion
  78.9 0.1 fusion.20
  79.0 0.2 fusion.44
  79.3 0.8 maximum_maximum_fusion
  80.1 11.2 %all-to-all-start.2 = ((f32[16,24,128]{2,1,0:T(8,128)}), f32[16,24,128]{2,1,0:T(8,128)S(1)}, u32[]{:S(2)}, u32[]{:S(2)}) async-start(f32[16,24,128]{2,1,0:T(8,128)} %maximum_maximum_fusion), calls=%async_computation.2 | async-start | bytes 393216 | tf_op jit(solution)/shard_map/all_to_all | solution.py:83
  91.4 8.2 %all-to-all-done.2 = f32[16,24,128]{2,1,0:T(8,128)S(1)} async-done(((f32[16,24,128]{2,1,0:T(8,128)}), f32[16,24,128]{2,1,0:T(8,128)S(1)}, u32[]{:S(2)}, u32[]{:S(2)}) %all-to-all-start.2) | async-done | bytes 196640 | tf_op jit(solution)/shard_map/all_to_all | solution.py:83
  99.6 0.2 select_reduce_fusion
  99.8 0.2 fusion.29
  100.3 12.1 %all_to_all.30 = bf16[16,24,128]{2,1,0:T(8,128)(2,1)S(1)} all-to-all(bf16[16,24,128]{2,1,0:T(8,128)(2,1)S(1)} %broadcast_in_dim.21), channel_id=1, replica_groups=mesh['chip'=64,'core'=2,'u'=4,'par'=2] {'core','u','par'}, dimensions={0} | all-to-all | bytes 196608 | tf_op jit(solution)/shard_map/all_to_all | solution.py:104
  112.4 0.2 fusion.45
  112.8 0.2 fusion.9
  113.0 0.8 broadcast_in_dim.22
  113.8 4.5 %all-to-all-start.4 = ((bf16[8,128,256]{2,1,0:T(8,128)(2,1)}), bf16[8,128,256]{2,1,0:T(8,128)(2,1)S(1)}, u32[]{:S(2)}, u32[]{:S(2)}) async-start(bf16[8,128,256]{2,1,0:T(8,128)(2,1)} %bitcast.25), calls=%async_computation.4 | async-start | bytes 1048576 | tf_op jit(solution)/shard_map/all_to_all | solution.py:131
  118.3 0.1 subtract_convert_fusion
  118.4 0.3 convolution_bitcast_fusion
  118.7 2.1 %collective-permute-start.7 = (bf16[8,16,256]{2,0,1:T(8,128)(2,1)S(1)}, bf16[8,16,256]{2,0,1:T(8,128)(2,1)S(1)}, u32[]{:S(2)}, u32[]{:S(2)}) collective-permute-start(bf16[8,16,256]{2,0,1:T(8,128)(2,1)S(1)} %slice.190), channel_id=1, source_target_pairs={{0,64},{16,80},{32,96},{48,112},{64,128},{80,144},{96,160},{112,17... | collective-permute-start | bytes 196616 | tf_op jit(solution)/shard_map/ppermute | solution.py:18
  120.8 9.5 %collective-permute-done.7 = bf16[8,16,256]{2,0,1:T(8,128)(2,1)S(1)} collective-permute-done((bf16[8,16,256]{2,0,1:T(8,128)(2,1)S(1)}, bf16[8,16,256]{2,0,1:T(8,128)(2,1)S(1)}, u32[]{:S(2)}, u32[]{:S(2)}) %collective-permute-start.7) | collective-permute-done | bytes 65568 | tf_op jit(solution)/shard_map/ppermute | solution.py:18
  130.4 8.8 %collective-permute-start.10 = (bf16[2,16,256]{2,0,1:T(2,128)(2,1)S(1)}, bf16[2,16,256]{2,0,1:T(2,128)(2,1)S(1)}, u32[]{:S(2)}, u32[]{:S(2)}) collective-permute-start(bf16[2,16,256]{2,0,1:T(2,128)(2,1)S(1)} %get-tuple-element.31), channel_id=1, source_target_pairs={{0,48},{16,64},{32,80},{48,96},{64,112},{80,128},{96,144},{112,160... | collective-permute-start | bytes 49160 | tf_op jit(solution)/shard_map/ppermute | solution.py:18
  139.2 1.9 %collective-permute-start.8 = (bf16[2,16,256]{2,0,1:T(2,128)(2,1)S(1)}, bf16[2,16,256]{2,0,1:T(2,128)(2,1)S(1)}, u32[]{:S(2)}, u32[]{:S(2)}) collective-permute-start(bf16[2,16,256]{2,0,1:T(2,128)(2,1)S(1)} %get-tuple-element.30), channel_id=1, source_target_pairs={{0,16},{16,32},{32,48},{48,64},{64,80},{80,96},{96,112},{112,128},... | collective-permute-start | bytes 49160 | tf_op jit(solution)/shard_map/ppermute | solution.py:18
  141.1 2.2 %collective-permute-start.9 = (bf16[2,16,256]{2,0,1:T(2,128)(2,1)S(1)}, bf16[2,16,256]{2,0,1:T(2,128)(2,1)S(1)}, u32[]{:S(2)}, u32[]{:S(2)}) collective-permute-start(bf16[2,16,256]{2,0,1:T(2,128)(2,1)S(1)} %get-tuple-element.32), channel_id=1, source_target_pairs={{0,32},{16,48},{32,64},{48,80},{64,96},{80,112},{96,128},{112,144}... | collective-permute-start | bytes 49160 | tf_op jit(solution)/shard_map/ppermute | solution.py:18
  143.3 3.7 %collective-permute-done.8 = bf16[2,16,256]{2,0,1:T(2,128)(2,1)S(1)} collective-permute-done((bf16[2,16,256]{2,0,1:T(2,128)(2,1)S(1)}, bf16[2,16,256]{2,0,1:T(2,128)(2,1)S(1)}, u32[]{:S(2)}, u32[]{:S(2)}) %collective-permute-start.8) | collective-permute-done | bytes 16416 | tf_op jit(solution)/shard_map/ppermute | solution.py:18
  147.0 2.8 %collective-permute-done.9 = bf16[2,16,256]{2,0,1:T(2,128)(2,1)S(1)} collective-permute-done((bf16[2,16,256]{2,0,1:T(2,128)(2,1)S(1)}, bf16[2,16,256]{2,0,1:T(2,128)(2,1)S(1)}, u32[]{:S(2)}, u32[]{:S(2)}) %collective-permute-start.9) | collective-permute-done | bytes 16416 | tf_op jit(solution)/shard_map/ppermute | solution.py:18
  149.8 0.7 broadcast_in_dim.23
  150.5 9.1 %all-to-all-start.5 = ((bf16[16,16,256]{2,1,0:T(8,128)(2,1)}), bf16[16,16,256]{2,1,0:T(8,128)(2,1)S(1)}, u32[]{:S(2)}, u32[]{:S(2)}) async-start(bf16[16,16,256]{2,1,0:T(8,128)(2,1)} %bitcast.36), calls=%async_computation.5 | async-start | bytes 262144 | tf_op jit(solution)/shard_map/all_to_all | solution.py:134
  159.6 0.6 select_n.73
  160.2 3.3 %collective-permute-start.11 = (bf16[4,128,256]{2,1,0:T(8,128)(2,1)S(1)}, bf16[4,128,256]{2,1,0:T(8,128)(2,1)S(1)}, u32[]{:S(2)}, u32[]{:S(2)}) collective-permute-start(bf16[4,128,256]{2,1,0:T(8,128)(2,1)S(1)} %get-tuple-element.26), channel_id=1, source_target_pairs={{0,1},{1,0},{2,3},{3,2},{4,5},{5,4},{6,7},{7,6},{8,9},{9,8},{10,11... | collective-permute-start | bytes 786440 | tf_op jit(solution)/shard_map/ppermute | solution.py:23
  163.5 4.3 %collective-permute-start.12 = (bf16[4,128,256]{2,1,0:T(8,128)(2,1)S(1)}, bf16[4,128,256]{2,1,0:T(8,128)(2,1)S(1)}, u32[]{:S(2)}, u32[]{:S(2)}) collective-permute-start(bf16[4,128,256]{2,1,0:T(8,128)(2,1)S(1)} %get-tuple-element.27), channel_id=1, source_target_pairs={{0,7},{1,2},{2,1},{3,4},{4,3},{5,6},{6,5},{7,0},{8,15},{9,10},{10,... | collective-permute-start | bytes 786440 | tf_op jit(solution)/shard_map/ppermute | solution.py:23
  167.8 4.1 %fusion.16 = bf16[16,512]{1,0:T(8,128)(2,1)} fusion(bf16[16,16,256]{2,1,0:T(8,128)(2,1)S(1)} %all-to-all-done.5, bf16[64,16,8,256]{3,2,1,0:T(8,128)(2,1)} %bitcast.104), kind=kOutput, calls=%fused_computation.15 | convolution fusion | flops 67117056 | bytes 4341760 | tf_op jit(solution)/shard_map/mrf,hmf->rh/dot_general | solution.py:128
  172.0 1.8 %collective-permute-done.12 = bf16[4,128,256]{2,1,0:T(8,128)(2,1)S(1)} collective-permute-done((bf16[4,128,256]{2,1,0:T(8,128)(2,1)S(1)}, bf16[4,128,256]{2,1,0:T(8,128)(2,1)S(1)}, u32[]{:S(2)}, u32[]{:S(2)}) %collective-permute-start.12) | collective-permute-done | bytes 262176 | tf_op jit(solution)/shard_map/ppermute | solution.py:23
  174.0 2.2 %fusion.10 = bf16[128,512]{1,0:T(8,128)(2,1)} fusion(bf16[16,128,256]{2,1,0:T(8,128)(2,1)S(1)} %bitcast.112, bf16[64,16,8,256]{3,2,1,0:T(8,128)(2,1)S(1)} %bitcast.105), kind=kOutput, calls=%fused_computation.13 | convolution fusion | flops 536936448 | bytes 5373952 | tf_op jit(solution)/shard_map/mrf,hmf->rh/dot_general | solution.py:128
  (70 shorter events, 1.7 us)
Async XLA Ops:
  0.6 23.2 %copy-start = (bf16[128,512]{1,0:T(8,128)(2,1)S(1)}, bf16[128,512]{1,0:T(8,128)(2,1)}, u32[]{:S(2)}) copy-start(bf16[128,512]{1,0:T(8,128)(2,1)} %param.5) | copy-start | bytes 393220
  0.6 21.1 %copy-start.2 = (s32[1,8]{1,0:T(1,128)S(1)}, s32[1,8]{1,0:T(1,128)}, u32[]{:S(2)}) copy-start(s32[1,8]{1,0:T(1,128)} %param.8) | copy-start | bytes 100
  4.2 37.8 %all-to-all-start.1 = ((bf16[16,16,256]{2,1,0:T(8,128)(2,1)}), bf16[16,16,256]{2,1,0:T(8,128)(2,1)S(1)}, u32[]{:S(2)}, u32[]{:S(2)}) async-start(bf16[16,16,256]{2,1,0:T(8,128)(2,1)} %bitcast.102), calls=%async_computation.1 | async-start | bytes 262144 | tf_op jit(solution)/shard_map/all_to_all | solution.py:55
  21.7 13.1 %collective-permute-start.6 = (s32[1,8]{1,0:T(1,128)S(1)}, s32[1,8]{1,0:T(1,128)S(1)}, u32[]{:S(2)}, u32[]{:S(2)}) collective-permute-start(s32[1,8]{1,0:T(1,128)S(1)} %copy-done.2), channel_id=1, source_target_pairs={{0,8},{8,0},{1,9},{9,1},{2,10},{10,2},{3,11},{11,3},{4,12},{12,4},... | collective-permute-start | bytes 104 | tf_op jit(solution)/shard_map/ppermute | solution.py:46
  27.0 64.3 %copy-start.3 = (s32[128]{0:T(128)S(1)}, s32[128]{0:T(128)}, u32[]{:S(2)}) copy-start(s32[128]{0:T(128)} %param.9) | copy-start | bytes 1540
  27.0 9.6 %collective-permute-start = (bf16[4,128,256]{2,1,0:T(8,128)(2,1)S(1)}, bf16[4,128,256]{2,1,0:T(8,128)(2,1)S(1)}, u32[]{:S(2)}, u32[]{:S(2)}) collective-permute-start(bf16[4,128,256]{2,1,0:T(8,128)(2,1)S(1)} %get-tuple-element.28), channel_id=1, source_target_pairs={{0,1},{1,0},{2,3},{3,2},{4,5},{5,4},{6,7},{7,6},{8,9},{9,8},{10,11... | collective-permute-start | bytes 786440 | tf_op jit(solution)/shard_map/ppermute | solution.py:23
  30.4 10.5 %collective-permute-start.1 = (bf16[4,128,256]{2,1,0:T(8,128)(2,1)S(1)}, bf16[4,128,256]{2,1,0:T(8,128)(2,1)S(1)}, u32[]{:S(2)}, u32[]{:S(2)}) collective-permute-start(bf16[4,128,256]{2,1,0:T(8,128)(2,1)S(1)} %get-tuple-element.29), channel_id=1, source_target_pairs={{0,7},{1,2},{2,1},{3,4},{4,3},{5,6},{6,5},{7,0},{8,15},{9,10},{10,... | collective-permute-start | bytes 786440 | tf_op jit(solution)/shard_map/ppermute | solution.py:23
  42.0 36.8 %all-to-all-start = ((bf16[8,128,256]{2,1,0:T(8,128)(2,1)}), bf16[8,128,256]{2,1,0:T(8,128)(2,1)S(1)}, u32[]{:S(2)}, u32[]{:S(2)}) async-start(bf16[8,128,256]{2,1,0:T(8,128)(2,1)} %fusion.19), calls=%async_computation | async-start | bytes 1048576 | tf_op jit(solution)/shard_map/all_to_all | solution.py:68
  49.1 16.9 %collective-permute-start.2 = (bf16[2,16,256]{2,1,0:T(8,128)(2,1)S(1)}, bf16[2,16,256]{2,1,0:T(8,128)(2,1)S(1)}, u32[]{:S(2)}, u32[]{:S(2)}) collective-permute-start(bf16[2,16,256]{2,1,0:T(8,128)(2,1)S(1)} %bitcast_reduce_fusion.1), channel_id=1, source_target_pairs={{0,1008},{16,0},{32,16},{48,32},{64,48},{80,64},{96,80},{112,96},{... | collective-permute-start | bytes 49160 | tf_op jit(solution)/shard_map/ppermute | solution.py:18
  60.4 5.6 %collective-permute-start.3 = (bf16[2,16,256]{2,1,0:T(8,128)(2,1)S(1)}, bf16[2,16,256]{2,1,0:T(8,128)(2,1)S(1)}, u32[]{:S(2)}, u32[]{:S(2)}) collective-permute-start(bf16[2,16,256]{2,1,0:T(8,128)(2,1)S(1)} %bitcast_reduce_fusion.1), channel_id=1, source_target_pairs={{0,992},{16,1008},{32,0},{48,16},{64,32},{80,48},{96,64},{112,80},... | collective-permute-start | bytes 49160 | tf_op jit(solution)/shard_map/ppermute | solution.py:18
  62.6 6.3 %collective-permute-start.4 = (bf16[2,16,256]{2,1,0:T(8,128)(2,1)S(1)}, bf16[2,16,256]{2,1,0:T(8,128)(2,1)S(1)}, u32[]{:S(2)}, u32[]{:S(2)}) collective-permute-start(bf16[2,16,256]{2,1,0:T(8,128)(2,1)S(1)} %bitcast_reduce_fusion.1), channel_id=1, source_target_pairs={{0,976},{16,992},{32,1008},{48,0},{64,16},{80,32},{96,48},{112,64}... | collective-permute-start | bytes 49160 | tf_op jit(solution)/shard_map/ppermute | solution.py:18
  68.9 9.2 %collective-permute-start.5 = (bf16[8,16,256]{2,1,0:T(8,128)(2,1)S(1)}, bf16[8,16,256]{2,1,0:T(8,128)(2,1)S(1)}, u32[]{:S(2)}, u32[]{:S(2)}) collective-permute-start(bf16[8,16,256]{2,1,0:T(8,128)(2,1)S(1)} %pad_maximum_fusion.1), channel_id=1, source_target_pairs={{0,960},{16,976},{32,992},{48,1008},{64,0},{80,16},{96,32},{112,48... | collective-permute-start | bytes 196616 | tf_op jit(solution)/shard_map/ppermute | solution.py:18
  80.1 19.5 %all-to-all-start.2 = ((f32[16,24,128]{2,1,0:T(8,128)}), f32[16,24,128]{2,1,0:T(8,128)S(1)}, u32[]{:S(2)}, u32[]{:S(2)}) async-start(f32[16,24,128]{2,1,0:T(8,128)} %maximum_maximum_fusion), calls=%async_computation.2 | async-start | bytes 393216 | tf_op jit(solution)/shard_map/all_to_all | solution.py:83
  113.8 36.0 %all-to-all-start.4 = ((bf16[8,128,256]{2,1,0:T(8,128)(2,1)}), bf16[8,128,256]{2,1,0:T(8,128)(2,1)S(1)}, u32[]{:S(2)}, u32[]{:S(2)}) async-start(bf16[8,128,256]{2,1,0:T(8,128)(2,1)} %bitcast.25), calls=%async_computation.4 | async-start | bytes 1048576 | tf_op jit(solution)/shard_map/all_to_all | solution.py:131
  118.7 11.6 %collective-permute-start.7 = (bf16[8,16,256]{2,0,1:T(8,128)(2,1)S(1)}, bf16[8,16,256]{2,0,1:T(8,128)(2,1)S(1)}, u32[]{:S(2)}, u32[]{:S(2)}) collective-permute-start(bf16[8,16,256]{2,0,1:T(8,128)(2,1)S(1)} %slice.190), channel_id=1, source_target_pairs={{0,64},{16,80},{32,96},{48,112},{64,128},{80,144},{96,160},{112,17... | collective-permute-start | bytes 196616 | tf_op jit(solution)/shard_map/ppermute | solution.py:18
  130.4 12.9 %collective-permute-start.10 = (bf16[2,16,256]{2,0,1:T(2,128)(2,1)S(1)}, bf16[2,16,256]{2,0,1:T(2,128)(2,1)S(1)}, u32[]{:S(2)}, u32[]{:S(2)}) collective-permute-start(bf16[2,16,256]{2,0,1:T(2,128)(2,1)S(1)} %get-tuple-element.31), channel_id=1, source_target_pairs={{0,48},{16,64},{32,80},{48,96},{64,112},{80,128},{96,144},{112,160... | collective-permute-start | bytes 49160 | tf_op jit(solution)/shard_map/ppermute | solution.py:18
  139.2 7.8 %collective-permute-start.8 = (bf16[2,16,256]{2,0,1:T(2,128)(2,1)S(1)}, bf16[2,16,256]{2,0,1:T(2,128)(2,1)S(1)}, u32[]{:S(2)}, u32[]{:S(2)}) collective-permute-start(bf16[2,16,256]{2,0,1:T(2,128)(2,1)S(1)} %get-tuple-element.30), channel_id=1, source_target_pairs={{0,16},{16,32},{32,48},{48,64},{64,80},{80,96},{96,112},{112,128},... | collective-permute-start | bytes 49160 | tf_op jit(solution)/shard_map/ppermute | solution.py:18
  141.1 8.7 %collective-permute-start.9 = (bf16[2,16,256]{2,0,1:T(2,128)(2,1)S(1)}, bf16[2,16,256]{2,0,1:T(2,128)(2,1)S(1)}, u32[]{:S(2)}, u32[]{:S(2)}) collective-permute-start(bf16[2,16,256]{2,0,1:T(2,128)(2,1)S(1)} %get-tuple-element.32), channel_id=1, source_target_pairs={{0,32},{16,48},{32,64},{48,80},{64,96},{80,112},{96,128},{112,144}... | collective-permute-start | bytes 49160 | tf_op jit(solution)/shard_map/ppermute | solution.py:18
  150.5 17.3 %all-to-all-start.5 = ((bf16[16,16,256]{2,1,0:T(8,128)(2,1)}), bf16[16,16,256]{2,1,0:T(8,128)(2,1)S(1)}, u32[]{:S(2)}, u32[]{:S(2)}) async-start(bf16[16,16,256]{2,1,0:T(8,128)(2,1)} %bitcast.36), calls=%async_computation.5 | async-start | bytes 262144 | tf_op jit(solution)/shard_map/all_to_all | solution.py:134
  160.2 11.8 %collective-permute-start.11 = (bf16[4,128,256]{2,1,0:T(8,128)(2,1)S(1)}, bf16[4,128,256]{2,1,0:T(8,128)(2,1)S(1)}, u32[]{:S(2)}, u32[]{:S(2)}) collective-permute-start(bf16[4,128,256]{2,1,0:T(8,128)(2,1)S(1)} %get-tuple-element.26), channel_id=1, source_target_pairs={{0,1},{1,0},{2,3},{3,2},{4,5},{5,4},{6,7},{7,6},{8,9},{9,8},{10,11... | collective-permute-start | bytes 786440 | tf_op jit(solution)/shard_map/ppermute | solution.py:23
  163.5 10.3 %collective-permute-start.12 = (bf16[4,128,256]{2,1,0:T(8,128)(2,1)S(1)}, bf16[4,128,256]{2,1,0:T(8,128)(2,1)S(1)}, u32[]{:S(2)}, u32[]{:S(2)}) collective-permute-start(bf16[4,128,256]{2,1,0:T(8,128)(2,1)S(1)} %get-tuple-element.27), channel_id=1, source_target_pairs={{0,7},{1,2},{2,1},{3,4},{4,3},{5,6},{6,5},{7,0},{8,15},{9,10},{10,... | collective-permute-start | bytes 786440 | tf_op jit(solution)/shard_map/ppermute | solution.py:23
  167.8 6.2 %copy-start.1 = (bf16[512,4096]{1,0:T(8,128)(2,1)S(1)}, bf16[512,4096]{1,0:T(8,128)(2,1)}, u32[]{:S(2)}) copy-start(bf16[512,4096]{1,0:T(8,128)(2,1)} %param.7) | copy-start | bytes 12582916

commit v4 on v2

v4 whole, which is shorter than its diff:
```python
import jax
import jax.numpy as jnp
from jax import lax
from jax.experimental import pallas as pl
from jax.experimental.pallas import tpu as pltpu
from jax.sharding import Mesh
from jax.sharding import PartitionSpec as P

SCALE = 50.0
EPS = 1e-06
WINDOW = 8
CORES = 2
MEMBERS = ("core", "tensor")
STEPS = 4
NT = (((1,), (1,)), ((), ()))


def shift_chips(value, by):
    chips = lax.axis_size("chip")
    return lax.ppermute(value, "chip", [(i, (i + by) % chips) for i in range(chips)])


def halves(value, parts):
    out = []
    for _ in range(parts):
        top = lax.reduce_precision(value, 8, 7)
        out.append(top.astype(jnp.bfloat16))
        value = value - top
    return out


def project_kernel(x_ref, w_ref, _, out_ref):
    per, _, feats = out_ref.shape
    for j in range(per):
        part = jnp.dot(x_ref[...], w_ref[:, j * feats : (j + 1) * feats], preferred_element_type=jnp.float32)
        out_ref[j] = part.astype(out_ref.dtype)


def project(rows, weight, members, wanted):
    (count, depth), width = rows.shape, weight.shape[1]
    per, feats = members // STEPS, width // members
    return pl.pallas_call(
        project_kernel,
        grid=(STEPS,),
        in_specs=[
            pl.BlockSpec((count, depth), lambda g: (0, 0)),
            pl.BlockSpec((depth, width // STEPS), lambda g: (0, g)),
            pl.BlockSpec(memory_space=pl.ANY),
        ],
        out_specs=pl.BlockSpec((per, count, feats), lambda g: (g, 0, 0)),
        out_shape=jax.ShapeDtypeStruct((members, count, feats), jnp.bfloat16),
        cost_estimate=pl.CostEstimate(
            flops=2 * count * depth * width, bytes_accessed=2 * depth * width, transcendentals=0
        ),
    )(rows, weight, wanted)


def unproject_kernel(x_ref, w_ref, out_ref, sum_ref):
    step = pl.program_id(0)
    per, feats = x_ref.shape[0] // STEPS, x_ref.shape[2]

    @pl.when(step == 0)
    def _():
        sum_ref[...] = jnp.zeros_like(sum_ref)

    total = sum_ref[...]
    for j in range(per):
        total += lax.dot_general(
            x_ref[step * per + j], w_ref[:, j * feats : (j + 1) * feats], NT, preferred_element_type=jnp.float32
        )
    sum_ref[...] = total

    @pl.when(step == STEPS - 1)
    def _():
        out_ref[...] = total.astype(out_ref.dtype)


def unproject(part, weight):
    _, rows, _ = part.shape
    depth, width = weight.shape
    return pl.pallas_call(
        unproject_kernel,
        grid=(STEPS,),
        in_specs=[
            pl.BlockSpec(memory_space=pltpu.VMEM),
            pl.BlockSpec((depth, width // STEPS), lambda g: (0, g)),
        ],
        out_specs=pl.BlockSpec((rows, depth), lambda g: (0, 0)),
        out_shape=jax.ShapeDtypeStruct((rows, depth), jnp.bfloat16),
        scratch_shapes=[pltpu.VMEM((rows, depth), jnp.float32)],
        cost_estimate=pl.CostEstimate(
            flops=2 * rows * depth * width, bytes_accessed=2 * depth * width, transcendentals=0
        ),
    )(part, weight)


def on_device(q_ctx, p_ctx, out_weight, neighbours, positive):
    f32, bf16 = jnp.float32, jnp.bfloat16
    q_rows, p_rows = q_ctx.shape[0], p_ctx.shape[0]
    listed = neighbours.shape[1]
    slots = listed * p_rows
    tensors = lax.axis_size("tensor")
    members = CORES * tensors
    feats = out_weight.shape[1] // members
    q_share = q_rows // tensors
    core, chip = lax.axis_index("core"), lax.axis_index("chip")

    other = lax.ppermute(neighbours, "core", [(0, 1), (1, 0)])
    lists = jnp.concatenate([neighbours, other], axis=0)
    lists = jnp.where(core == 0, lists, lists[::-1])

    def reduce_over_tensor(part):
        got = lax.all_to_all(part, MEMBERS, 0, 0)
        got = got.reshape(CORES, tensors, part.shape[1], feats).astype(f32)
        return jnp.sum(got, axis=1).astype(bf16)

    window = reduce_over_tensor(project(p_ctx, out_weight, members, neighbours))
    q_pre = reduce_over_tensor(project(q_ctx, out_weight, members, other))

    reach = WINDOW // 2
    while reach:
        window = jnp.concatenate([window, shift_chips(window, -reach)], axis=0)
        reach //= 2
    ahead = (lists - CORES * chip) % (CORES * lax.axis_size("chip"))
    places = jnp.array([0, 4, 2, 6, 1, 5, 3, 7], jnp.int32)
    spots = jnp.sum(jnp.where(ahead[..., None] // CORES == places, jnp.arange(WINDOW, dtype=jnp.int32), 0), axis=-1)
    spots = spots * CORES + ahead % CORES
    cand = window[spots].reshape(CORES, slots, feats)

    raw = jnp.einsum("kqf,kcf->kqc", q_pre, cand, preferred_element_type=f32)
    q_sq = jnp.sum(jnp.square(q_pre.astype(f32)), axis=-1)
    c_sq = jnp.sum(jnp.square(cand.astype(f32)), axis=-1)
    q_sq = jnp.pad(q_sq.reshape(CORES, tensors, 1, q_share), ((0, 0), (0, 0), (0, 0), (0, slots - q_share)))
    c_sq = jnp.broadcast_to(c_sq[:, None, None, :], (CORES, tensors, 1, slots))
    extra = jnp.zeros((CORES, tensors, 6, slots), f32)
    sums = jnp.concatenate([raw.reshape(CORES, tensors, q_share, slots), q_sq, c_sq, extra], axis=2)
    sums = lax.all_to_all(sums.reshape(members, q_share + 8, slots), MEMBERS, 0, 0)
    sums = jnp.sum(sums, axis=0)
    raw = sums[:q_share]
    inv_q = lax.rsqrt(sums[q_share, :q_share] + EPS)
    inv_c = lax.rsqrt(sums[q_share + 1] + EPS)

    scores = raw * (SCALE * inv_q)[:, None] * inv_c[None, :]
    lse = jnp.log(jnp.sum(jnp.exp(scores), axis=-1))
    pos = lax.dynamic_slice_in_dim(positive, lax.axis_index("tensor") * q_share, q_share)
    onehot = (jnp.arange(slots, dtype=jnp.int32)[None, :] == pos[:, None]).astype(f32)
    loss = lse - jnp.sum(scores * onehot, axis=-1)
    dscore = jnp.exp(scores - lse[:, None]) - onehot
    coef = lax.reduce_precision(dscore * (SCALE * inv_q)[:, None] * inv_c[None, :], 8, 7)
    weighted = coef * raw
    q_inner = jnp.square(inv_q) * jnp.sum(weighted, axis=-1)
    c_inner = jnp.square(inv_c) * jnp.sum(weighted, axis=0)

    row = jnp.concatenate(halves(q_inner, 2) + halves(loss, 3))
    row = jnp.pad(row, (0, slots - row.shape[0]))
    c_rows = jnp.stack([row] + halves(c_inner, 2) + [jnp.zeros((slots,), bf16)] * 5)
    told = jnp.concatenate([coef.astype(bf16), c_rows], axis=0)
    told = lax.all_to_all(jnp.broadcast_to(told[None], (members,) + told.shape), MEMBERS, 0, 0)
    told = told.reshape(CORES, tensors, q_share + 8, slots)
    coef = told[:, :, :q_share].reshape(CORES, q_rows, slots)
    row = told[:, :, q_share].astype(f32)
    q_inner = (row[..., :q_share] + row[..., q_share : 2 * q_share]).reshape(CORES, q_rows, 1)
    loss = row[..., 2 * q_share : 3 * q_share] + row[..., 3 * q_share : 4 * q_share] + row[..., 4 * q_share : 5 * q_share]
    losses = jnp.where(core == 0, loss[0], loss[1]).reshape(q_rows)
    c_inner = jnp.sum(told[:, :, q_share + 1 : q_share + 3].astype(f32), axis=(1, 2))[..., None]

    dq = jnp.einsum("kqc,kcf->kqf", coef, cand, preferred_element_type=f32)
    dq = (dq - q_inner * q_pre.astype(f32)).astype(bf16)
    dc = jnp.einsum("kqc,kqf->kcf", coef, q_pre, preferred_element_type=f32)
    dc = (dc - c_inner * cand.astype(f32)).astype(bf16)
    match = (jnp.arange(WINDOW * CORES, dtype=jnp.int32)[:, None, None] == spots[None]).astype(bf16)
    dwin = jnp.einsum("wks,kspf->wpf", match, dc.reshape(CORES, listed, p_rows, feats), preferred_element_type=f32)

    def gather_features(part):
        part = jnp.broadcast_to(part[:, None], (CORES, tensors) + part.shape[1:])
        return lax.all_to_all(part.reshape((members,) + part.shape[2:]), MEMBERS, 0, 0)

    dq = gather_features(dq)
    reach = 1
    while reach < WINDOW:
        half = dwin.shape[0] // 2
        dwin = dwin[:half] + shift_chips(dwin[half:].astype(bf16), reach).astype(f32)
        reach *= 2
    dp, dq = lax.optimization_barrier((dwin.astype(bf16), dq))

    return unproject(dq, out_weight), unproject(gather_features(dp), out_weight), losses


def solution(mesh):
    dp, tensors = mesh.shape["dp"], mesh.shape["tensor"]
    fine = Mesh(mesh.devices.reshape(dp // CORES, CORES, tensors), ("chip",) + MEMBERS)
    rows = ("chip", "core")
    placed = (P(rows, "tensor"), P(rows, "tensor"), P("tensor", None), P(rows, None), P(rows))
    return jax.shard_map(
        on_device,
        mesh=fine,
        in_specs=placed,
        out_specs=(P(rows, "tensor"), P(rows, "tensor"), P(rows)),
        check_vma=False,
    )
```

time: 156 us -> 164 us (1.051)
  Pallas kernels: 0 us -> 18.1 us
  matrix products: 15 us -> 0.88 us
  starting transfers between devices: 79.9 us -> 86.2 us
  waiting for transfers between devices: 39.7 us -> 36.9 us
    pallas_call x0 -> x4, Pallas kernels: none -> 18.1 us  [the longest x2 9.3 us: unproject(): pl.pallas_call(unproject_kernel, grid=(STEPS,), in_specs=[pl.BlockSpec(me...]
    dot_general x4 -> x0, matrix products: 14.2 us -> none  [the longest x2 8.36 us: unproject(): jnp.einsum('mrf,hmf->rh', part, weight, preferred_element_type=f32)]
    all_to_all x2, waiting for transfers between devices: 3.32 us -> 0.01 us  [reduce_over_tensor(): got = lax.all_to_all(part, MEMBERS, 0, 0)]
    ppermute x6, starting transfers between devices: 31.4 us -> 34.6 us  [shift_chips(): lax.ppermute(value, 'chip', [(i, (i + by) % chips) for i in range(chips)])]
    all_to_all x2, starting transfers between devices: 22.2 us -> 24.8 us  [reduce_over_tensor(): got = lax.all_to_all(part, MEMBERS, 0, 0)]
    reshape x3 -> x1, local copies, waits for them, and re-layouts: 1.85 us -> 0.08 us  [on_device(): q_sq.reshape(CORES, tensors, 1, q_share)]
  transfers between devices with their start and end apart: 12 -> 12, of which waited for: 9 -> 9; matrix products, arithmetic and copies ran while one was open for 7% -> 2% of each run, Pallas kernels for 0% -> 6%
where the time goes in v4:
time: 164 us; the launch traced here: 163 us
  starting transfers between devices  86.2 us (53%)
  waiting for transfers between devices  36.9 us (22%)
  Pallas kernels  18.1 us (11%)
  blocking collectives  12.1 us (7%)
  local copies, waits for them, and re-layouts  4.86 us (3%)
  other arithmetic  3.35 us (2%)
    ppermute x6, starting transfers between devices, shift_chips(): lax.ppermute(value, 'chip', [(i, (i + by) % chips) for i in range(chips)])  34.6 us
    ppermute x6, waiting for transfers between devices, shift_chips(): lax.ppermute(value, 'chip', [(i, (i + by) % chips) for i in range(chips)])  26.1 us
    all_to_all x2, starting transfers between devices, reduce_over_tensor(): got = lax.all_to_all(part, MEMBERS, 0, 0)  24.8 us
    all_to_all x2, starting transfers between devices, gather_features(): lax.all_to_all(part.reshape((members,) + part.shape[2:]), MEMBERS, 0, 0)  14.4 us
    all_to_all x1, blocking collectives, on_device(): lax.all_to_all(jnp.broadcast_to(told[None], (members,) + told.shape), MEM...  12.1 us
    all_to_all x1, starting transfers between devices, on_device(): lax.all_to_all(sums.reshape(members, q_share + 8, slots), MEMBERS, 0, 0)  10.3 us
    pallas_call x2, Pallas kernels, unproject(): pl.pallas_call(unproject_kernel, grid=(STEPS,), in_specs=[pl.BlockSpec(me...  9.3 us
    pallas_call x2, Pallas kernels, project(): pl.pallas_call(project_kernel, grid=(STEPS,), in_specs=[pl.BlockSpec((cou...  8.83 us
  transfers between devices with their start and end apart: 12, of which 9 were waited for; matrix products, arithmetic and copies ran while one was open for 2% of the time, Pallas kernels for 6%

profile of v4, /device:TPU:1, one launch (start us, length us, event | category | flops | bytes accessed | tf_op | source)
XLA Modules:
  0.0 163.5 jit_solution(6626020227687491163)
XLA Ops:
  0.6 4.3 %shard_map.86 = bf16[16,16,256]{2,1,0:T(8,128)(2,1)} custom-call(bf16[16,512]{1,0:T(8,128)(2,1)} %x_ref.3, bf16[512,4096]{1,0:T(8,128)(2,1)} %w_ref.7, s32[1,8]{1,0:T(1,128)} %_.1), custom_call_target="tpu_custom_call" | custom-call | flops 67108864 | bytes 4194304 | tf_op jit(solution)/shard_map/pallas_call | solution.py:42
  4.9 17.6 %all-to-all-start.1 = ((bf16[16,16,256]{2,1,0:T(8,128)(2,1)}), bf16[16,16,256]{2,1,0:T(8,128)(2,1)S(1)}, u32[]{:S(2)}, u32[]{:S(2)}) async-start(bf16[16,16,256]{2,1,0:T(8,128)(2,1)} %shard_map.86), calls=%async_computation.1 | async-start | bytes 262144 | tf_op jit(solution)/shard_map/all_to_all | solution.py:113
  22.6 2.1 %collective-permute-start = (s32[1,8]{1,0:T(1,128)S(1)}, s32[1,8]{1,0:T(1,128)S(1)}, u32[]{:S(2)}, u32[]{:S(2)}) collective-permute-start(s32[1,8]{1,0:T(1,128)S(1)} %copy-done.2), channel_id=1, source_target_pairs={{0,8},{8,0},{1,9},{9,1},{2,10},{10,2},{3,11},{11,3},{4,12},{12,4},... | collective-permute-start | bytes 104 | tf_op jit(solution)/shard_map/ppermute | solution.py:108
  24.7 0.9 collective-permute-done._
  25.6 0.5 copy-done.3
  26.1 4.6 %shard_map.85 = bf16[16,128,256]{2,1,0:T(8,128)(2,1)} custom-call(bf16[128,512]{1,0:T(8,128)(2,1)} %x_ref.2, bf16[512,4096]{1,0:T(8,128)(2,1)} %w_ref.7, s32[1,8]{1,0:T(1,128)} %copy-done.3), custom_call_target="tpu_custom_call" | custom-call | flops 536870912 | bytes 4194304 | tf_op jit(solution)/shard_map/pallas_call | solution.py:42
  30.7 7.2 %all-to-all-start = ((bf16[16,128,256]{2,1,0:T(8,128)(2,1)}), bf16[16,128,256]{2,1,0:T(8,128)(2,1)S(1)}, u32[]{:S(2)}, u32[]{:S(2)}) async-start(bf16[16,128,256]{2,1,0:T(8,128)(2,1)} %shard_map.85), calls=%async_computation | async-start | bytes 2097152 | tf_op jit(solution)/shard_map/all_to_all | solution.py:113
  37.9 0.7 pad_add_fusion
  38.6 0.7 and_select_fusion.1
  39.3 11.3 %collective-permute-start.1 = (bf16[2,16,256]{2,1,0:T(8,128)(2,1)S(1)}, bf16[2,16,256]{2,1,0:T(8,128)(2,1)S(1)}, u32[]{:S(2)}, u32[]{:S(2)}) collective-permute-start(bf16[2,16,256]{2,1,0:T(8,128)(2,1)S(1)} %bitcast_reduce_fusion.1), channel_id=1, source_target_pairs={{0,960},{16,976},{32,992},{48,1008},{64,0},{80,16},{96,32},{112,48... | collective-permute-start | bytes 49160 | tf_op jit(solution)/shard_map/ppermute | solution.py:20
  50.6 0.2 select_reduce_fusion.1
  50.8 0.6 collective-permute-done.1
  51.5 9.7 %collective-permute-start.2 = (bf16[4,16,256]{2,1,0:T(8,128)(2,1)S(1)}, bf16[4,16,256]{2,1,0:T(8,128)(2,1)S(1)}, u32[]{:S(2)}, u32[]{:S(2)}) collective-permute-start(bf16[4,16,256]{2,1,0:T(8,128)(2,1)S(1)} %pad_maximum_fusion.2), channel_id=1, source_target_pairs={{0,992},{16,1008},{32,0},{48,16},{64,32},{80,48},{96,64},{112,80},... | collective-permute-start | bytes 98312 | tf_op jit(solution)/shard_map/ppermute | solution.py:20
  61.2 0.1 reshape.113
  61.2 0.9 collective-permute-done.2
  62.2 7.9 %collective-permute-start.3 = (bf16[8,16,256]{2,1,0:T(8,128)(2,1)S(1)}, bf16[8,16,256]{2,1,0:T(8,128)(2,1)S(1)}, u32[]{:S(2)}, u32[]{:S(2)}) collective-permute-start(bf16[8,16,256]{2,1,0:T(8,128)(2,1)S(1)} %pad_maximum_fusion.1), channel_id=1, source_target_pairs={{0,1008},{16,0},{32,16},{48,32},{64,48},{80,64},{96,80},{112,96},{... | collective-permute-start | bytes 196616 | tf_op jit(solution)/shard_map/ppermute | solution.py:20
  70.1 1.3 collective-permute-done.3
  71.4 0.6 gather_fusion
  71.9 0.1 multiply_reduce_fusion
  72.1 0.1 bitcast_reduce_fusion
  72.3 0.1 fusion.2
  72.5 0.2 fusion.22
  72.7 0.8 maximum_maximum_fusion
  73.4 10.3 %all-to-all-start.2 = ((f32[16,24,128]{2,1,0:T(8,128)}), f32[16,24,128]{2,1,0:T(8,128)S(1)}, u32[]{:S(2)}, u32[]{:S(2)}) async-start(f32[16,24,128]{2,1,0:T(8,128)} %maximum_maximum_fusion), calls=%async_computation.2 | async-start | bytes 393216 | tf_op jit(solution)/shard_map/all_to_all | solution.py:137
  83.9 8.2 %all-to-all-done.2 = f32[16,24,128]{2,1,0:T(8,128)S(1)} async-done(((f32[16,24,128]{2,1,0:T(8,128)}), f32[16,24,128]{2,1,0:T(8,128)S(1)}, u32[]{:S(2)}, u32[]{:S(2)}) %all-to-all-start.2) | async-done | bytes 196640 | tf_op jit(solution)/shard_map/all_to_all | solution.py:137
  92.1 0.2 select_reduce_fusion
  92.3 0.2 fusion.8
  92.6 0.1 concatenate.38
  92.8 12.1 %all_to_all.30 = bf16[16,24,128]{2,1,0:T(8,128)(2,1)S(1)} all-to-all(bf16[16,24,128]{2,1,0:T(8,128)(2,1)S(1)} %broadcast_in_dim.31), channel_id=1, replica_groups=mesh['chip'=64,'core'=2,'tensor'=8] {'core','tensor'}, dimensions={0} | all-to-all | bytes 196608 | tf_op jit(solution)/shard_map/all_to_all | solution.py:158
  104.9 0.1 mul.100
  105.0 0.2 fusion.1
  105.2 1.1 broadcast_in_dim.32
  106.3 4.6 %all-to-all-start.4 = ((bf16[16,128,256]{2,1,0:T(8,128)(2,1)}), bf16[16,128,256]{2,1,0:T(8,128)(2,1)S(1)}, u32[]{:S(2)}, u32[]{:S(2)}) async-start(bf16[16,128,256]{2,1,0:T(8,128)(2,1)} %bitcast.18), calls=%async_computation.4 | async-start | bytes 2097152 | tf_op jit(solution)/shard_map/all_to_all | solution.py:176
  110.9 0.2 fusion
  111.1 0.3 convolution_bitcast_fusion
  111.5 1.9 %collective-permute-start.4 = (bf16[8,16,256]{2,0,1:T(8,128)(2,1)S(1)}, bf16[8,16,256]{2,0,1:T(8,128)(2,1)S(1)}, u32[]{:S(2)}, u32[]{:S(2)}) collective-permute-start(bf16[8,16,256]{2,0,1:T(8,128)(2,1)S(1)} %slice.145), channel_id=1, source_target_pairs={{0,16},{16,32},{32,48},{48,64},{64,80},{80,96},{96,112},{112,128},... | collective-permute-start | bytes 196616 | tf_op jit(solution)/shard_map/ppermute | solution.py:20
  113.4 7.8 %collective-permute-done.4 = bf16[8,16,256]{2,0,1:T(8,128)(2,1)S(1)} collective-permute-done((bf16[8,16,256]{2,0,1:T(8,128)(2,1)S(1)}, bf16[8,16,256]{2,0,1:T(8,128)(2,1)S(1)}, u32[]{:S(2)}, u32[]{:S(2)}) %collective-permute-start.4) | collective-permute-done | bytes 65568 | tf_op jit(solution)/shard_map/ppermute | solution.py:20
  121.2 1.9 %collective-permute-start.5 = (bf16[4,16,256]{2,0,1:T(4,128)(2,1)S(1)}, bf16[4,16,256]{2,0,1:T(4,128)(2,1)S(1)}, u32[]{:S(2)}, u32[]{:S(2)}) collective-permute-start(bf16[4,16,256]{2,0,1:T(4,128)(2,1)S(1)} %slice.146), channel_id=1, source_target_pairs={{0,32},{16,48},{32,64},{48,80},{64,96},{80,112},{96,128},{112,144}... | collective-permute-start | bytes 98312 | tf_op jit(solution)/shard_map/ppermute | solution.py:20
  123.1 6.9 %collective-permute-done.5 = bf16[4,16,256]{2,0,1:T(4,128)(2,1)S(1)} collective-permute-done((bf16[4,16,256]{2,0,1:T(4,128)(2,1)S(1)}, bf16[4,16,256]{2,0,1:T(4,128)(2,1)S(1)}, u32[]{:S(2)}, u32[]{:S(2)}) %collective-permute-start.5) | collective-permute-done | bytes 32800 | tf_op jit(solution)/shard_map/ppermute | solution.py:20
  130.1 1.9 %collective-permute-start.6 = (bf16[2,16,256]{2,0,1:T(2,128)(2,1)S(1)}, bf16[2,16,256]{2,0,1:T(2,128)(2,1)S(1)}, u32[]{:S(2)}, u32[]{:S(2)}) collective-permute-start(bf16[2,16,256]{2,0,1:T(2,128)(2,1)S(1)} %slice.147), channel_id=1, source_target_pairs={{0,64},{16,80},{32,96},{48,112},{64,128},{80,144},{96,160},{112,17... | collective-permute-start | bytes 49160 | tf_op jit(solution)/shard_map/ppermute | solution.py:20
  132.0 8.6 %collective-permute-done.6 = bf16[2,16,256]{2,0,1:T(2,128)(2,1)S(1)} collective-permute-done((bf16[2,16,256]{2,0,1:T(2,128)(2,1)S(1)}, bf16[2,16,256]{2,0,1:T(2,128)(2,1)S(1)}, u32[]{:S(2)}, u32[]{:S(2)}) %collective-permute-start.6) | collective-permute-done | bytes 16416 | tf_op jit(solution)/shard_map/ppermute | solution.py:20
  140.7 0.7 broadcast_in_dim.33
  141.4 9.8 %all-to-all-start.5 = ((bf16[16,16,256]{2,1,0:T(8,128)(2,1)}), bf16[16,16,256]{2,1,0:T(8,128)(2,1)S(1)}, u32[]{:S(2)}, u32[]{:S(2)}) async-start(bf16[16,16,256]{2,1,0:T(8,128)(2,1)} %bitcast.19), calls=%async_computation.5 | async-start | bytes 262144 | tf_op jit(solution)/shard_map/all_to_all | solution.py:176
  151.2 0.6 select_n.57
  151.8 5.0 %shard_map.87 = bf16[128,512]{1,0:T(8,128)(2,1)} custom-call(bf16[16,128,256]{2,1,0:T(8,128)(2,1)} %copy-done, bf16[512,4096]{1,0:T(8,128)(2,1)} %w_ref.7), custom_call_target="tpu_custom_call" | custom-call | flops 536870912 | bytes 4194304 | tf_op jit(solution)/shard_map/pallas_call | solution.py:81
  156.8 1.7 %all-to-all-done.5.x_ref = bf16[16,16,256]{2,1,0:T(8,128)(2,1)S(1)} async-done(((bf16[16,16,256]{2,1,0:T(8,128)(2,1)}), bf16[16,16,256]{2,1,0:T(8,128)(2,1)S(1)}, u32[]{:S(2)}, u32[]{:S(2)}) %all-to-all-start.5) | async-done | bytes 131104 | tf_op jit(solution)/shard_map/all_to_all | solution.py:176
  158.5 0.6 copy-done.1
  159.1 4.3 %shard_map.88 = bf16[16,512]{1,0:T(8,128)(2,1)} custom-call(bf16[16,16,256]{2,1,0:T(8,128)(2,1)} %copy-done.1, bf16[512,4096]{1,0:T(8,128)(2,1)} %w_ref.7), custom_call_target="tpu_custom_call" | custom-call | flops 67108864 | bytes 4194304 | tf_op jit(solution)/shard_map/pallas_call | solution.py:81
  (52 shorter events, 0.8 us)
Async XLA Ops:
  0.6 21.9 %copy-start.2 = (s32[1,8]{1,0:T(1,128)S(1)}, s32[1,8]{1,0:T(1,128)}, u32[]{:S(2)}) copy-start(s32[1,8]{1,0:T(1,128)} %_.1) | copy-start | bytes 100
  4.9 45.7 %copy-start.4 = (s32[8]{0:T(128)S(1)}, s32[8]{0:T(128)}, u32[]{:S(2)}) copy-start(s32[8]{0:T(128)} %constant.76.clone) | copy-start | bytes 100
  4.9 25.7 %all-to-all-start.1 = ((bf16[16,16,256]{2,1,0:T(8,128)(2,1)}), bf16[16,16,256]{2,1,0:T(8,128)(2,1)S(1)}, u32[]{:S(2)}, u32[]{:S(2)}) async-start(bf16[16,16,256]{2,1,0:T(8,128)(2,1)} %shard_map.86), calls=%async_computation.1 | async-start | bytes 262144 | tf_op jit(solution)/shard_map/all_to_all | solution.py:113
  22.6 61.2 %copy-start.5 = (s32[128]{0:T(128)S(1)}, s32[128]{0:T(128)}, u32[]{:S(2)}) copy-start(s32[128]{0:T(128)} %param.10) | copy-start | bytes 1540
  22.6 3.0 %collective-permute-start = (s32[1,8]{1,0:T(1,128)S(1)}, s32[1,8]{1,0:T(1,128)S(1)}, u32[]{:S(2)}, u32[]{:S(2)}) collective-permute-start(s32[1,8]{1,0:T(1,128)S(1)} %copy-done.2), channel_id=1, source_target_pairs={{0,8},{8,0},{1,9},{9,1},{2,10},{10,2},{3,11},{11,3},{4,12},{12,4},... | collective-permute-start | bytes 104 | tf_op jit(solution)/shard_map/ppermute | solution.py:108
  25.6 0.5 copy-start.3
  30.7 41.5 %all-to-all-start = ((bf16[16,128,256]{2,1,0:T(8,128)(2,1)}), bf16[16,128,256]{2,1,0:T(8,128)(2,1)S(1)}, u32[]{:S(2)}, u32[]{:S(2)}) async-start(bf16[16,128,256]{2,1,0:T(8,128)(2,1)} %shard_map.85), calls=%async_computation | async-start | bytes 2097152 | tf_op jit(solution)/shard_map/all_to_all | solution.py:113
  39.3 12.1 %collective-permute-start.1 = (bf16[2,16,256]{2,1,0:T(8,128)(2,1)S(1)}, bf16[2,16,256]{2,1,0:T(8,128)(2,1)S(1)}, u32[]{:S(2)}, u32[]{:S(2)}) collective-permute-start(bf16[2,16,256]{2,1,0:T(8,128)(2,1)S(1)} %bitcast_reduce_fusion.1), channel_id=1, source_target_pairs={{0,960},{16,976},{32,992},{48,1008},{64,0},{80,16},{96,32},{112,48... | collective-permute-start | bytes 49160 | tf_op jit(solution)/shard_map/ppermute | solution.py:20
  51.5 10.7 %collective-permute-start.2 = (bf16[4,16,256]{2,1,0:T(8,128)(2,1)S(1)}, bf16[4,16,256]{2,1,0:T(8,128)(2,1)S(1)}, u32[]{:S(2)}, u32[]{:S(2)}) collective-permute-start(bf16[4,16,256]{2,1,0:T(8,128)(2,1)S(1)} %pad_maximum_fusion.2), channel_id=1, source_target_pairs={{0,992},{16,1008},{32,0},{48,16},{64,32},{80,48},{96,64},{112,80},... | collective-permute-start | bytes 98312 | tf_op jit(solution)/shard_map/ppermute | solution.py:20
  62.2 9.2 %collective-permute-start.3 = (bf16[8,16,256]{2,1,0:T(8,128)(2,1)S(1)}, bf16[8,16,256]{2,1,0:T(8,128)(2,1)S(1)}, u32[]{:S(2)}, u32[]{:S(2)}) collective-permute-start(bf16[8,16,256]{2,1,0:T(8,128)(2,1)S(1)} %pad_maximum_fusion.1), channel_id=1, source_target_pairs={{0,1008},{16,0},{32,16},{48,32},{64,48},{80,64},{96,80},{112,96},{... | collective-permute-start | bytes 196616 | tf_op jit(solution)/shard_map/ppermute | solution.py:20
  73.4 18.6 %all-to-all-start.2 = ((f32[16,24,128]{2,1,0:T(8,128)}), f32[16,24,128]{2,1,0:T(8,128)S(1)}, u32[]{:S(2)}, u32[]{:S(2)}) async-start(f32[16,24,128]{2,1,0:T(8,128)} %maximum_maximum_fusion), calls=%async_computation.2 | async-start | bytes 393216 | tf_op jit(solution)/shard_map/all_to_all | solution.py:137
  106.3 34.3 %all-to-all-start.4 = ((bf16[16,128,256]{2,1,0:T(8,128)(2,1)}), bf16[16,128,256]{2,1,0:T(8,128)(2,1)S(1)}, u32[]{:S(2)}, u32[]{:S(2)}) async-start(bf16[16,128,256]{2,1,0:T(8,128)(2,1)} %bitcast.18), calls=%async_computation.4 | async-start | bytes 2097152 | tf_op jit(solution)/shard_map/all_to_all | solution.py:176
  111.5 9.7 %collective-permute-start.4 = (bf16[8,16,256]{2,0,1:T(8,128)(2,1)S(1)}, bf16[8,16,256]{2,0,1:T(8,128)(2,1)S(1)}, u32[]{:S(2)}, u32[]{:S(2)}) collective-permute-start(bf16[8,16,256]{2,0,1:T(8,128)(2,1)S(1)} %slice.145), channel_id=1, source_target_pairs={{0,16},{16,32},{32,48},{48,64},{64,80},{80,96},{96,112},{112,128},... | collective-permute-start | bytes 196616 | tf_op jit(solution)/shard_map/ppermute | solution.py:20
  121.2 8.9 %collective-permute-start.5 = (bf16[4,16,256]{2,0,1:T(4,128)(2,1)S(1)}, bf16[4,16,256]{2,0,1:T(4,128)(2,1)S(1)}, u32[]{:S(2)}, u32[]{:S(2)}) collective-permute-start(bf16[4,16,256]{2,0,1:T(4,128)(2,1)S(1)} %slice.146), channel_id=1, source_target_pairs={{0,32},{16,48},{32,64},{48,80},{64,96},{80,112},{96,128},{112,144}... | collective-permute-start | bytes 98312 | tf_op jit(solution)/shard_map/ppermute | solution.py:20
  130.1 10.5 %collective-permute-start.6 = (bf16[2,16,256]{2,0,1:T(2,128)(2,1)S(1)}, bf16[2,16,256]{2,0,1:T(2,128)(2,1)S(1)}, u32[]{:S(2)}, u32[]{:S(2)}) collective-permute-start(bf16[2,16,256]{2,0,1:T(2,128)(2,1)S(1)} %slice.147), channel_id=1, source_target_pairs={{0,64},{16,80},{32,96},{48,112},{64,128},{80,144},{96,160},{112,17... | collective-permute-start | bytes 49160 | tf_op jit(solution)/shard_map/ppermute | solution.py:20
  140.7 11.2 %copy-start = (bf16[16,128,256]{2,1,0:T(8,128)(2,1)}, bf16[16,128,256]{2,1,0:T(8,128)(2,1)S(1)}, u32[]{:S(2)}) copy-start(bf16[16,128,256]{2,1,0:T(8,128)(2,1)S(1)} %all-to-all-done.4.x_ref) | copy-start | bytes 3145732
  141.4 17.1 %all-to-all-start.5 = ((bf16[16,16,256]{2,1,0:T(8,128)(2,1)}), bf16[16,16,256]{2,1,0:T(8,128)(2,1)S(1)}, u32[]{:S(2)}, u32[]{:S(2)}) async-start(bf16[16,16,256]{2,1,0:T(8,128)(2,1)} %bitcast.19), calls=%async_computation.5 | async-start | bytes 262144 | tf_op jit(solution)/shard_map/all_to_all | solution.py:176
  158.5 0.6 copy-start.1

commit v5 on v2

v5 whole, which is shorter than its diff:
```python
import jax
import jax.numpy as jnp
from jax import lax
from jax.sharding import Mesh
from jax.sharding import PartitionSpec as P

SCALE = 50.0
EPS = 1e-06
WINDOW = 8
PLACES = (0, 4, 2, 6, 1, 5, 3, 7)
CORES = 2


def shift_chips(value, by):
    chips = lax.axis_size("chip")
    return lax.ppermute(value, "chip", [(i, (i + by) % chips) for i in range(chips)])


def swap_cores(value):
    return lax.ppermute(value, "core", [(0, 1), (1, 0)])


def halves(value, parts):
    out = []
    for _ in range(parts):
        top = lax.reduce_precision(value, 8, 7)
        out.append(top.astype(jnp.bfloat16))
        value = value - top
    return out


def on_device(q_ctx, p_ctx, out_weight, neighbours, positive):
    f32, bf16 = jnp.float32, jnp.bfloat16
    q_rows, p_rows = q_ctx.shape[0], p_ctx.shape[0]
    listed = neighbours.shape[1]
    slots = listed * p_rows
    tensors = lax.axis_size("tensor")
    feats = out_weight.shape[1] // tensors
    q_share = q_rows // tensors
    core, chip = lax.axis_index("core"), lax.axis_index("chip")

    ahead = (neighbours[0] - CORES * chip) % (CORES * lax.axis_size("chip"))
    spots = jnp.sum(
        jnp.where(ahead[:, None] // CORES == jnp.array(PLACES), jnp.arange(WINDOW, dtype=jnp.int32), 0), axis=-1
    )
    spots = spots + jnp.where(ahead % CORES == core, 0, WINDOW)

    def project(rows):
        part = jnp.dot(rows, out_weight, preferred_element_type=f32).astype(bf16)
        return part.reshape(rows.shape[0], tensors, feats).transpose(1, 0, 2)

    def exchange(part):
        return lax.all_to_all(part, "tensor", 0, 0)

    p_part = project(p_ctx)
    q_ctx, p_part = lax.optimization_barrier((q_ctx, p_part))
    window = jnp.sum(exchange(p_part).astype(f32), axis=0).astype(bf16)[None]
    q_pre = jnp.sum(exchange(project(q_ctx)).astype(f32), axis=0).astype(bf16)

    reach = WINDOW // 2
    while reach:
        window = jnp.concatenate([window, shift_chips(window, -reach)], axis=0)
        reach //= 2
    window = jnp.concatenate([window, swap_cores(window)], axis=0)
    cand = window[spots].reshape(slots, feats)

    whole = lax.all_gather(jnp.concatenate([q_pre, cand], axis=0), "tensor")
    weight = out_weight.reshape(out_weight.shape[0], tensors, feats)
    back = jnp.einsum("mrf,hmf->rh", whole, weight, preferred_element_type=f32)

    raw = jnp.dot(q_pre, cand.T, preferred_element_type=f32)
    q_sq = jnp.sum(jnp.square(q_pre.astype(f32)), axis=-1)
    c_sq = jnp.sum(jnp.square(cand.astype(f32)), axis=-1)
    q_sq = jnp.pad(q_sq.reshape(tensors, 1, q_share), ((0, 0), (0, 0), (0, slots - q_share)))
    c_sq = jnp.broadcast_to(c_sq[None, None, :], (tensors, 1, slots))
    extra = jnp.zeros((tensors, 6, slots), f32)
    sums = jnp.concatenate([raw.reshape(tensors, q_share, slots), q_sq, c_sq, extra], axis=1)
    sums = jnp.sum(exchange(sums), axis=0)
    raw = sums[:q_share]
    inv_q = lax.rsqrt(sums[q_share, :q_share] + EPS)
    inv_c = lax.rsqrt(sums[q_share + 1] + EPS)

    scores = raw * (SCALE * inv_q)[:, None] * inv_c[None, :]
    lse = jnp.log(jnp.sum(jnp.exp(scores), axis=-1))
    pos = lax.dynamic_slice_in_dim(positive, lax.axis_index("tensor") * q_share, q_share)
    onehot = (jnp.arange(slots, dtype=jnp.int32)[None, :] == pos[:, None]).astype(f32)
    loss = lse - jnp.sum(scores * onehot, axis=-1)
    dscore = jnp.exp(scores - lse[:, None]) - onehot
    coef = lax.reduce_precision(dscore * (SCALE * inv_q)[:, None] * inv_c[None, :], 8, 7)
    weighted = coef * raw
    q_inner = jnp.square(inv_q) * jnp.sum(weighted, axis=-1)
    c_inner = jnp.square(inv_c) * jnp.sum(weighted, axis=0)

    row = jnp.concatenate(halves(q_inner, 2) + halves(loss, 3))
    row = jnp.pad(row, (0, slots - row.shape[0]))
    c_rows = jnp.stack([row] + halves(c_inner, 2) + [jnp.zeros((slots,), bf16)] * 5)
    told = jnp.concatenate([coef.astype(bf16), c_rows], axis=0)
    told = exchange(jnp.broadcast_to(told[None], (tensors,) + told.shape))
    coef = told[:, :q_share].reshape(q_rows, slots)
    row = told[:, q_share].astype(f32)
    q_inner = (row[:, :q_share] + row[:, q_share : 2 * q_share]).reshape(q_rows, 1)
    losses = row[:, 2 * q_share : 3 * q_share] + row[:, 3 * q_share : 4 * q_share] + row[:, 4 * q_share : 5 * q_share]
    c_inner = jnp.sum(told[:, q_share + 1 : q_share + 3].astype(f32), axis=(0, 1))[:, None]

    dc = lax.dot_general(coef, q_pre, (((0,), (0,)), ((), ())), preferred_element_type=f32)
    dc = (dc - c_inner * cand.astype(f32)).astype(bf16).reshape(listed, p_rows * feats)
    match = (jnp.arange(CORES * WINDOW, dtype=jnp.int32)[:, None] == spots[None]).astype(bf16)
    dwin = jnp.dot(match, dc, preferred_element_type=f32).reshape(CORES * WINDOW, p_rows, feats)
    dwin = dwin[:WINDOW] + swap_cores(dwin[WINDOW:].astype(bf16)).astype(f32)
    reach = 1
    while reach < WINDOW:
        half = dwin.shape[0] // 2
        dwin = dwin[:half] + shift_chips(dwin[half:].astype(bf16), reach).astype(f32)
        reach *= 2
    dp = exchange(jnp.broadcast_to(dwin.astype(bf16), (tensors, p_rows, feats)))
    p_grad = jnp.einsum("mrf,hmf->rh", dp, weight, preferred_element_type=f32).astype(bf16)

    q_grad = jnp.dot(coef, back[q_rows:].astype(bf16), preferred_element_type=f32) - q_inner * back[:q_rows]
    return q_grad.astype(bf16), p_grad, losses.reshape(q_rows)


def solution(mesh):
    dp, tensors = mesh.shape["dp"], mesh.shape["tensor"]
    fine = Mesh(mesh.devices.reshape(dp // CORES, CORES, tensors), ("chip", "core", "tensor"))
    rows = ("chip", "core")
    placed = (P(rows, "tensor"), P(rows, "tensor"), P("tensor", None), P(rows, None), P(rows))
    return jax.shard_map(
        on_device,
        mesh=fine,
        in_specs=placed,
        out_specs=(P(rows, "tensor"), P(rows, "tensor"), P(rows)),
        check_vma=False,
    )
```

time: 156 us -> 173 us (1.11)
  between operations: 0.98 us -> 14.5 us
  waiting for transfers between devices: 39.7 us -> 52.5 us
  blocking collectives: 12.1 us -> 0 us
    all_to_all x5, starting transfers between devices: 46.4 us -> 24.9 us  [exchange(): return lax.all_to_all(part, 'tensor', 0, 0)]
    all_to_all x1 -> x0, blocking collectives: 12.1 us -> none  [on_device(): lax.all_to_all(jnp.broadcast_to(told[None], (members,) + told.shape), MEM...]
    ppermute x6, starting transfers between devices: 31.4 us -> 43.3 us  [shift_chips(): lax.ppermute(value, 'chip', [(i, (i + by) % chips) for i in range(chips)])]
    ppermute x1 -> x2, starting transfers between devices: 2.08 us -> 12.6 us  [swap_cores(): return lax.ppermute(value, 'core', [(0, 1), (1, 0)])]
    all_to_all x5, waiting for transfers between devices: 14.4 us -> 24.6 us  [exchange(): return lax.all_to_all(part, 'tensor', 0, 0)]
    ppermute x1 -> x2, waiting for transfers between devices: 0.01 us -> 1.87 us  [swap_cores(): return lax.ppermute(value, 'core', [(0, 1), (1, 0)])]
  transfers between devices with their start and end apart: 12 -> 14, of which waited for: 9 -> 12; matrix products, arithmetic and copies ran while one was open for 7% -> 8% of each run, Pallas kernels for 0% -> 0%
where the time goes in v5:
time: 173 us; the launch traced here: 171 us
  starting transfers between devices  80.8 us (47%)
  waiting for transfers between devices  52.5 us (30%)
  matrix products  15.4 us (9%)
  between operations  14.5 us (8%)
  local copies, waits for them, and re-layouts  4.99 us (3%)
  other arithmetic  2.87 us (2%)
    ppermute x6, starting transfers between devices, shift_chips(): lax.ppermute(value, 'chip', [(i, (i + by) % chips) for i in range(chips)])  43.3 us
    ppermute x6, waiting for transfers between devices, shift_chips(): lax.ppermute(value, 'chip', [(i, (i + by) % chips) for i in range(chips)])  26 us
    all_to_all x5, starting transfers between devices, exchange(): return lax.all_to_all(part, 'tensor', 0, 0)  24.9 us
    all_to_all x5, waiting for transfers between devices, exchange(): return lax.all_to_all(part, 'tensor', 0, 0)  24.6 us
    ppermute x2, starting transfers between devices, swap_cores(): return lax.ppermute(value, 'core', [(0, 1), (1, 0)])  12.6 us
    dot_general x2, matrix products, project(): part = jnp.dot(rows, out_weight, preferred_element_type=f32).astype(bf16)  5.81 us
    dot_general x1, matrix products, on_device(): back = jnp.einsum('mrf,hmf->rh', whole, weight, preferred_element_type=f32)  4.1 us
    dot_general x1, matrix products, on_device(): jnp.einsum('mrf,hmf->rh', dp, weight, preferred_element_type=f32)  3.99 us
  transfers between devices with their start and end apart: 14, of which 12 were waited for; matrix products, arithmetic and copies ran while one was open for 8% of the time, Pallas kernels for 0%

profile of v5, /device:TPU:1, one launch (start us, length us, event | category | flops | bytes accessed | tf_op | source)
XLA Modules:
  0.0 170.9 jit_solution(2523513860583918326)
XLA Ops:
  7.2 2.9 %convolution_convert_fusion.1 = bf16[16,4096]{1,0:T(8,128)(2,1)S(1)} fusion(bf16[16,512]{1,0:T(8,128)(2,1)} %param.7, bf16[512,4096]{1,0:T(8,128)(2,1)} %param.8), kind=kOutput, calls=%fused_computation.2 | convolution fusion | flops 67174400 | bytes 4341760 | tf_op jit(solution)/shard_map/dot_general | solution.py:49
  10.1 0.7 copy.52
  10.7 7.7 %all-to-all-start.1 = ((bf16[8,16,512]{2,1,0:T(8,128)(2,1)}), bf16[8,16,512]{2,1,0:T(8,128)(2,1)S(1)}, u32[]{:S(2)}, u32[]{:S(2)}) async-start(bf16[8,16,512]{2,1,0:T(8,128)(2,1)} %bitcast.90), calls=%async_computation.1 | async-start | bytes 262144 | tf_op jit(solution)/shard_map/all_to_all | solution.py:53
  18.4 2.9 %convolution_convert_fusion = bf16[128,4096]{1,0:T(8,128)(2,1)S(1)} fusion(bf16[128,512]{1,0:T(8,128)(2,1)S(1)} %copy-done, bf16[512,4096]{1,0:T(8,128)(2,1)} %param.8), kind=kOutput, calls=%fused_computation.1 | convolution fusion | flops 537395200 | bytes 5373952 | tf_op jit(solution)/shard_map/dot_general | solution.py:49
  21.4 1.1 copy.51
  22.4 3.9 %all-to-all-done.1 = bf16[8,16,512]{2,1,0:T(8,128)(2,1)S(1)} async-done(((bf16[8,16,512]{2,1,0:T(8,128)(2,1)}), bf16[8,16,512]{2,1,0:T(8,128)(2,1)S(1)}, u32[]{:S(2)}, u32[]{:S(2)}) %all-to-all-start.1) | async-done | bytes 131104 | tf_op jit(solution)/shard_map/all_to_all | solution.py:53
  26.3 3.6 %all-to-all-start = ((bf16[8,128,512]{2,1,0:T(8,128)(2,1)}), bf16[8,128,512]{2,1,0:T(8,128)(2,1)S(1)}, u32[]{:S(2)}, u32[]{:S(2)}) async-start(bf16[8,128,512]{2,1,0:T(8,128)(2,1)} %bitcast.88), calls=%async_computation | async-start | bytes 2097152 | tf_op jit(solution)/shard_map/all_to_all | solution.py:53
  29.9 0.2 select_reduce_fusion.1
  30.2 19.9 %collective-permute-start = (bf16[1,16,512]{2,1,0:T(8,128)(2,1)S(1)}, bf16[1,16,512]{2,1,0:T(8,128)(2,1)S(1)}, u32[]{:S(2)}, u32[]{:S(2)}) collective-permute-start(bf16[1,16,512]{2,1,0:T(8,128)(2,1)S(1)} %bitcast.100), channel_id=1, source_target_pairs={{0,960},{16,976},{32,992},{48,1008},{64,0},{80,16},{96,32},{112,48... | collective-permute-start | bytes 49160 | tf_op jit(solution)/shard_map/ppermute | solution.py:16
  50.2 0.7 collective-permute-done
  51.0 9.7 %collective-permute-start.1 = (bf16[2,16,512]{2,1,0:T(8,128)(2,1)S(1)}, bf16[2,16,512]{2,1,0:T(8,128)(2,1)S(1)}, u32[]{:S(2)}, u32[]{:S(2)}) collective-permute-start(bf16[2,16,512]{2,1,0:T(8,128)(2,1)S(1)} %pad_maximum_fusion.3), channel_id=1, source_target_pairs={{0,992},{16,1008},{32,0},{48,16},{64,32},{80,48},{96,64},{112,80},... | collective-permute-start | bytes 98312 | tf_op jit(solution)/shard_map/ppermute | solution.py:16
  60.7 1.0 collective-permute-done.1
  61.7 7.9 %collective-permute-start.2 = (bf16[4,16,512]{2,1,0:T(8,128)(2,1)S(1)}, bf16[4,16,512]{2,1,0:T(8,128)(2,1)S(1)}, u32[]{:S(2)}, u32[]{:S(2)}) collective-permute-start(bf16[4,16,512]{2,1,0:T(8,128)(2,1)S(1)} %pad_maximum_fusion.2), channel_id=1, source_target_pairs={{0,1008},{16,0},{32,16},{48,32},{64,48},{80,64},{96,80},{112,96},{... | collective-permute-start | bytes 196616 | tf_op jit(solution)/shard_map/ppermute | solution.py:16
  69.6 1.3 collective-permute-done.2
  70.9 7.3 %collective-permute-start.3 = (bf16[8,16,512]{2,1,0:T(8,128)(2,1)S(1)}, bf16[8,16,512]{2,1,0:T(8,128)(2,1)S(1)}, u32[]{:S(2)}, u32[]{:S(2)}) collective-permute-start(bf16[8,16,512]{2,1,0:T(8,128)(2,1)S(1)} %pad_maximum_fusion.1), channel_id=1, source_target_pairs={{0,8},{8,0},{1,9},{9,1},{2,10},{10,2},{3,11},{11,3},{4,12},{12,4},... | collective-permute-start | bytes 393224 | tf_op jit(solution)/shard_map/ppermute | solution.py:20
  78.3 0.9 collective-permute-done.3
  79.2 0.6 gather_fusion
  79.8 0.1 multiply_reduce_fusion
  80.0 0.1 reduce_sum.111
  80.1 0.1 multiply_reduce_fusion.1
  80.3 0.2 fusion.43
  80.5 0.7 fusion.17
  81.3 7.0 %all-to-all-start.2 = ((f32[8,24,128]{2,1,0:T(8,128)}), f32[8,24,128]{2,1,0:T(8,128)S(1)}, u32[]{:S(2)}, u32[]{:S(2)}) async-start(f32[8,24,128]{2,1,0:T(8,128)} %fusion.17), calls=%async_computation.2 | async-start | bytes 196608 | tf_op jit(solution)/shard_map/all_to_all | solution.py:53
  88.4 0.7 pad_maximum_fusion
  89.1 6.6 %all-to-all-done.2 = f32[8,24,128]{2,1,0:T(8,128)S(1)} async-done(((f32[8,24,128]{2,1,0:T(8,128)}), f32[8,24,128]{2,1,0:T(8,128)S(1)}, u32[]{:S(2)}, u32[]{:S(2)}) %all-to-all-start.2) | async-done | bytes 98336 | tf_op jit(solution)/shard_map/all_to_all | solution.py:53
  95.7 0.2 select_reduce_fusion
  95.9 0.2 fusion.23
  96.4 0.6 broadcast_in_dim.63
  97.0 3.3 %all-to-all-start.3 = ((bf16[8,24,128]{2,1,0:T(8,128)(2,1)}), bf16[8,24,128]{2,1,0:T(8,128)(2,1)S(1)}, u32[]{:S(2)}, u32[]{:S(2)}) async-start(bf16[8,24,128]{2,1,0:T(8,128)(2,1)} %broadcast_in_dim.63), calls=%async_computation.3 | async-start | bytes 98304 | tf_op jit(solution)/shard_map/all_to_all | solution.py:53
  100.4 6.9 %all-to-all-done.3 = bf16[8,24,128]{2,1,0:T(8,128)(2,1)S(1)} async-done(((bf16[8,24,128]{2,1,0:T(8,128)(2,1)}), bf16[8,24,128]{2,1,0:T(8,128)(2,1)S(1)}, u32[]{:S(2)}, u32[]{:S(2)}) %all-to-all-start.3) | async-done | bytes 49184 | tf_op jit(solution)/shard_map/all_to_all | solution.py:53
  107.4 0.2 subtract_convert_fusion
  107.6 0.2 fusion.21
  107.9 5.2 %collective-permute-start.4 = (bf16[8,16,512]{2,1,0:T(8,128)(2,1)S(1)}, bf16[8,16,512]{2,1,0:T(8,128)(2,1)S(1)}, u32[]{:S(2)}, u32[]{:S(2)}) collective-permute-start(bf16[8,16,512]{2,1,0:T(8,128)(2,1)S(1)} %copy.28), channel_id=1, source_target_pairs={{0,8},{8,0},{1,9},{9,1},{2,10},{10,2},{3,11},{11,3},{4,12},{12,4},... | collective-permute-start | bytes 393224 | tf_op jit(solution)/shard_map/ppermute | solution.py:20
  113.2 0.9 collective-permute-done.4
  114.1 0.2 copy_add_fusion
  114.3 1.9 %collective-permute-start.5 = (bf16[4,16,512]{2,1,0:T(8,128)(2,1)S(1)}, bf16[4,16,512]{2,1,0:T(8,128)(2,1)S(1)}, u32[]{:S(2)}, u32[]{:S(2)}) collective-permute-start(bf16[4,16,512]{2,1,0:T(8,128)(2,1)S(1)} %slice.162), channel_id=1, source_target_pairs={{0,16},{16,32},{32,48},{48,64},{64,80},{80,96},{96,112},{112,128},... | collective-permute-start | bytes 196616 | tf_op jit(solution)/shard_map/ppermute | solution.py:16
  116.2 7.5 %collective-permute-done.5 = bf16[4,16,512]{2,1,0:T(8,128)(2,1)S(1)} collective-permute-done((bf16[4,16,512]{2,1,0:T(8,128)(2,1)S(1)}, bf16[4,16,512]{2,1,0:T(8,128)(2,1)S(1)}, u32[]{:S(2)}, u32[]{:S(2)}) %collective-permute-start.5) | collective-permute-done | bytes 65568 | tf_op jit(solution)/shard_map/ppermute | solution.py:16
  123.8 1.9 %collective-permute-start.6 = (bf16[2,16,512]{2,1,0:T(8,128)(2,1)S(1)}, bf16[2,16,512]{2,1,0:T(8,128)(2,1)S(1)}, u32[]{:S(2)}, u32[]{:S(2)}) collective-permute-start(bf16[2,16,512]{2,1,0:T(8,128)(2,1)S(1)} %slice.163), channel_id=1, source_target_pairs={{0,32},{16,48},{32,64},{48,80},{64,96},{80,112},{96,128},{112,144}... | collective-permute-start | bytes 98312 | tf_op jit(solution)/shard_map/ppermute | solution.py:16
  125.7 6.9 %collective-permute-done.6 = bf16[2,16,512]{2,1,0:T(8,128)(2,1)S(1)} collective-permute-done((bf16[2,16,512]{2,1,0:T(8,128)(2,1)S(1)}, bf16[2,16,512]{2,1,0:T(8,128)(2,1)S(1)}, u32[]{:S(2)}, u32[]{:S(2)}) %collective-permute-start.6) | collective-permute-done | bytes 32800 | tf_op jit(solution)/shard_map/ppermute | solution.py:16
  132.7 1.9 %collective-permute-start.7 = (bf16[1,16,512]{2,1,0:T(8,128)(2,1)S(1)}, bf16[1,16,512]{2,1,0:T(8,128)(2,1)S(1)}, u32[]{:S(2)}, u32[]{:S(2)}) collective-permute-start(bf16[1,16,512]{2,1,0:T(8,128)(2,1)S(1)} %slice.164), channel_id=1, source_target_pairs={{0,64},{16,80},{32,96},{48,112},{64,128},{80,144},{96,160},{112,17... | collective-permute-start | bytes 49160 | tf_op jit(solution)/shard_map/ppermute | solution.py:16
  134.6 8.6 %collective-permute-done.7 = bf16[1,16,512]{2,1,0:T(8,128)(2,1)S(1)} collective-permute-done((bf16[1,16,512]{2,1,0:T(8,128)(2,1)S(1)}, bf16[1,16,512]{2,1,0:T(8,128)(2,1)S(1)}, u32[]{:S(2)}, u32[]{:S(2)}) %collective-permute-start.7) | collective-permute-done | bytes 16416 | tf_op jit(solution)/shard_map/ppermute | solution.py:16
  143.2 0.7 broadcast_in_dim.66
  143.8 3.4 %all-to-all-start.4 = ((bf16[8,16,512]{2,1,0:T(8,128)(2,1)}), bf16[8,16,512]{2,1,0:T(8,128)(2,1)S(1)}, u32[]{:S(2)}, u32[]{:S(2)}) async-start(bf16[8,16,512]{2,1,0:T(8,128)(2,1)} %broadcast_in_dim.66), calls=%async_computation.4 | async-start | bytes 262144 | tf_op jit(solution)/shard_map/all_to_all | solution.py:53
  147.4 0.6 reshape.213
  148.0 7.2 %all-to-all-done.4 = bf16[8,16,512]{2,1,0:T(8,128)(2,1)S(1)} async-done(((bf16[8,16,512]{2,1,0:T(8,128)(2,1)}), bf16[8,16,512]{2,1,0:T(8,128)(2,1)S(1)}, u32[]{:S(2)}, u32[]{:S(2)}) %all-to-all-start.4) | async-done | bytes 131104 | tf_op jit(solution)/shard_map/all_to_all | solution.py:53
  155.2 4.0 %fusion.13 = bf16[16,512]{1,0:T(8,128)(2,1)} fusion(bf16[8,16,512]{2,1,0:T(8,128)(2,1)S(1)} %all-to-all-done.4, bf16[64,8,8,512]{3,2,1,0:T(8,128)(2,1)} %bitcast.91), kind=kOutput, calls=%fused_computation.13 | convolution fusion | flops 67117056 | bytes 4341760 | tf_op jit(solution)/shard_map/mrf,hmf->rh/dot_general | solution.py:116
  159.1 4.1 %fusion.6 = f32[256,512]{1,0:T(8,128)S(1)} fusion(bf16[8,256,512]{2,1,0:T(8,128)(2,1)} %bitcast.108, bf16[64,8,8,512]{3,2,1,0:T(8,128)(2,1)} %bitcast.92), kind=kOutput, calls=%fused_computation.9 | convolution fusion | flops 1073741824 | bytes 6815744 | tf_op jit(solution)/shard_map/mrf,hmf->rh/dot_general | solution.py:69
  163.3 0.8 fusion.9
  (59 shorter events, 1.2 us)
Async XLA Ops:
  7.2 11.2 %copy-start = (bf16[128,512]{1,0:T(8,128)(2,1)S(1)}, bf16[128,512]{1,0:T(8,128)(2,1)}, u32[]{:S(2)}) copy-start(bf16[128,512]{1,0:T(8,128)(2,1)} %param.6) | copy-start | bytes 393220
  10.7 15.6 %all-to-all-start.1 = ((bf16[8,16,512]{2,1,0:T(8,128)(2,1)}), bf16[8,16,512]{2,1,0:T(8,128)(2,1)S(1)}, u32[]{:S(2)}, u32[]{:S(2)}) async-start(bf16[8,16,512]{2,1,0:T(8,128)(2,1)} %bitcast.90), calls=%async_computation.1 | async-start | bytes 262144 | tf_op jit(solution)/shard_map/all_to_all | solution.py:53
  18.4 11.5 %copy-start.1 = (s32[1,8]{1,0:T(1,128)S(1)}, s32[1,8]{1,0:T(1,128)}, u32[]{:S(2)}) copy-start(s32[1,8]{1,0:T(1,128)} %param.9) | copy-start | bytes 100
  18.4 11.5 %copy-start.3 = (s32[8]{0:T(128)S(1)}, s32[8]{0:T(128)}, u32[]{:S(2)}) copy-start(s32[8]{0:T(128)} %constant.81.clone) | copy-start | bytes 100
  21.4 66.9 %copy-start.2 = (s32[128]{0:T(128)S(1)}, s32[128]{0:T(128)}, u32[]{:S(2)}) copy-start(s32[128]{0:T(128)} %param.10) | copy-start | bytes 1540
  26.3 53.7 %all-to-all-start = ((bf16[8,128,512]{2,1,0:T(8,128)(2,1)}), bf16[8,128,512]{2,1,0:T(8,128)(2,1)S(1)}, u32[]{:S(2)}, u32[]{:S(2)}) async-start(bf16[8,128,512]{2,1,0:T(8,128)(2,1)} %bitcast.88), calls=%async_computation | async-start | bytes 2097152 | tf_op jit(solution)/shard_map/all_to_all | solution.py:53
  30.2 20.8 %collective-permute-start = (bf16[1,16,512]{2,1,0:T(8,128)(2,1)S(1)}, bf16[1,16,512]{2,1,0:T(8,128)(2,1)S(1)}, u32[]{:S(2)}, u32[]{:S(2)}) collective-permute-start(bf16[1,16,512]{2,1,0:T(8,128)(2,1)S(1)} %bitcast.100), channel_id=1, source_target_pairs={{0,960},{16,976},{32,992},{48,1008},{64,0},{80,16},{96,32},{112,48... | collective-permute-start | bytes 49160 | tf_op jit(solution)/shard_map/ppermute | solution.py:16
  51.0 10.7 %collective-permute-start.1 = (bf16[2,16,512]{2,1,0:T(8,128)(2,1)S(1)}, bf16[2,16,512]{2,1,0:T(8,128)(2,1)S(1)}, u32[]{:S(2)}, u32[]{:S(2)}) collective-permute-start(bf16[2,16,512]{2,1,0:T(8,128)(2,1)S(1)} %pad_maximum_fusion.3), channel_id=1, source_target_pairs={{0,992},{16,1008},{32,0},{48,16},{64,32},{80,48},{96,64},{112,80},... | collective-permute-start | bytes 98312 | tf_op jit(solution)/shard_map/ppermute | solution.py:16
  61.7 9.2 %collective-permute-start.2 = (bf16[4,16,512]{2,1,0:T(8,128)(2,1)S(1)}, bf16[4,16,512]{2,1,0:T(8,128)(2,1)S(1)}, u32[]{:S(2)}, u32[]{:S(2)}) collective-permute-start(bf16[4,16,512]{2,1,0:T(8,128)(2,1)S(1)} %pad_maximum_fusion.2), channel_id=1, source_target_pairs={{0,1008},{16,0},{32,16},{48,32},{64,48},{80,64},{96,80},{112,96},{... | collective-permute-start | bytes 196616 | tf_op jit(solution)/shard_map/ppermute | solution.py:16
  70.9 8.3 %collective-permute-start.3 = (bf16[8,16,512]{2,1,0:T(8,128)(2,1)S(1)}, bf16[8,16,512]{2,1,0:T(8,128)(2,1)S(1)}, u32[]{:S(2)}, u32[]{:S(2)}) collective-permute-start(bf16[8,16,512]{2,1,0:T(8,128)(2,1)S(1)} %pad_maximum_fusion.1), channel_id=1, source_target_pairs={{0,8},{8,0},{1,9},{9,1},{2,10},{10,2},{3,11},{11,3},{4,12},{12,4},... | collective-permute-start | bytes 393224 | tf_op jit(solution)/shard_map/ppermute | solution.py:20
  81.3 14.4 %all-to-all-start.2 = ((f32[8,24,128]{2,1,0:T(8,128)}), f32[8,24,128]{2,1,0:T(8,128)S(1)}, u32[]{:S(2)}, u32[]{:S(2)}) async-start(f32[8,24,128]{2,1,0:T(8,128)} %fusion.17), calls=%async_computation.2 | async-start | bytes 196608 | tf_op jit(solution)/shard_map/all_to_all | solution.py:53
  88.2 70.9 %all-gather.3.cloned.1.call-start = ((), (), s32[]{:S(2)}) async-start(), calls=%async_computation.5 | async-start | bytes 2359296 | tf_op jit(solution)/shard_map/all_gather | solution.py:67
  97.0 10.3 %all-to-all-start.3 = ((bf16[8,24,128]{2,1,0:T(8,128)(2,1)}), bf16[8,24,128]{2,1,0:T(8,128)(2,1)S(1)}, u32[]{:S(2)}, u32[]{:S(2)}) async-start(bf16[8,24,128]{2,1,0:T(8,128)(2,1)} %broadcast_in_dim.63), calls=%async_computation.3 | async-start | bytes 98304 | tf_op jit(solution)/shard_map/all_to_all | solution.py:53
  107.9 6.2 %collective-permute-start.4 = (bf16[8,16,512]{2,1,0:T(8,128)(2,1)S(1)}, bf16[8,16,512]{2,1,0:T(8,128)(2,1)S(1)}, u32[]{:S(2)}, u32[]{:S(2)}) collective-permute-start(bf16[8,16,512]{2,1,0:T(8,128)(2,1)S(1)} %copy.28), channel_id=1, source_target_pairs={{0,8},{8,0},{1,9},{9,1},{2,10},{10,2},{3,11},{11,3},{4,12},{12,4},... | collective-permute-start | bytes 393224 | tf_op jit(solution)/shard_map/ppermute | solution.py:20
  114.3 9.4 %collective-permute-start.5 = (bf16[4,16,512]{2,1,0:T(8,128)(2,1)S(1)}, bf16[4,16,512]{2,1,0:T(8,128)(2,1)S(1)}, u32[]{:S(2)}, u32[]{:S(2)}) collective-permute-start(bf16[4,16,512]{2,1,0:T(8,128)(2,1)S(1)} %slice.162), channel_id=1, source_target_pairs={{0,16},{16,32},{32,48},{48,64},{64,80},{80,96},{96,112},{112,128},... | collective-permute-start | bytes 196616 | tf_op jit(solution)/shard_map/ppermute | solution.py:16
  123.8 8.9 %collective-permute-start.6 = (bf16[2,16,512]{2,1,0:T(8,128)(2,1)S(1)}, bf16[2,16,512]{2,1,0:T(8,128)(2,1)S(1)}, u32[]{:S(2)}, u32[]{:S(2)}) collective-permute-start(bf16[2,16,512]{2,1,0:T(8,128)(2,1)S(1)} %slice.163), channel_id=1, source_target_pairs={{0,32},{16,48},{32,64},{48,80},{64,96},{80,112},{96,128},{112,144}... | collective-permute-start | bytes 98312 | tf_op jit(solution)/shard_map/ppermute | solution.py:16
  132.7 10.5 %collective-permute-start.7 = (bf16[1,16,512]{2,1,0:T(8,128)(2,1)S(1)}, bf16[1,16,512]{2,1,0:T(8,128)(2,1)S(1)}, u32[]{:S(2)}, u32[]{:S(2)}) collective-permute-start(bf16[1,16,512]{2,1,0:T(8,128)(2,1)S(1)} %slice.164), channel_id=1, source_target_pairs={{0,64},{16,80},{32,96},{48,112},{64,128},{80,144},{96,160},{112,17... | collective-permute-start | bytes 49160 | tf_op jit(solution)/shard_map/ppermute | solution.py:16
  143.8 11.3 %all-to-all-start.4 = ((bf16[8,16,512]{2,1,0:T(8,128)(2,1)}), bf16[8,16,512]{2,1,0:T(8,128)(2,1)S(1)}, u32[]{:S(2)}, u32[]{:S(2)}) async-start(bf16[8,16,512]{2,1,0:T(8,128)(2,1)} %broadcast_in_dim.66), calls=%async_computation.4 | async-start | bytes 262144 | tf_op jit(solution)/shard_map/all_to_all | solution.py:53
Sparse Core Ops, SparseCore 0:
  91.7 38.8 all-gather.2

commit v6 on v2

--- a/solution.py
+++ b/solution.py
@@ -14,6 +14,11 @@
 def shift_chips(value, by):
     chips = lax.axis_size("chip")
     return lax.ppermute(value, "chip", [(i, (i + by) % chips) for i in range(chips)])
+
+
+def once(there, value):
+    mark = there.ravel()[0]
+    return jnp.where(mark == mark, value, jnp.zeros_like(value))
 
 
 def halves(value, parts):
@@ -40,6 +45,10 @@
     lists = jnp.concatenate([neighbours, other], axis=0)
     lists = jnp.where(core == 0, lists, lists[::-1])
 
+    ahead = (lists - CORES * chip) % (CORES * lax.axis_size("chip"))
+    far = ahead // CORES
+    spots = (far % 2 * 4 + far // 2 % 2 * 2 + far // 4) * CORES + ahead % CORES
+
     def project(rows):
         part = jnp.dot(rows, out_weight, preferred_element_type=f32).astype(bf16)
         return part.reshape(rows.shape[0], members, feats).transpose(1, 0, 2)
@@ -50,15 +59,14 @@
         return jnp.sum(got, axis=1).astype(bf16)
 
     p_part = project(p_ctx)
-    q_ctx, p_part = lax.optimization_barrier((q_ctx, p_part))
+    q_ctx = once(spots.astype(f32), q_ctx)
     window = reduce_over_tensor(p_part)
     q_pre = reduce_over_tensor(project(q_ctx))
 
-    reach = 1
-    while reach < WINDOW:
+    reach = WINDOW // 2
+    while reach:
         window = jnp.concatenate([window, shift_chips(window, -reach)], axis=0)
-        reach *= 2
-    spots = (lists - CORES * chip) % (CORES * lax.axis_size("chip"))
+        reach //= 2
     cand = window[spots].reshape(CORES, slots, feats)
 
     raw = jnp.einsum("kqf,kcf->kqc", q_pre, cand, preferred_element_type=f32)
@@ -105,10 +113,11 @@
     match = (jnp.arange(WINDOW * CORES, dtype=jnp.int32)[:, None, None] == spots[None]).astype(bf16)
     dwin = jnp.einsum("wks,kspf->wpf", match, dc.reshape(CORES, listed, p_rows, feats), preferred_element_type=f32)
 
-    while reach > 1:
-        reach //= 2
-        away = shift_chips(dwin[CORES * reach :].astype(bf16), reach)
-        dwin = dwin[: CORES * reach] + away.astype(f32)
+    reach = 1
+    while reach < WINDOW:
+        half = dwin.shape[0] // 2
+        dwin = dwin[:half] + shift_chips(dwin[half:].astype(bf16), reach).astype(f32)
+        reach *= 2
     dp = dwin.astype(bf16)
 
     def gather_features(part):

time: 156 us -> 161 us (1.032)
  starting transfers between devices: 79.9 us -> 86 us
  waiting for transfers between devices: 39.7 us -> 37.8 us
    all_to_all x2, waiting for transfers between devices: 3.32 us -> 0.09 us  [reduce_over_tensor(): got = lax.all_to_all(part, MEMBERS, 0, 0)]
    ppermute x6, starting transfers between devices: 31.4 us -> 34.6 us  [shift_chips(): lax.ppermute(value, 'chip', [(i, (i + by) % chips) for i in range(chips)])]
    all_to_all x2, starting transfers between devices: 22.2 us -> 24.6 us  [reduce_over_tensor(): got = lax.all_to_all(part, MEMBERS, 0, 0)]
  transfers between devices with their start and end apart: 12 -> 12, of which waited for: 9 -> 10; matrix products, arithmetic and copies ran while one was open for 7% -> 7% of each run, Pallas kernels for 0% -> 0%
where the time goes in v6:
time: 161 us; the launch traced here: 160 us
  starting transfers between devices  86 us (53%)
  waiting for transfers between devices  37.8 us (23%)
  matrix products  15 us (9%)
  blocking collectives  12.1 us (8%)
  local copies, waits for them, and re-layouts  6.21 us (4%)
  other arithmetic  1.85 us (1%)
    ppermute x6, starting transfers between devices, shift_chips(): lax.ppermute(value, 'chip', [(i, (i + by) % chips) for i in range(chips)])  34.6 us
    ppermute x6, waiting for transfers between devices, shift_chips(): lax.ppermute(value, 'chip', [(i, (i + by) % chips) for i in range(chips)])  25.6 us
    all_to_all x2, starting transfers between devices, reduce_over_tensor(): got = lax.all_to_all(part, MEMBERS, 0, 0)  24.6 us
    all_to_all x2, starting transfers between devices, gather_features(): lax.all_to_all(part.reshape((members,) + part.shape[2:]), MEMBERS, 0, 0)  14.4 us
    all_to_all x1, blocking collectives, on_device(): lax.all_to_all(jnp.broadcast_to(told[None], (members,) + told.shape), MEM...  12.1 us
    all_to_all x1, starting transfers between devices, on_device(): lax.all_to_all(sums.reshape(members, q_part + 8, slots), MEMBERS, 0, 0)  10.4 us
    dot_general x2, matrix products, unproject(): jnp.einsum('mrf,hmf->rh', part, weight, preferred_element_type=f32)  8.36 us
    all_to_all x1, waiting for transfers between devices, on_device(): lax.all_to_all(sums.reshape(members, q_part + 8, slots), MEMBERS, 0, 0)  8.2 us
  transfers between devices with their start and end apart: 12, of which 10 were waited for; matrix products, arithmetic and copies ran while one was open for 7% of the time, Pallas kernels for 0%

profile of v6, /device:TPU:1, one launch (start us, length us, event | category | flops | bytes accessed | tf_op | source)
XLA Modules:
  0.0 160.0 jit_solution(14878094310966602302)
XLA Ops:
  0.7 0.7 copy-done
  1.4 2.8 %convolution_convert_fusion.1 = bf16[16,4096]{1,0:T(8,128)(2,1)S(1)} fusion(bf16[16,512]{1,0:T(8,128)(2,1)S(1)} %copy-done, bf16[512,4096]{1,0:T(8,128)(2,1)} %param.7), kind=kOutput, calls=%fused_computation.2 | convolution fusion | flops 67174400 | bytes 4341760 | tf_op jit(solution)/shard_map/dot_general | solution.py:53
  4.2 0.7 copy.77
  4.9 17.5 %all-to-all-start.1 = ((bf16[16,16,256]{2,1,0:T(8,128)(2,1)}), bf16[16,16,256]{2,1,0:T(8,128)(2,1)S(1)}, u32[]{:S(2)}, u32[]{:S(2)}) async-start(bf16[16,16,256]{2,1,0:T(8,128)(2,1)} %bitcast.83), calls=%async_computation.1 | async-start | bytes 262144 | tf_op jit(solution)/shard_map/all_to_all | solution.py:57
  22.4 2.1 %collective-permute-start = (s32[1,8]{1,0:T(1,128)S(1)}, s32[1,8]{1,0:T(1,128)S(1)}, u32[]{:S(2)}, u32[]{:S(2)}) collective-permute-start(s32[1,8]{1,0:T(1,128)S(1)} %copy-done.2), channel_id=1, source_target_pairs={{0,8},{8,0},{1,9},{9,1},{2,10},{10,2},{3,11},{11,3},{4,12},{12,4},... | collective-permute-start | bytes 104 | tf_op jit(solution)/shard_map/ppermute | solution.py:44
  24.5 0.9 collective-permute-done
  25.5 0.1 reshape.95
  25.6 2.9 %convolution_convert_fusion = bf16[128,4096]{1,0:T(8,128)(2,1)S(1)} fusion(bf16[512,4096]{1,0:T(8,128)(2,1)} %param.7, bf16[128,512]{1,0:T(8,128)(2,1)S(1)} %copy-done.1, pred[]{:T(512)} %bitcast), kind=kOutput, calls=%fused_computation.1 | convolution fusion | flops 537460736 | bytes 5373953 | tf_op jit(solution)/shard_map/dot_general | solution.py:53
  28.5 1.1 copy.76
  29.6 0.1 all-to-all-done.1
  29.7 7.1 %all-to-all-start = ((bf16[16,128,256]{2,1,0:T(8,128)(2,1)}), bf16[16,128,256]{2,1,0:T(8,128)(2,1)S(1)}, u32[]{:S(2)}, u32[]{:S(2)}) async-start(bf16[16,128,256]{2,1,0:T(8,128)(2,1)} %bitcast.81), calls=%async_computation | async-start | bytes 2097152 | tf_op jit(solution)/shard_map/all_to_all | solution.py:57
  36.9 11.3 %collective-permute-start.1 = (bf16[2,16,256]{2,1,0:T(8,128)(2,1)S(1)}, bf16[2,16,256]{2,1,0:T(8,128)(2,1)S(1)}, u32[]{:S(2)}, u32[]{:S(2)}) collective-permute-start(bf16[2,16,256]{2,1,0:T(8,128)(2,1)S(1)} %bitcast_reduce_fusion.1), channel_id=1, source_target_pairs={{0,960},{16,976},{32,992},{48,1008},{64,0},{80,16},{96,32},{112,48... | collective-permute-start | bytes 49160 | tf_op jit(solution)/shard_map/ppermute | solution.py:16
  48.2 0.8 collective-permute-done.1
  49.0 9.7 %collective-permute-start.2 = (bf16[4,16,256]{2,1,0:T(8,128)(2,1)S(1)}, bf16[4,16,256]{2,1,0:T(8,128)(2,1)S(1)}, u32[]{:S(2)}, u32[]{:S(2)}) collective-permute-start(bf16[4,16,256]{2,1,0:T(8,128)(2,1)S(1)} %pad_maximum_fusion.2), channel_id=1, source_target_pairs={{0,992},{16,1008},{32,0},{48,16},{64,32},{80,48},{96,64},{112,80},... | collective-permute-start | bytes 98312 | tf_op jit(solution)/shard_map/ppermute | solution.py:16
  58.7 0.1 reshape.111
  58.8 0.9 collective-permute-done.2
  59.7 7.9 %collective-permute-start.3 = (bf16[8,16,256]{2,1,0:T(8,128)(2,1)S(1)}, bf16[8,16,256]{2,1,0:T(8,128)(2,1)S(1)}, u32[]{:S(2)}, u32[]{:S(2)}) collective-permute-start(bf16[8,16,256]{2,1,0:T(8,128)(2,1)S(1)} %pad_maximum_fusion.1), channel_id=1, source_target_pairs={{0,1008},{16,0},{32,16},{48,32},{64,48},{80,64},{96,80},{112,96},{... | collective-permute-start | bytes 196616 | tf_op jit(solution)/shard_map/ppermute | solution.py:16
  67.6 1.3 collective-permute-done.3
  68.9 0.6 gather_fusion
  69.5 0.1 multiply_reduce_fusion
  69.7 0.1 bitcast_reduce_fusion
  69.8 0.1 fusion.20
  69.9 0.2 fusion.51
  70.2 0.8 maximum_maximum_fusion
  71.0 10.4 %all-to-all-start.2 = ((f32[16,24,128]{2,1,0:T(8,128)}), f32[16,24,128]{2,1,0:T(8,128)S(1)}, u32[]{:S(2)}, u32[]{:S(2)}) async-start(f32[16,24,128]{2,1,0:T(8,128)} %maximum_maximum_fusion), calls=%async_computation.2 | async-start | bytes 393216 | tf_op jit(solution)/shard_map/all_to_all | solution.py:79
  81.4 8.2 %all-to-all-done.2 = f32[16,24,128]{2,1,0:T(8,128)S(1)} async-done(((f32[16,24,128]{2,1,0:T(8,128)}), f32[16,24,128]{2,1,0:T(8,128)S(1)}, u32[]{:S(2)}, u32[]{:S(2)}) %all-to-all-start.2) | async-done | bytes 196640 | tf_op jit(solution)/shard_map/all_to_all | solution.py:79
  89.6 0.2 select_reduce_fusion
  89.9 0.2 fusion.30
  90.1 0.1 concatenate.38
  90.3 12.1 %all_to_all.30 = bf16[16,24,128]{2,1,0:T(8,128)(2,1)S(1)} all-to-all(bf16[16,24,128]{2,1,0:T(8,128)(2,1)S(1)} %broadcast_in_dim.24), channel_id=1, replica_groups=mesh['chip'=64,'core'=2,'tensor'=8] {'core','tensor'}, dimensions={0} | all-to-all | bytes 196608 | tf_op jit(solution)/shard_map/all_to_all | solution.py:100
  102.5 0.1 mul.106
  102.5 0.2 fusion.9
  102.7 1.1 broadcast_in_dim.25
  103.8 4.6 %all-to-all-start.4 = ((bf16[16,128,256]{2,1,0:T(8,128)(2,1)}), bf16[16,128,256]{2,1,0:T(8,128)(2,1)S(1)}, u32[]{:S(2)}, u32[]{:S(2)}) async-start(bf16[16,128,256]{2,1,0:T(8,128)(2,1)} %bitcast.18), calls=%async_computation.4 | async-start | bytes 2097152 | tf_op jit(solution)/shard_map/all_to_all | solution.py:125
  108.4 0.2 fusion.10
  108.7 0.3 convolution_bitcast_fusion
  109.0 1.9 %collective-permute-start.4 = (bf16[8,16,256]{2,0,1:T(8,128)(2,1)S(1)}, bf16[8,16,256]{2,0,1:T(8,128)(2,1)S(1)}, u32[]{:S(2)}, u32[]{:S(2)}) collective-permute-start(bf16[8,16,256]{2,0,1:T(8,128)(2,1)S(1)} %slice.148), channel_id=1, source_target_pairs={{0,16},{16,32},{32,48},{48,64},{64,80},{80,96},{96,112},{112,128},... | collective-permute-start | bytes 196616 | tf_op jit(solution)/shard_map/ppermute | solution.py:16
  110.9 7.8 %collective-permute-done.4 = bf16[8,16,256]{2,0,1:T(8,128)(2,1)S(1)} collective-permute-done((bf16[8,16,256]{2,0,1:T(8,128)(2,1)S(1)}, bf16[8,16,256]{2,0,1:T(8,128)(2,1)S(1)}, u32[]{:S(2)}, u32[]{:S(2)}) %collective-permute-start.4) | collective-permute-done | bytes 65568 | tf_op jit(solution)/shard_map/ppermute | solution.py:16
  118.7 1.9 %collective-permute-start.5 = (bf16[4,16,256]{2,0,1:T(4,128)(2,1)S(1)}, bf16[4,16,256]{2,0,1:T(4,128)(2,1)S(1)}, u32[]{:S(2)}, u32[]{:S(2)}) collective-permute-start(bf16[4,16,256]{2,0,1:T(4,128)(2,1)S(1)} %slice.149), channel_id=1, source_target_pairs={{0,32},{16,48},{32,64},{48,80},{64,96},{80,112},{96,128},{112,144}... | collective-permute-start | bytes 98312 | tf_op jit(solution)/shard_map/ppermute | solution.py:16
  120.6 6.9 %collective-permute-done.5 = bf16[4,16,256]{2,0,1:T(4,128)(2,1)S(1)} collective-permute-done((bf16[4,16,256]{2,0,1:T(4,128)(2,1)S(1)}, bf16[4,16,256]{2,0,1:T(4,128)(2,1)S(1)}, u32[]{:S(2)}, u32[]{:S(2)}) %collective-permute-start.5) | collective-permute-done | bytes 32800 | tf_op jit(solution)/shard_map/ppermute | solution.py:16
  127.6 1.9 %collective-permute-start.6 = (bf16[2,16,256]{2,0,1:T(2,128)(2,1)S(1)}, bf16[2,16,256]{2,0,1:T(2,128)(2,1)S(1)}, u32[]{:S(2)}, u32[]{:S(2)}) collective-permute-start(bf16[2,16,256]{2,0,1:T(2,128)(2,1)S(1)} %slice.150), channel_id=1, source_target_pairs={{0,64},{16,80},{32,96},{48,112},{64,128},{80,144},{96,160},{112,17... | collective-permute-start | bytes 49160 | tf_op jit(solution)/shard_map/ppermute | solution.py:16
  129.6 0.6 select_n.79
  130.2 8.0 %collective-permute-done.6 = bf16[2,16,256]{2,0,1:T(2,128)(2,1)S(1)} collective-permute-done((bf16[2,16,256]{2,0,1:T(2,128)(2,1)S(1)}, bf16[2,16,256]{2,0,1:T(2,128)(2,1)S(1)}, u32[]{:S(2)}, u32[]{:S(2)}) %collective-permute-start.6) | collective-permute-done | bytes 16416 | tf_op jit(solution)/shard_map/ppermute | solution.py:16
  138.2 0.6 broadcast_in_dim.26
  138.8 9.8 %all-to-all-start.5 = ((bf16[16,16,256]{2,1,0:T(8,128)(2,1)}), bf16[16,16,256]{2,1,0:T(8,128)(2,1)S(1)}, u32[]{:S(2)}, u32[]{:S(2)}) async-start(bf16[16,16,256]{2,1,0:T(8,128)(2,1)} %bitcast.24), calls=%async_computation.5 | async-start | bytes 262144 | tf_op jit(solution)/shard_map/all_to_all | solution.py:125
  148.7 4.4 %fusion.11 = bf16[128,512]{1,0:T(8,128)(2,1)} fusion(bf16[16,128,256]{2,1,0:T(8,128)(2,1)S(1)} %all-to-all-done.4, bf16[64,16,8,256]{3,2,1,0:T(8,128)(2,1)} %bitcast.85), kind=kOutput, calls=%fused_computation.15 | convolution fusion | flops 536936448 | bytes 5373952 | tf_op jit(solution)/shard_map/mrf,hmf->rh/dot_general | solution.py:129
  153.0 2.9 %all-to-all-done.5 = bf16[16,16,256]{2,1,0:T(8,128)(2,1)S(1)} async-done(((bf16[16,16,256]{2,1,0:T(8,128)(2,1)}), bf16[16,16,256]{2,1,0:T(8,128)(2,1)S(1)}, u32[]{:S(2)}, u32[]{:S(2)}) %all-to-all-start.5) | async-done | bytes 131104 | tf_op jit(solution)/shard_map/all_to_all | solution.py:125
  156.0 4.0 %fusion.17 = bf16[16,512]{1,0:T(8,128)(2,1)} fusion(bf16[16,16,256]{2,1,0:T(8,128)(2,1)S(1)} %all-to-all-done.5, bf16[64,16,8,256]{3,2,1,0:T(8,128)(2,1)} %bitcast.86), kind=kOutput, calls=%fused_computation.17 | convolution fusion | flops 67117056 | bytes 4341760 | tf_op jit(solution)/shard_map/mrf,hmf->rh/dot_general | solution.py:129
  (51 shorter events, 0.9 us)
Async XLA Ops:
  0.6 0.7 copy-start
  0.6 21.7 %copy-start.2 = (s32[1,8]{1,0:T(1,128)S(1)}, s32[1,8]{1,0:T(1,128)}, u32[]{:S(2)}) copy-start(s32[1,8]{1,0:T(1,128)} %param.8) | copy-start | bytes 100
  0.7 25.0 %copy-start.1 = (bf16[128,512]{1,0:T(8,128)(2,1)S(1)}, bf16[128,512]{1,0:T(8,128)(2,1)}, u32[]{:S(2)}) copy-start(bf16[128,512]{1,0:T(8,128)(2,1)} %param.5) | copy-start | bytes 393220
  4.9 24.9 %all-to-all-start.1 = ((bf16[16,16,256]{2,1,0:T(8,128)(2,1)}), bf16[16,16,256]{2,1,0:T(8,128)(2,1)S(1)}, u32[]{:S(2)}, u32[]{:S(2)}) async-start(bf16[16,16,256]{2,1,0:T(8,128)(2,1)} %bitcast.83), calls=%async_computation.1 | async-start | bytes 262144 | tf_op jit(solution)/shard_map/all_to_all | solution.py:57
  22.4 3.0 %collective-permute-start = (s32[1,8]{1,0:T(1,128)S(1)}, s32[1,8]{1,0:T(1,128)S(1)}, u32[]{:S(2)}, u32[]{:S(2)}) collective-permute-start(s32[1,8]{1,0:T(1,128)S(1)} %copy-done.2), channel_id=1, source_target_pairs={{0,8},{8,0},{1,9},{9,1},{2,10},{10,2},{3,11},{11,3},{4,12},{12,4},... | collective-permute-start | bytes 104 | tf_op jit(solution)/shard_map/ppermute | solution.py:44
  28.5 52.8 %copy-start.3 = (s32[128]{0:T(128)S(1)}, s32[128]{0:T(128)}, u32[]{:S(2)}) copy-start(s32[128]{0:T(128)} %param.9) | copy-start | bytes 1540
  29.7 39.9 %all-to-all-start = ((bf16[16,128,256]{2,1,0:T(8,128)(2,1)}), bf16[16,128,256]{2,1,0:T(8,128)(2,1)S(1)}, u32[]{:S(2)}, u32[]{:S(2)}) async-start(bf16[16,128,256]{2,1,0:T(8,128)(2,1)} %bitcast.81), calls=%async_computation | async-start | bytes 2097152 | tf_op jit(solution)/shard_map/all_to_all | solution.py:57
  36.9 12.1 %collective-permute-start.1 = (bf16[2,16,256]{2,1,0:T(8,128)(2,1)S(1)}, bf16[2,16,256]{2,1,0:T(8,128)(2,1)S(1)}, u32[]{:S(2)}, u32[]{:S(2)}) collective-permute-start(bf16[2,16,256]{2,1,0:T(8,128)(2,1)S(1)} %bitcast_reduce_fusion.1), channel_id=1, source_target_pairs={{0,960},{16,976},{32,992},{48,1008},{64,0},{80,16},{96,32},{112,48... | collective-permute-start | bytes 49160 | tf_op jit(solution)/shard_map/ppermute | solution.py:16
  49.0 10.7 %collective-permute-start.2 = (bf16[4,16,256]{2,1,0:T(8,128)(2,1)S(1)}, bf16[4,16,256]{2,1,0:T(8,128)(2,1)S(1)}, u32[]{:S(2)}, u32[]{:S(2)}) collective-permute-start(bf16[4,16,256]{2,1,0:T(8,128)(2,1)S(1)} %pad_maximum_fusion.2), channel_id=1, source_target_pairs={{0,992},{16,1008},{32,0},{48,16},{64,32},{80,48},{96,64},{112,80},... | collective-permute-start | bytes 98312 | tf_op jit(solution)/shard_map/ppermute | solution.py:16
  59.7 9.2 %collective-permute-start.3 = (bf16[8,16,256]{2,1,0:T(8,128)(2,1)S(1)}, bf16[8,16,256]{2,1,0:T(8,128)(2,1)S(1)}, u32[]{:S(2)}, u32[]{:S(2)}) collective-permute-start(bf16[8,16,256]{2,1,0:T(8,128)(2,1)S(1)} %pad_maximum_fusion.1), channel_id=1, source_target_pairs={{0,1008},{16,0},{32,16},{48,32},{64,48},{80,64},{96,80},{112,96},{... | collective-permute-start | bytes 196616 | tf_op jit(solution)/shard_map/ppermute | solution.py:16
  71.0 18.6 %all-to-all-start.2 = ((f32[16,24,128]{2,1,0:T(8,128)}), f32[16,24,128]{2,1,0:T(8,128)S(1)}, u32[]{:S(2)}, u32[]{:S(2)}) async-start(f32[16,24,128]{2,1,0:T(8,128)} %maximum_maximum_fusion), calls=%async_computation.2 | async-start | bytes 393216 | tf_op jit(solution)/shard_map/all_to_all | solution.py:79
  103.8 34.3 %all-to-all-start.4 = ((bf16[16,128,256]{2,1,0:T(8,128)(2,1)}), bf16[16,128,256]{2,1,0:T(8,128)(2,1)S(1)}, u32[]{:S(2)}, u32[]{:S(2)}) async-start(bf16[16,128,256]{2,1,0:T(8,128)(2,1)} %bitcast.18), calls=%async_computation.4 | async-start | bytes 2097152 | tf_op jit(solution)/shard_map/all_to_all | solution.py:125
  109.0 9.7 %collective-permute-start.4 = (bf16[8,16,256]{2,0,1:T(8,128)(2,1)S(1)}, bf16[8,16,256]{2,0,1:T(8,128)(2,1)S(1)}, u32[]{:S(2)}, u32[]{:S(2)}) collective-permute-start(bf16[8,16,256]{2,0,1:T(8,128)(2,1)S(1)} %slice.148), channel_id=1, source_target_pairs={{0,16},{16,32},{32,48},{48,64},{64,80},{80,96},{96,112},{112,128},... | collective-permute-start | bytes 196616 | tf_op jit(solution)/shard_map/ppermute | solution.py:16
  118.7 8.9 %collective-permute-start.5 = (bf16[4,16,256]{2,0,1:T(4,128)(2,1)S(1)}, bf16[4,16,256]{2,0,1:T(4,128)(2,1)S(1)}, u32[]{:S(2)}, u32[]{:S(2)}) collective-permute-start(bf16[4,16,256]{2,0,1:T(4,128)(2,1)S(1)} %slice.149), channel_id=1, source_target_pairs={{0,32},{16,48},{32,64},{48,80},{64,96},{80,112},{96,128},{112,144}... | collective-permute-start | bytes 98312 | tf_op jit(solution)/shard_map/ppermute | solution.py:16
  127.6 10.5 %collective-permute-start.6 = (bf16[2,16,256]{2,0,1:T(2,128)(2,1)S(1)}, bf16[2,16,256]{2,0,1:T(2,128)(2,1)S(1)}, u32[]{:S(2)}, u32[]{:S(2)}) collective-permute-start(bf16[2,16,256]{2,0,1:T(2,128)(2,1)S(1)} %slice.150), channel_id=1, source_target_pairs={{0,64},{16,80},{32,96},{48,112},{64,128},{80,144},{96,160},{112,17... | collective-permute-start | bytes 49160 | tf_op jit(solution)/shard_map/ppermute | solution.py:16
  138.8 17.1 %all-to-all-start.5 = ((bf16[16,16,256]{2,1,0:T(8,128)(2,1)}), bf16[16,16,256]{2,1,0:T(8,128)(2,1)S(1)}, u32[]{:S(2)}, u32[]{:S(2)}) async-start(bf16[16,16,256]{2,1,0:T(8,128)(2,1)} %bitcast.24), calls=%async_computation.5 | async-start | bytes 262144 | tf_op jit(solution)/shard_map/all_to_all | solution.py:125

commit v7 on v5

v7 whole, which is shorter than its diff:
```python
import jax
import jax.numpy as jnp
from jax import lax
from jax.sharding import Mesh
from jax.sharding import PartitionSpec as P

SCALE = 50.0
EPS = 1e-06
WINDOW = 8
CORES = 2


def shift_chips(value, by):
    chips = lax.axis_size("chip")
    return lax.ppermute(value, "chip", [(i, (i + by) % chips) for i in range(chips)])


def swap_cores(value):
    return lax.ppermute(value, "core", [(0, 1), (1, 0)])


def on_device(q_ctx, p_ctx, out_weight, neighbours, positive):
    f32, bf16 = jnp.float32, jnp.bfloat16
    q_rows, p_rows = q_ctx.shape[0], p_ctx.shape[0]
    listed = neighbours.shape[1]
    slots = listed * p_rows
    tensors = lax.axis_size("tensor")
    feats = out_weight.shape[1] // tensors
    core, chip = lax.axis_index("core"), lax.axis_index("chip")

    ahead = (neighbours[0] - CORES * chip) % (CORES * lax.axis_size("chip"))
    spots = ahead // CORES + jnp.where(ahead % CORES == core, 0, WINDOW)

    def project(rows):
        part = jnp.dot(rows, out_weight, preferred_element_type=f32).astype(bf16)
        return part.reshape(rows.shape[0], tensors, feats).transpose(1, 0, 2)

    def exchange(part):
        return lax.all_to_all(part, "tensor", 0, 0)

    p_part = project(p_ctx)
    q_ctx, p_part = lax.optimization_barrier((q_ctx, p_part))
    window = jnp.sum(exchange(p_part).astype(f32), axis=0).astype(bf16)[None]
    q_pre = jnp.sum(exchange(project(q_ctx)).astype(f32), axis=0).astype(bf16)

    reach = 1
    while reach < WINDOW:
        window = jnp.concatenate([window, shift_chips(window, -reach)], axis=0)
        reach *= 2
    window = jnp.concatenate([window, swap_cores(window)], axis=0)
    cand = window[spots].reshape(slots, feats)

    raw = jnp.dot(q_pre, cand.T, preferred_element_type=f32)
    q_sq = jnp.sum(jnp.square(q_pre.astype(f32)), axis=-1)
    c_sq = jnp.sum(jnp.square(cand.astype(f32)), axis=-1)
    sums = jnp.concatenate([raw, q_sq.reshape(-1, slots), c_sq[None], jnp.zeros((7 - q_rows // slots, slots), f32)])
    sums = jnp.sum(exchange(jnp.broadcast_to(sums, (tensors,) + sums.shape)), axis=0)
    raw = sums[:q_rows]
    inv_q = lax.rsqrt(sums[q_rows : q_rows + q_rows // slots].reshape(q_rows) + EPS)
    inv_c = lax.rsqrt(sums[q_rows + q_rows // slots] + EPS)

    scores = raw * (SCALE * inv_q)[:, None] * inv_c[None, :]
    lse = jnp.log(jnp.sum(jnp.exp(scores), axis=-1))
    onehot = (jnp.arange(slots, dtype=jnp.int32)[None, :] == positive[:, None]).astype(f32)
    losses = lse - jnp.sum(scores * onehot, axis=-1)
    dscore = jnp.exp(scores - lse[:, None]) - onehot
    coef = lax.reduce_precision(dscore * (SCALE * inv_q)[:, None] * inv_c[None, :], 8, 7)
    weighted = coef * raw
    q_inner = (jnp.square(inv_q) * jnp.sum(weighted, axis=-1))[:, None]
    c_inner = (jnp.square(inv_c) * jnp.sum(weighted, axis=0))[:, None]
    coef = coef.astype(bf16)

    dq = jnp.dot(coef, cand, preferred_element_type=f32)
    dq = (dq - q_inner * q_pre.astype(f32)).astype(bf16)
    dq = exchange(jnp.broadcast_to(dq, (tensors,) + dq.shape))

    dc = lax.dot_general(coef, q_pre, (((0,), (0,)), ((), ())), preferred_element_type=f32)
    dc = (dc - c_inner * cand.astype(f32)).astype(bf16).reshape(listed, p_rows * feats)
    match = (jnp.arange(CORES * WINDOW, dtype=jnp.int32)[:, None] == spots[None]).astype(bf16)
    dwin = jnp.dot(match, dc, preferred_element_type=f32).reshape(CORES * WINDOW, p_rows, feats)
    dwin = dwin[:WINDOW] + swap_cores(dwin[WINDOW:].astype(bf16)).astype(f32)
    reach = WINDOW
    while reach > 1:
        reach //= 2
        dwin = dwin[:reach] + shift_chips(dwin[reach:].astype(bf16), reach).astype(f32)
    dp = dwin.astype(bf16)

    dq, dp = lax.optimization_barrier((dq, dp))
    dp = exchange(jnp.broadcast_to(dp, (tensors, p_rows, feats)))
    weight = out_weight.reshape(out_weight.shape[0], tensors, feats)

    def unproject(part):
        return jnp.einsum("mrf,hmf->rh", part, weight, preferred_element_type=f32).astype(bf16)

    return unproject(dq), unproject(dp), losses


def solution(mesh):
    dp, tensors = mesh.shape["dp"], mesh.shape["tensor"]
    fine = Mesh(mesh.devices.reshape(dp // CORES, CORES, tensors), ("chip", "core", "tensor"))
    rows = ("chip", "core")
    placed = (P(rows, "tensor"), P(rows, "tensor"), P("tensor", None), P(rows, None), P(rows))
    return jax.shard_map(
        on_device,
        mesh=fine,
        in_specs=placed,
        out_specs=(P(rows, "tensor"), P(rows, "tensor"), P(rows)),
        check_vma=False,
    )
```

time: 173 us -> 158 us (0.913)
  between operations: 14.5 us -> 0.98 us
  waiting for transfers between devices: 52.5 us -> 48.1 us
  starting transfers between devices: 80.8 us -> 84.1 us
    ppermute x6, waiting for transfers between devices: 26 us -> 20 us  [shift_chips(): lax.ppermute(value, 'chip', [(i, (i + by) % chips) for i in range(chips)])]
    all_to_all x5, starting transfers between devices: 24.9 us -> 28.7 us  [exchange(): return lax.all_to_all(part, 'tensor', 0, 0)]
    ppermute x2, starting transfers between devices: 12.6 us -> 9.55 us  [swap_cores(): return lax.ppermute(value, 'core', [(0, 1), (1, 0)])]
    ppermute x6, starting transfers between devices: 43.3 us -> 45.9 us  [shift_chips(): lax.ppermute(value, 'chip', [(i, (i + by) % chips) for i in range(chips)])]
  transfers between devices with their start and end apart: 14 -> 13, of which waited for: 12 -> 11; matrix products, arithmetic and copies ran while one was open for 8% -> 7% of each run, Pallas kernels for 0% -> 0%
where the time goes in v7:
time: 158 us; the launch traced here: 155 us
  starting transfers between devices  84.1 us (53%)
  waiting for transfers between devices  48.1 us (30%)
  matrix products  15.1 us (10%)
  local copies, waits for them, and re-layouts  5.24 us (3%)
  other arithmetic  1.7 us (1%)
    ppermute x6, starting transfers between devices, shift_chips(): lax.ppermute(value, 'chip', [(i, (i + by) % chips) for i in range(chips)])  45.9 us
    all_to_all x5, starting transfers between devices, exchange(): return lax.all_to_all(part, 'tensor', 0, 0)  28.7 us
    all_to_all x5, waiting for transfers between devices, exchange(): return lax.all_to_all(part, 'tensor', 0, 0)  26.2 us
    ppermute x6, waiting for transfers between devices, shift_chips(): lax.ppermute(value, 'chip', [(i, (i + by) % chips) for i in range(chips)])  20 us
    ppermute x2, starting transfers between devices, swap_cores(): return lax.ppermute(value, 'core', [(0, 1), (1, 0)])  9.55 us
    dot_general x2, matrix products, unproject(): jnp.einsum('mrf,hmf->rh', part, weight, preferred_element_type=f32)  8.36 us
    dot_general x2, matrix products, project(): part = jnp.dot(rows, out_weight, preferred_element_type=f32).astype(bf16)  5.81 us
  transfers between devices with their start and end apart: 13, of which 11 were waited for; matrix products, arithmetic and copies ran while one was open for 7% of the time, Pallas kernels for 0%

profile of v7, /device:TPU:1, one launch (start us, length us, event | category | flops | bytes accessed | tf_op | source)
XLA Modules:
  0.0 155.3 jit_solution(7129877387781114814)
XLA Ops:
  0.6 2.9 %convolution_convert_fusion.1 = bf16[16,4096]{1,0:T(8,128)(2,1)S(1)} fusion(bf16[16,512]{1,0:T(8,128)(2,1)} %param.6, bf16[512,4096]{1,0:T(8,128)(2,1)} %param.7), kind=kOutput, calls=%fused_computation.2 | convolution fusion | flops 67174400 | bytes 4341760 | tf_op jit(solution)/shard_map/dot_general | solution.py:35
  3.5 0.7 copy.49
  4.2 7.7 %all-to-all-start.1 = ((bf16[8,16,512]{2,1,0:T(8,128)(2,1)}), bf16[8,16,512]{2,1,0:T(8,128)(2,1)S(1)}, u32[]{:S(2)}, u32[]{:S(2)}) async-start(bf16[8,16,512]{2,1,0:T(8,128)(2,1)} %bitcast.69), calls=%async_computation.1 | async-start | bytes 262144 | tf_op jit(solution)/shard_map/all_to_all | solution.py:39
  11.9 2.9 %convolution_convert_fusion = bf16[128,4096]{1,0:T(8,128)(2,1)S(1)} fusion(bf16[128,512]{1,0:T(8,128)(2,1)S(1)} %copy-done, bf16[512,4096]{1,0:T(8,128)(2,1)} %param.7), kind=kOutput, calls=%fused_computation.1 | convolution fusion | flops 537395200 | bytes 5373952 | tf_op jit(solution)/shard_map/dot_general | solution.py:35
  14.8 1.1 copy.48
  15.9 3.9 %all-to-all-done.1 = bf16[8,16,512]{2,1,0:T(8,128)(2,1)S(1)} async-done(((bf16[8,16,512]{2,1,0:T(8,128)(2,1)}), bf16[8,16,512]{2,1,0:T(8,128)(2,1)S(1)}, u32[]{:S(2)}, u32[]{:S(2)}) %all-to-all-start.1) | async-done | bytes 131104 | tf_op jit(solution)/shard_map/all_to_all | solution.py:39
  19.8 3.6 %all-to-all-start = ((bf16[8,128,512]{2,1,0:T(8,128)(2,1)}), bf16[8,128,512]{2,1,0:T(8,128)(2,1)S(1)}, u32[]{:S(2)}, u32[]{:S(2)}) async-start(bf16[8,128,512]{2,1,0:T(8,128)(2,1)} %bitcast.67), calls=%async_computation | async-start | bytes 2097152 | tf_op jit(solution)/shard_map/all_to_all | solution.py:39
  23.4 20.0 %collective-permute-start = (bf16[1,16,512]{2,1,0:T(8,128)(2,1)S(1)}, bf16[1,16,512]{2,1,0:T(8,128)(2,1)S(1)}, u32[]{:S(2)}, u32[]{:S(2)}) collective-permute-start(bf16[1,16,512]{2,1,0:T(8,128)(2,1)S(1)} %bitcast.79), channel_id=1, source_target_pairs={{0,1008},{16,0},{32,16},{48,32},{64,48},{80,64},{96,80},{112,96},{... | collective-permute-start | bytes 49160 | tf_op jit(solution)/shard_map/ppermute | solution.py:15
  43.4 0.1 pad.3.clone
  43.5 0.7 collective-permute-done
  44.3 3.6 %collective-permute-start.1 = (bf16[2,16,512]{2,1,0:T(8,128)(2,1)S(1)}, bf16[2,16,512]{2,1,0:T(8,128)(2,1)S(1)}, u32[]{:S(2)}, u32[]{:S(2)}) collective-permute-start(bf16[2,16,512]{2,1,0:T(8,128)(2,1)S(1)} %pad_maximum_fusion.2), channel_id=1, source_target_pairs={{0,992},{16,1008},{32,0},{48,16},{64,32},{80,48},{96,64},{112,80},... | collective-permute-start | bytes 98312 | tf_op jit(solution)/shard_map/ppermute | solution.py:15
  47.9 1.9 %collective-permute-done.1 = bf16[2,16,512]{2,1,0:T(8,128)(2,1)S(1)} collective-permute-done((bf16[2,16,512]{2,1,0:T(8,128)(2,1)S(1)}, bf16[2,16,512]{2,1,0:T(8,128)(2,1)S(1)}, u32[]{:S(2)}, u32[]{:S(2)}) %collective-permute-start.1) | collective-permute-done | bytes 32800 | tf_op jit(solution)/shard_map/ppermute | solution.py:15
  49.8 3.9 %collective-permute-start.2 = (bf16[4,16,512]{2,1,0:T(8,128)(2,1)S(1)}, bf16[4,16,512]{2,1,0:T(8,128)(2,1)S(1)}, u32[]{:S(2)}, u32[]{:S(2)}) collective-permute-start(bf16[4,16,512]{2,1,0:T(8,128)(2,1)S(1)} %pad_maximum_fusion.1), channel_id=1, source_target_pairs={{0,960},{16,976},{32,992},{48,1008},{64,0},{80,16},{96,32},{112,48... | collective-permute-start | bytes 196616 | tf_op jit(solution)/shard_map/ppermute | solution.py:15
  53.7 5.2 %collective-permute-done.2 = bf16[4,16,512]{2,1,0:T(8,128)(2,1)S(1)} collective-permute-done((bf16[4,16,512]{2,1,0:T(8,128)(2,1)S(1)}, bf16[4,16,512]{2,1,0:T(8,128)(2,1)S(1)}, u32[]{:S(2)}, u32[]{:S(2)}) %collective-permute-start.2) | collective-permute-done | bytes 65568 | tf_op jit(solution)/shard_map/ppermute | solution.py:15
  59.0 7.1 %collective-permute-start.3 = (bf16[8,16,512]{2,1,0:T(8,128)(2,1)S(1)}, bf16[8,16,512]{2,1,0:T(8,128)(2,1)S(1)}, u32[]{:S(2)}, u32[]{:S(2)}) collective-permute-start(bf16[8,16,512]{2,1,0:T(8,128)(2,1)S(1)} %pad_maximum_fusion), channel_id=1, source_target_pairs={{0,8},{8,0},{1,9},{9,1},{2,10},{10,2},{3,11},{11,3},{4,12},{12,4},... | collective-permute-start | bytes 393224 | tf_op jit(solution)/shard_map/ppermute | solution.py:19
  66.2 0.9 collective-permute-done.3
  67.1 0.6 gather_fusion
  67.7 0.1 multiply_reduce_fusion
  67.8 0.1 broadcast_in_dim.44
  67.9 0.1 reduce_sum.87
  68.0 0.1 fusion.19
  68.1 0.2 fusion.39
  68.3 0.1 maximum_maximum_fusion
  68.4 0.8 broadcast_in_dim.46
  69.2 6.8 %all-to-all-start.2 = ((f32[8,136,128]{2,1,0:T(8,128)}), f32[8,136,128]{2,1,0:T(8,128)S(1)}, u32[]{:S(2)}, u32[]{:S(2)}) async-start(f32[8,136,128]{2,1,0:T(8,128)} %broadcast_in_dim.46), calls=%async_computation.2 | async-start | bytes 1114112 | tf_op jit(solution)/shard_map/all_to_all | solution.py:39
  76.1 18.6 %all-to-all-done.2 = f32[8,136,128]{2,1,0:T(8,128)S(1)} async-done(((f32[8,136,128]{2,1,0:T(8,128)}), f32[8,136,128]{2,1,0:T(8,128)S(1)}, u32[]{:S(2)}, u32[]{:S(2)}) %all-to-all-start.2) | async-done | bytes 557088 | tf_op jit(solution)/shard_map/all_to_all | solution.py:39
  94.8 0.2 exponential_reduce_fusion
  95.0 0.2 fusion.21
  95.2 0.3 fusion.9
  95.5 1.1 broadcast_in_dim.47
  96.6 3.6 %all-to-all-start.3 = ((bf16[8,128,512]{2,1,0:T(8,128)(2,1)}), bf16[8,128,512]{2,1,0:T(8,128)(2,1)S(1)}, u32[]{:S(2)}, u32[]{:S(2)}) async-start(bf16[8,128,512]{2,1,0:T(8,128)(2,1)} %broadcast_in_dim.47), calls=%async_computation.3 | async-start | bytes 2097152 | tf_op jit(solution)/shard_map/all_to_all | solution.py:39
  100.2 0.3 subtract_convert_fusion
  100.5 0.2 fusion.28
  100.8 2.4 %collective-permute-start.4 = (bf16[8,16,512]{2,1,0:T(8,128)(2,1)S(1)}, bf16[8,16,512]{2,1,0:T(8,128)(2,1)S(1)}, u32[]{:S(2)}, u32[]{:S(2)}) collective-permute-start(bf16[8,16,512]{2,1,0:T(8,128)(2,1)S(1)} %copy.22), channel_id=1, source_target_pairs={{0,8},{8,0},{1,9},{9,1},{2,10},{10,2},{3,11},{11,3},{4,12},{12,4},... | collective-permute-start | bytes 393224 | tf_op jit(solution)/shard_map/ppermute | solution.py:19
  103.3 0.9 collective-permute-done.4
  104.2 0.2 copy_add_fusion
  104.4 1.9 %collective-permute-start.5 = (bf16[4,16,512]{2,1,0:T(8,128)(2,1)S(1)}, bf16[4,16,512]{2,1,0:T(8,128)(2,1)S(1)}, u32[]{:S(2)}, u32[]{:S(2)}) collective-permute-start(bf16[4,16,512]{2,1,0:T(8,128)(2,1)S(1)} %slice.112), channel_id=1, source_target_pairs={{0,64},{16,80},{32,96},{48,112},{64,128},{80,144},{96,160},{112,17... | collective-permute-start | bytes 196616 | tf_op jit(solution)/shard_map/ppermute | solution.py:15
  106.3 9.2 %collective-permute-done.5 = bf16[4,16,512]{2,1,0:T(8,128)(2,1)S(1)} collective-permute-done((bf16[4,16,512]{2,1,0:T(8,128)(2,1)S(1)}, bf16[4,16,512]{2,1,0:T(8,128)(2,1)S(1)}, u32[]{:S(2)}, u32[]{:S(2)}) %collective-permute-start.5) | collective-permute-done | bytes 65568 | tf_op jit(solution)/shard_map/ppermute | solution.py:15
  115.5 7.7 %collective-permute-start.6 = (bf16[2,16,512]{2,1,0:T(8,128)(2,1)S(1)}, bf16[2,16,512]{2,1,0:T(8,128)(2,1)S(1)}, u32[]{:S(2)}, u32[]{:S(2)}) collective-permute-start(bf16[2,16,512]{2,1,0:T(8,128)(2,1)S(1)} %slice.113), channel_id=1, source_target_pairs={{0,32},{16,48},{32,64},{48,80},{64,96},{80,112},{96,128},{112,144}... | collective-permute-start | bytes 98312 | tf_op jit(solution)/shard_map/ppermute | solution.py:15
  123.2 1.3 collective-permute-done.6
  124.6 8.8 %collective-permute-start.7 = (bf16[1,16,512]{2,1,0:T(8,128)(2,1)S(1)}, bf16[1,16,512]{2,1,0:T(8,128)(2,1)S(1)}, u32[]{:S(2)}, u32[]{:S(2)}) collective-permute-start(bf16[1,16,512]{2,1,0:T(8,128)(2,1)S(1)} %slice.114), channel_id=1, source_target_pairs={{0,16},{16,32},{32,48},{48,64},{64,80},{80,96},{96,112},{112,128},... | collective-permute-start | bytes 49160 | tf_op jit(solution)/shard_map/ppermute | solution.py:15
  133.4 0.5 log_subtract_fusion
  133.9 1.6 %collective-permute-done.7 = bf16[1,16,512]{2,1,0:T(8,128)(2,1)S(1)} collective-permute-done((bf16[1,16,512]{2,1,0:T(8,128)(2,1)S(1)}, bf16[1,16,512]{2,1,0:T(8,128)(2,1)S(1)}, u32[]{:S(2)}, u32[]{:S(2)}) %collective-permute-start.7) | collective-permute-done | bytes 16416 | tf_op jit(solution)/shard_map/ppermute | solution.py:15
  135.5 0.6 broadcast_in_dim.50
  136.2 7.1 %all-to-all-start.4 = ((bf16[8,16,512]{2,1,0:T(8,128)(2,1)}), bf16[8,16,512]{2,1,0:T(8,128)(2,1)S(1)}, u32[]{:S(2)}, u32[]{:S(2)}) async-start(bf16[8,16,512]{2,1,0:T(8,128)(2,1)} %broadcast_in_dim.50), calls=%async_computation.4 | async-start | bytes 262144 | tf_op jit(solution)/shard_map/all_to_all | solution.py:39
  143.3 4.4 %fusion.10 = bf16[128,512]{1,0:T(8,128)(2,1)} fusion(bf16[8,128,512]{2,1,0:T(8,128)(2,1)S(1)} %all-to-all-done.3, bf16[64,8,8,512]{3,2,1,0:T(8,128)(2,1)} %bitcast.70), kind=kOutput, calls=%fused_computation.12 | convolution fusion | flops 536936448 | bytes 5373952 | tf_op jit(solution)/shard_map/mrf,hmf->rh/dot_general | solution.py:93
  147.7 3.7 %all-to-all-done.4 = bf16[8,16,512]{2,1,0:T(8,128)(2,1)S(1)} async-done(((bf16[8,16,512]{2,1,0:T(8,128)(2,1)}), bf16[8,16,512]{2,1,0:T(8,128)(2,1)S(1)}, u32[]{:S(2)}, u32[]{:S(2)}) %all-to-all-start.4) | async-done | bytes 131104 | tf_op jit(solution)/shard_map/all_to_all | solution.py:39
  151.3 4.0 %fusion.16 = bf16[16,512]{1,0:T(8,128)(2,1)} fusion(bf16[8,16,512]{2,1,0:T(8,128)(2,1)S(1)} %all-to-all-done.4, bf16[64,8,8,512]{3,2,1,0:T(8,128)(2,1)} %bitcast.71), kind=kOutput, calls=%fused_computation.14 | convolution fusion | flops 67117056 | bytes 4341760 | tf_op jit(solution)/shard_map/mrf,hmf->rh/dot_general | solution.py:93
  (35 shorter events, 0.4 us)
Async XLA Ops:
  0.6 11.2 %copy-start = (bf16[128,512]{1,0:T(8,128)(2,1)S(1)}, bf16[128,512]{1,0:T(8,128)(2,1)}, u32[]{:S(2)}) copy-start(bf16[128,512]{1,0:T(8,128)(2,1)} %param.5) | copy-start | bytes 393220
  4.2 15.6 %all-to-all-start.1 = ((bf16[8,16,512]{2,1,0:T(8,128)(2,1)}), bf16[8,16,512]{2,1,0:T(8,128)(2,1)S(1)}, u32[]{:S(2)}, u32[]{:S(2)}) async-start(bf16[8,16,512]{2,1,0:T(8,128)(2,1)} %bitcast.69), calls=%async_computation.1 | async-start | bytes 262144 | tf_op jit(solution)/shard_map/all_to_all | solution.py:39
  11.9 11.5 %copy-start.1 = (s32[1,8]{1,0:T(1,128)S(1)}, s32[1,8]{1,0:T(1,128)}, u32[]{:S(2)}) copy-start(s32[1,8]{1,0:T(1,128)} %param.8) | copy-start | bytes 100
  15.9 79.1 %copy-start.2 = (s32[128]{0:T(128)S(1)}, s32[128]{0:T(128)}, u32[]{:S(2)}) copy-start(s32[128]{0:T(128)} %param.9) | copy-start | bytes 1540
  19.8 48.1 %all-to-all-start = ((bf16[8,128,512]{2,1,0:T(8,128)(2,1)}), bf16[8,128,512]{2,1,0:T(8,128)(2,1)S(1)}, u32[]{:S(2)}, u32[]{:S(2)}) async-start(bf16[8,128,512]{2,1,0:T(8,128)(2,1)} %bitcast.67), calls=%async_computation | async-start | bytes 2097152 | tf_op jit(solution)/shard_map/all_to_all | solution.py:39
  23.4 20.8 %collective-permute-start = (bf16[1,16,512]{2,1,0:T(8,128)(2,1)S(1)}, bf16[1,16,512]{2,1,0:T(8,128)(2,1)S(1)}, u32[]{:S(2)}, u32[]{:S(2)}) collective-permute-start(bf16[1,16,512]{2,1,0:T(8,128)(2,1)S(1)} %bitcast.79), channel_id=1, source_target_pairs={{0,1008},{16,0},{32,16},{48,32},{64,48},{80,64},{96,80},{112,96},{... | collective-permute-start | bytes 49160 | tf_op jit(solution)/shard_map/ppermute | solution.py:15
  44.3 5.5 %collective-permute-start.1 = (bf16[2,16,512]{2,1,0:T(8,128)(2,1)S(1)}, bf16[2,16,512]{2,1,0:T(8,128)(2,1)S(1)}, u32[]{:S(2)}, u32[]{:S(2)}) collective-permute-start(bf16[2,16,512]{2,1,0:T(8,128)(2,1)S(1)} %pad_maximum_fusion.2), channel_id=1, source_target_pairs={{0,992},{16,1008},{32,0},{48,16},{64,32},{80,48},{96,64},{112,80},... | collective-permute-start | bytes 98312 | tf_op jit(solution)/shard_map/ppermute | solution.py:15
  49.8 9.1 %collective-permute-start.2 = (bf16[4,16,512]{2,1,0:T(8,128)(2,1)S(1)}, bf16[4,16,512]{2,1,0:T(8,128)(2,1)S(1)}, u32[]{:S(2)}, u32[]{:S(2)}) collective-permute-start(bf16[4,16,512]{2,1,0:T(8,128)(2,1)S(1)} %pad_maximum_fusion.1), channel_id=1, source_target_pairs={{0,960},{16,976},{32,992},{48,1008},{64,0},{80,16},{96,32},{112,48... | collective-permute-start | bytes 196616 | tf_op jit(solution)/shard_map/ppermute | solution.py:15
  59.0 8.1 %collective-permute-start.3 = (bf16[8,16,512]{2,1,0:T(8,128)(2,1)S(1)}, bf16[8,16,512]{2,1,0:T(8,128)(2,1)S(1)}, u32[]{:S(2)}, u32[]{:S(2)}) collective-permute-start(bf16[8,16,512]{2,1,0:T(8,128)(2,1)S(1)} %pad_maximum_fusion), channel_id=1, source_target_pairs={{0,8},{8,0},{1,9},{9,1},{2,10},{10,2},{3,11},{11,3},{4,12},{12,4},... | collective-permute-start | bytes 393224 | tf_op jit(solution)/shard_map/ppermute | solution.py:19
  69.2 25.5 %all-to-all-start.2 = ((f32[8,136,128]{2,1,0:T(8,128)}), f32[8,136,128]{2,1,0:T(8,128)S(1)}, u32[]{:S(2)}, u32[]{:S(2)}) async-start(f32[8,136,128]{2,1,0:T(8,128)} %broadcast_in_dim.46), calls=%async_computation.2 | async-start | bytes 1114112 | tf_op jit(solution)/shard_map/all_to_all | solution.py:39
  96.6 38.9 %all-to-all-start.3 = ((bf16[8,128,512]{2,1,0:T(8,128)(2,1)}), bf16[8,128,512]{2,1,0:T(8,128)(2,1)S(1)}, u32[]{:S(2)}, u32[]{:S(2)}) async-start(bf16[8,128,512]{2,1,0:T(8,128)(2,1)} %broadcast_in_dim.47), calls=%async_computation.3 | async-start | bytes 2097152 | tf_op jit(solution)/shard_map/all_to_all | solution.py:39
  100.8 3.4 %collective-permute-start.4 = (bf16[8,16,512]{2,1,0:T(8,128)(2,1)S(1)}, bf16[8,16,512]{2,1,0:T(8,128)(2,1)S(1)}, u32[]{:S(2)}, u32[]{:S(2)}) collective-permute-start(bf16[8,16,512]{2,1,0:T(8,128)(2,1)S(1)} %copy.22), channel_id=1, source_target_pairs={{0,8},{8,0},{1,9},{9,1},{2,10},{10,2},{3,11},{11,3},{4,12},{12,4},... | collective-permute-start | bytes 393224 | tf_op jit(solution)/shard_map/ppermute | solution.py:19
  104.4 11.1 %collective-permute-start.5 = (bf16[4,16,512]{2,1,0:T(8,128)(2,1)S(1)}, bf16[4,16,512]{2,1,0:T(8,128)(2,1)S(1)}, u32[]{:S(2)}, u32[]{:S(2)}) collective-permute-start(bf16[4,16,512]{2,1,0:T(8,128)(2,1)S(1)} %slice.112), channel_id=1, source_target_pairs={{0,64},{16,80},{32,96},{48,112},{64,128},{80,144},{96,160},{112,17... | collective-permute-start | bytes 196616 | tf_op jit(solution)/shard_map/ppermute | solution.py:15
  115.5 9.0 %collective-permute-start.6 = (bf16[2,16,512]{2,1,0:T(8,128)(2,1)S(1)}, bf16[2,16,512]{2,1,0:T(8,128)(2,1)S(1)}, u32[]{:S(2)}, u32[]{:S(2)}) collective-permute-start(bf16[2,16,512]{2,1,0:T(8,128)(2,1)S(1)} %slice.113), channel_id=1, source_target_pairs={{0,32},{16,48},{32,64},{48,80},{64,96},{80,112},{96,128},{112,144}... | collective-permute-start | bytes 98312 | tf_op jit(solution)/shard_map/ppermute | solution.py:15
  124.6 11.0 %collective-permute-start.7 = (bf16[1,16,512]{2,1,0:T(8,128)(2,1)S(1)}, bf16[1,16,512]{2,1,0:T(8,128)(2,1)S(1)}, u32[]{:S(2)}, u32[]{:S(2)}) collective-permute-start(bf16[1,16,512]{2,1,0:T(8,128)(2,1)S(1)} %slice.114), channel_id=1, source_target_pairs={{0,16},{16,32},{32,48},{48,64},{64,80},{80,96},{96,112},{112,128},... | collective-permute-start | bytes 49160 | tf_op jit(solution)/shard_map/ppermute | solution.py:15
  136.2 15.1 %all-to-all-start.4 = ((bf16[8,16,512]{2,1,0:T(8,128)(2,1)}), bf16[8,16,512]{2,1,0:T(8,128)(2,1)S(1)}, u32[]{:S(2)}, u32[]{:S(2)}) async-start(bf16[8,16,512]{2,1,0:T(8,128)(2,1)} %broadcast_in_dim.50), calls=%async_computation.4 | async-start | bytes 262144 | tf_op jit(solution)/shard_map/all_to_all | solution.py:39

commit v8 on v2

--- a/solution.py
+++ b/solution.py
@@ -1,6 +1,8 @@
 import jax
 import jax.numpy as jnp
 from jax import lax
+from jax.experimental import pallas as pl
+from jax.experimental.pallas import tpu as pltpu
 from jax.sharding import Mesh
 from jax.sharding import PartitionSpec as P
 
@@ -14,6 +16,20 @@
 def shift_chips(value, by):
     chips = lax.axis_size("chip")
     return lax.ppermute(value, "chip", [(i, (i + by) % chips) for i in range(chips)])
+
+
+def relay_kernel(value_ref, _, out_ref):
+    out_ref[...] = value_ref[...]
+
+
+def relay(value, wanted, cost):
+    return pl.pallas_call(
+        relay_kernel,
+        in_specs=[pl.BlockSpec(memory_space=pltpu.VMEM), pl.BlockSpec(memory_space=pl.ANY)],
+        out_specs=pl.BlockSpec(memory_space=pltpu.VMEM),
+        out_shape=jax.ShapeDtypeStruct(value.shape, value.dtype),
+        cost_estimate=pl.CostEstimate(flops=cost, bytes_accessed=cost // 1000, transcendentals=0),
+    )(value, wanted)
 
 
 def halves(value, parts):
@@ -95,7 +111,7 @@
     row = told[:, :, q_part].astype(f32)
     q_inner = (row[..., :q_part] + row[..., q_part : 2 * q_part]).reshape(CORES, q_rows, 1)
     loss = row[..., 2 * q_part : 3 * q_part] + row[..., 3 * q_part : 4 * q_part] + row[..., 4 * q_part : 5 * q_part]
-    losses = jnp.where(core == 0, loss[0], loss[1]).reshape(q_rows)
+    losses = relay(jnp.where(core == 0, loss[0], loss[1]), told, 12500000000).reshape(q_rows)
     c_inner = jnp.sum(told[:, :, q_part + 1 : q_part + 3].astype(f32), axis=(1, 2))[..., None]
 
     dq = jnp.einsum("kqc,kcf->kqf", coef, cand, preferred_element_type=f32)

time: 156 us -> 150 us (0.962)
  starting transfers between devices: 79.9 us -> 73.3 us
  waiting for transfers between devices: 39.7 us -> 37.6 us
    ppermute x6, waiting for transfers between devices: 25.3 us -> 17.4 us  [shift_chips(): lax.ppermute(value, 'chip', [(i, (i + by) % chips) for i in range(chips)])]
    all_to_all x2, waiting for transfers between devices: 2.92 us -> 8.71 us  [gather_features(): lax.all_to_all(part.reshape((members,) + part.shape[2:]), MEMBERS, 0, 0)]
    all_to_all x2, starting transfers between devices: 14.1 us -> 9.41 us  [gather_features(): lax.all_to_all(part.reshape((members,) + part.shape[2:]), MEMBERS, 0, 0)]
    ppermute x6, starting transfers between devices: 31.4 us -> 29.5 us  [shift_chips(): lax.ppermute(value, 'chip', [(i, (i + by) % chips) for i in range(chips)])]
  transfers between devices with their start and end apart: 12 -> 12, of which waited for: 9 -> 9; matrix products, arithmetic and copies ran while one was open for 7% -> 9% of each run, Pallas kernels for 0% -> 1%
where the time goes in v8:
time: 150 us; the launch traced here: 149 us
  starting transfers between devices  73.3 us (49%)
  waiting for transfers between devices  37.6 us (25%)
  matrix products  15 us (10%)
  blocking collectives  12.1 us (8%)
  local copies, waits for them, and re-layouts  6.1 us (4%)
  other arithmetic  2.42 us (2%)
    ppermute x6, starting transfers between devices, shift_chips(): lax.ppermute(value, 'chip', [(i, (i + by) % chips) for i in range(chips)])  29.5 us
    all_to_all x2, starting transfers between devices, reduce_over_tensor(): got = lax.all_to_all(part, MEMBERS, 0, 0)  22.2 us
    ppermute x6, waiting for transfers between devices, shift_chips(): lax.ppermute(value, 'chip', [(i, (i + by) % chips) for i in range(chips)])  17.4 us
    all_to_all x1, blocking collectives, on_device(): lax.all_to_all(jnp.broadcast_to(told[None], (members,) + told.shape), MEM...  12.1 us
    all_to_all x1, starting transfers between devices, on_device(): lax.all_to_all(sums.reshape(members, q_part + 8, slots), MEMBERS, 0, 0)  10.1 us
    all_to_all x2, starting transfers between devices, gather_features(): lax.all_to_all(part.reshape((members,) + part.shape[2:]), MEMBERS, 0, 0)  9.41 us
    all_to_all x2, waiting for transfers between devices, gather_features(): lax.all_to_all(part.reshape((members,) + part.shape[2:]), MEMBERS, 0, 0)  8.71 us
    dot_general x2, matrix products, unproject(): jnp.einsum('mrf,hmf->rh', part, weight, preferred_element_type=f32)  8.36 us
  transfers between devices with their start and end apart: 12, of which 9 were waited for; matrix products, arithmetic and copies ran while one was open for 9% of the time, Pallas kernels for 1%

profile of v8, /device:TPU:1, one launch (start us, length us, event | category | flops | bytes accessed | tf_op | source)
XLA Modules:
  0.0 148.8 jit_solution(11798801744881965152)
XLA Ops:
  0.6 2.9 %convolution_convert_fusion.1 = bf16[16,4096]{1,0:T(8,128)(2,1)S(1)} fusion(bf16[16,512]{1,0:T(8,128)(2,1)} %param.6, bf16[512,4096]{1,0:T(8,128)(2,1)} %param.7), kind=kOutput, calls=%fused_computation.2 | convolution fusion | flops 67174400 | bytes 4341760 | tf_op jit(solution)/shard_map/dot_general | solution.py:60
  3.5 0.7 copy.70
  4.2 17.5 %all-to-all-start.1 = ((bf16[16,16,256]{2,1,0:T(8,128)(2,1)}), bf16[16,16,256]{2,1,0:T(8,128)(2,1)S(1)}, u32[]{:S(2)}, u32[]{:S(2)}) async-start(bf16[16,16,256]{2,1,0:T(8,128)(2,1)} %bitcast.81), calls=%async_computation.1 | async-start | bytes 262144 | tf_op jit(solution)/shard_map/all_to_all | solution.py:64
  21.7 2.9 %convolution_convert_fusion = bf16[128,4096]{1,0:T(8,128)(2,1)S(1)} fusion(bf16[128,512]{1,0:T(8,128)(2,1)S(1)} %copy-done, bf16[512,4096]{1,0:T(8,128)(2,1)} %param.7), kind=kOutput, calls=%fused_computation.1 | convolution fusion | flops 537395200 | bytes 5373952 | tf_op jit(solution)/shard_map/dot_general | solution.py:60
  24.7 1.1 copy.69
  25.8 3.3 %all-to-all-done.1 = bf16[16,16,256]{2,1,0:T(8,128)(2,1)S(1)} async-done(((bf16[16,16,256]{2,1,0:T(8,128)(2,1)}), bf16[16,16,256]{2,1,0:T(8,128)(2,1)S(1)}, u32[]{:S(2)}, u32[]{:S(2)}) %all-to-all-start.1) | async-done | bytes 131104 | tf_op jit(solution)/shard_map/all_to_all | solution.py:64
  29.1 4.7 %all-to-all-start = ((bf16[16,128,256]{2,1,0:T(8,128)(2,1)}), bf16[16,128,256]{2,1,0:T(8,128)(2,1)S(1)}, u32[]{:S(2)}, u32[]{:S(2)}) async-start(bf16[16,128,256]{2,1,0:T(8,128)(2,1)} %bitcast.79), calls=%async_computation | async-start | bytes 2097152 | tf_op jit(solution)/shard_map/all_to_all | solution.py:64
  33.8 2.1 %collective-permute-start.3 = (s32[1,8]{1,0:T(1,128)S(1)}, s32[1,8]{1,0:T(1,128)S(1)}, u32[]{:S(2)}, u32[]{:S(2)}) collective-permute-start(s32[1,8]{1,0:T(1,128)S(1)} %copy-done.2), channel_id=1, source_target_pairs={{0,8},{8,0},{1,9},{9,1},{2,10},{10,2},{3,11},{11,3},{4,12},{12,4},... | collective-permute-start | bytes 104 | tf_op jit(solution)/shard_map/ppermute | solution.py:55
  36.0 11.2 %collective-permute-start = (bf16[2,16,256]{2,1,0:T(8,128)(2,1)S(1)}, bf16[2,16,256]{2,1,0:T(8,128)(2,1)S(1)}, u32[]{:S(2)}, u32[]{:S(2)}) collective-permute-start(bf16[2,16,256]{2,1,0:T(8,128)(2,1)S(1)} %bitcast_reduce_fusion.1), channel_id=1, source_target_pairs={{0,1008},{16,0},{32,16},{48,32},{64,48},{80,64},{96,80},{112,96},{... | collective-permute-start | bytes 49160 | tf_op jit(solution)/shard_map/ppermute | solution.py:18
  47.3 0.8 collective-permute-done
  48.1 3.9 %collective-permute-start.1 = (bf16[4,16,256]{2,1,0:T(8,128)(2,1)S(1)}, bf16[4,16,256]{2,1,0:T(8,128)(2,1)S(1)}, u32[]{:S(2)}, u32[]{:S(2)}) collective-permute-start(bf16[4,16,256]{2,1,0:T(8,128)(2,1)S(1)} %pad_maximum_fusion.2), channel_id=1, source_target_pairs={{0,992},{16,1008},{32,0},{48,16},{64,32},{80,48},{96,64},{112,80},... | collective-permute-start | bytes 98312 | tf_op jit(solution)/shard_map/ppermute | solution.py:18
  52.0 0.1 reshape.107
  52.1 1.8 %collective-permute-done.1 = bf16[4,16,256]{2,1,0:T(8,128)(2,1)S(1)} collective-permute-done((bf16[4,16,256]{2,1,0:T(8,128)(2,1)S(1)}, bf16[4,16,256]{2,1,0:T(8,128)(2,1)S(1)}, u32[]{:S(2)}, u32[]{:S(2)}) %collective-permute-start.1) | collective-permute-done | bytes 32800 | tf_op jit(solution)/shard_map/ppermute | solution.py:18
  54.0 3.9 %collective-permute-start.2 = (bf16[8,16,256]{2,1,0:T(8,128)(2,1)S(1)}, bf16[8,16,256]{2,1,0:T(8,128)(2,1)S(1)}, u32[]{:S(2)}, u32[]{:S(2)}) collective-permute-start(bf16[8,16,256]{2,1,0:T(8,128)(2,1)S(1)} %pad_maximum_fusion.1), channel_id=1, source_target_pairs={{0,960},{16,976},{32,992},{48,1008},{64,0},{80,16},{96,32},{112,48... | collective-permute-start | bytes 196616 | tf_op jit(solution)/shard_map/ppermute | solution.py:18
  57.9 5.8 %collective-permute-done.2 = bf16[8,16,256]{2,1,0:T(8,128)(2,1)S(1)} collective-permute-done((bf16[8,16,256]{2,1,0:T(8,128)(2,1)S(1)}, bf16[8,16,256]{2,1,0:T(8,128)(2,1)S(1)}, u32[]{:S(2)}, u32[]{:S(2)}) %collective-permute-start.2) | collective-permute-done | bytes 65568 | tf_op jit(solution)/shard_map/ppermute | solution.py:18
  63.7 0.6 gather_fusion
  64.2 0.1 multiply_reduce_fusion
  64.3 0.1 broadcast_in_dim.17
  64.4 0.1 bitcast_reduce_fusion
  64.6 0.1 fusion.20
  64.7 0.2 fusion.39
  65.0 0.8 maximum_maximum_fusion
  65.7 10.1 %all-to-all-start.2 = ((f32[16,24,128]{2,1,0:T(8,128)}), f32[16,24,128]{2,1,0:T(8,128)S(1)}, u32[]{:S(2)}, u32[]{:S(2)}) async-start(f32[16,24,128]{2,1,0:T(8,128)} %maximum_maximum_fusion), calls=%async_computation.2 | async-start | bytes 393216 | tf_op jit(solution)/shard_map/all_to_all | solution.py:87
  75.9 8.2 %all-to-all-done.2 = f32[16,24,128]{2,1,0:T(8,128)S(1)} async-done(((f32[16,24,128]{2,1,0:T(8,128)}), f32[16,24,128]{2,1,0:T(8,128)S(1)}, u32[]{:S(2)}, u32[]{:S(2)}) %all-to-all-start.2) | async-done | bytes 196640 | tf_op jit(solution)/shard_map/all_to_all | solution.py:87
  84.1 0.2 select_reduce_fusion
  84.3 0.2 fusion.27
  84.6 0.1 concatenate.38
  84.8 12.1 %all_to_all.30 = bf16[16,24,128]{2,1,0:T(8,128)(2,1)S(1)} all-to-all(bf16[16,24,128]{2,1,0:T(8,128)(2,1)S(1)} %broadcast_in_dim.21), channel_id=1, replica_groups=mesh['chip'=64,'core'=2,'tensor'=8] {'core','tensor'}, dimensions={0} | all-to-all | bytes 196608 | tf_op jit(solution)/shard_map/all_to_all | solution.py:108
  97.0 0.2 fusion.10
  97.2 0.3 convolution_bitcast_fusion
  97.5 1.9 %collective-permute-start.4 = (bf16[8,16,256]{2,0,1:T(8,128)(2,1)S(1)}, bf16[8,16,256]{2,0,1:T(8,128)(2,1)S(1)}, u32[]{:S(2)}, u32[]{:S(2)}) collective-permute-start(bf16[8,16,256]{2,0,1:T(8,128)(2,1)S(1)} %slice.147), channel_id=1, source_target_pairs={{0,64},{16,80},{32,96},{48,112},{64,128},{80,144},{96,160},{112,17... | collective-permute-start | bytes 196616 | tf_op jit(solution)/shard_map/ppermute | solution.py:18
  99.5 0.1 mul.90
  99.5 0.2 fusion.9
  99.7 1.1 broadcast_in_dim.22
  100.8 4.6 %all-to-all-start.4 = ((bf16[16,128,256]{2,1,0:T(8,128)(2,1)}), bf16[16,128,256]{2,1,0:T(8,128)(2,1)S(1)}, u32[]{:S(2)}, u32[]{:S(2)}) async-start(bf16[16,128,256]{2,1,0:T(8,128)(2,1)} %bitcast.16), calls=%async_computation.4 | async-start | bytes 2097152 | tf_op jit(solution)/shard_map/all_to_all | solution.py:132
  105.4 3.2 %collective-permute-done.4 = bf16[8,16,256]{2,0,1:T(8,128)(2,1)S(1)} collective-permute-done((bf16[8,16,256]{2,0,1:T(8,128)(2,1)S(1)}, bf16[8,16,256]{2,0,1:T(8,128)(2,1)S(1)}, u32[]{:S(2)}, u32[]{:S(2)}) %collective-permute-start.4) | collective-permute-done | bytes 65568 | tf_op jit(solution)/shard_map/ppermute | solution.py:18
  108.6 3.1 %collective-permute-start.5 = (bf16[4,16,256]{2,0,1:T(4,128)(2,1)S(1)}, bf16[4,16,256]{2,0,1:T(4,128)(2,1)S(1)}, u32[]{:S(2)}, u32[]{:S(2)}) collective-permute-start(bf16[4,16,256]{2,0,1:T(4,128)(2,1)S(1)} %slice.148), channel_id=1, source_target_pairs={{0,32},{16,48},{32,64},{48,80},{64,96},{80,112},{96,128},{112,144}... | collective-permute-start | bytes 98312 | tf_op jit(solution)/shard_map/ppermute | solution.py:18
  111.8 0.6 fusion.25.value_ref
  112.4 5.8 %collective-permute-done.5 = bf16[4,16,256]{2,0,1:T(4,128)(2,1)S(1)} collective-permute-done((bf16[4,16,256]{2,0,1:T(4,128)(2,1)S(1)}, bf16[4,16,256]{2,0,1:T(4,128)(2,1)S(1)}, u32[]{:S(2)}, u32[]{:S(2)}) %collective-permute-start.5) | collective-permute-done | bytes 32800 | tf_op jit(solution)/shard_map/ppermute | solution.py:18
  118.3 5.4 %collective-permute-start.6 = (bf16[2,16,256]{2,0,1:T(2,128)(2,1)S(1)}, bf16[2,16,256]{2,0,1:T(2,128)(2,1)S(1)}, u32[]{:S(2)}, u32[]{:S(2)}) collective-permute-start(bf16[2,16,256]{2,0,1:T(2,128)(2,1)S(1)} %slice.149), channel_id=1, source_target_pairs={{0,16},{16,32},{32,48},{48,64},{64,80},{80,96},{96,112},{112,128},... | collective-permute-start | bytes 49160 | tf_op jit(solution)/shard_map/ppermute | solution.py:18
  123.7 1.3 shard_map.76
  124.9 1.3 reshape.103
  126.2 5.8 %all-to-all-done.4 = bf16[16,128,256]{2,1,0:T(8,128)(2,1)S(1)} async-done(((bf16[16,128,256]{2,1,0:T(8,128)(2,1)}), bf16[16,128,256]{2,1,0:T(8,128)(2,1)S(1)}, u32[]{:S(2)}, u32[]{:S(2)}) %all-to-all-start.4) | async-done | bytes 1048608 | tf_op jit(solution)/shard_map/all_to_all | solution.py:132
  132.0 0.6 broadcast_in_dim.23
  132.7 4.8 %all-to-all-start.5 = ((bf16[16,16,256]{2,1,0:T(8,128)(2,1)}), bf16[16,16,256]{2,1,0:T(8,128)(2,1)S(1)}, u32[]{:S(2)}, u32[]{:S(2)}) async-start(bf16[16,16,256]{2,1,0:T(8,128)(2,1)} %bitcast.22), calls=%async_computation.5 | async-start | bytes 262144 | tf_op jit(solution)/shard_map/all_to_all | solution.py:132
  137.5 4.4 %fusion.11 = bf16[128,512]{1,0:T(8,128)(2,1)} fusion(bf16[16,128,256]{2,1,0:T(8,128)(2,1)S(1)} %all-to-all-done.4, bf16[64,16,8,256]{3,2,1,0:T(8,128)(2,1)} %bitcast.82), kind=kOutput, calls=%fused_computation.15 | convolution fusion | flops 536936448 | bytes 5373952 | tf_op jit(solution)/shard_map/mrf,hmf->rh/dot_general | solution.py:136
  141.9 2.9 %all-to-all-done.5 = bf16[16,16,256]{2,1,0:T(8,128)(2,1)S(1)} async-done(((bf16[16,16,256]{2,1,0:T(8,128)(2,1)}), bf16[16,16,256]{2,1,0:T(8,128)(2,1)S(1)}, u32[]{:S(2)}, u32[]{:S(2)}) %all-to-all-start.5) | async-done | bytes 131104 | tf_op jit(solution)/shard_map/all_to_all | solution.py:132
  144.8 4.0 %fusion.17 = bf16[16,512]{1,0:T(8,128)(2,1)} fusion(bf16[16,16,256]{2,1,0:T(8,128)(2,1)S(1)} %all-to-all-done.5, bf16[64,16,8,256]{3,2,1,0:T(8,128)(2,1)} %bitcast.83), kind=kOutput, calls=%fused_computation.17 | convolution fusion | flops 67117056 | bytes 4341760 | tf_op jit(solution)/shard_map/mrf,hmf->rh/dot_general | solution.py:136
  (49 shorter events, 0.8 us)
Async XLA Ops:
  0.6 21.1 %copy-start = (bf16[128,512]{1,0:T(8,128)(2,1)S(1)}, bf16[128,512]{1,0:T(8,128)(2,1)}, u32[]{:S(2)}) copy-start(bf16[128,512]{1,0:T(8,128)(2,1)} %param.5) | copy-start | bytes 393220
  4.2 24.9 %all-to-all-start.1 = ((bf16[16,16,256]{2,1,0:T(8,128)(2,1)}), bf16[16,16,256]{2,1,0:T(8,128)(2,1)S(1)}, u32[]{:S(2)}, u32[]{:S(2)}) async-start(bf16[16,16,256]{2,1,0:T(8,128)(2,1)} %bitcast.81), calls=%async_computation.1 | async-start | bytes 262144 | tf_op jit(solution)/shard_map/all_to_all | solution.py:64
  21.7 12.1 %copy-start.2 = (s32[1,8]{1,0:T(1,128)S(1)}, s32[1,8]{1,0:T(1,128)}, u32[]{:S(2)}) copy-start(s32[1,8]{1,0:T(1,128)} %param.8) | copy-start | bytes 100
  24.7 51.2 %copy-start.3 = (s32[128]{0:T(128)S(1)}, s32[128]{0:T(128)}, u32[]{:S(2)}) copy-start(s32[128]{0:T(128)} %param.9) | copy-start | bytes 1540
  29.1 35.4 %all-to-all-start = ((bf16[16,128,256]{2,1,0:T(8,128)(2,1)}), bf16[16,128,256]{2,1,0:T(8,128)(2,1)S(1)}, u32[]{:S(2)}, u32[]{:S(2)}) async-start(bf16[16,128,256]{2,1,0:T(8,128)(2,1)} %bitcast.79), calls=%async_computation | async-start | bytes 2097152 | tf_op jit(solution)/shard_map/all_to_all | solution.py:64
  33.8 13.4 %collective-permute-start.3 = (s32[1,8]{1,0:T(1,128)S(1)}, s32[1,8]{1,0:T(1,128)S(1)}, u32[]{:S(2)}, u32[]{:S(2)}) collective-permute-start(s32[1,8]{1,0:T(1,128)S(1)} %copy-done.2), channel_id=1, source_target_pairs={{0,8},{8,0},{1,9},{9,1},{2,10},{10,2},{3,11},{11,3},{4,12},{12,4},... | collective-permute-start | bytes 104 | tf_op jit(solution)/shard_map/ppermute | solution.py:55
  36.0 12.1 %collective-permute-start = (bf16[2,16,256]{2,1,0:T(8,128)(2,1)S(1)}, bf16[2,16,256]{2,1,0:T(8,128)(2,1)S(1)}, u32[]{:S(2)}, u32[]{:S(2)}) collective-permute-start(bf16[2,16,256]{2,1,0:T(8,128)(2,1)S(1)} %bitcast_reduce_fusion.1), channel_id=1, source_target_pairs={{0,1008},{16,0},{32,16},{48,32},{64,48},{80,64},{96,80},{112,96},{... | collective-permute-start | bytes 49160 | tf_op jit(solution)/shard_map/ppermute | solution.py:18
  48.1 5.8 %collective-permute-start.1 = (bf16[4,16,256]{2,1,0:T(8,128)(2,1)S(1)}, bf16[4,16,256]{2,1,0:T(8,128)(2,1)S(1)}, u32[]{:S(2)}, u32[]{:S(2)}) collective-permute-start(bf16[4,16,256]{2,1,0:T(8,128)(2,1)S(1)} %pad_maximum_fusion.2), channel_id=1, source_target_pairs={{0,992},{16,1008},{32,0},{48,16},{64,32},{80,48},{96,64},{112,80},... | collective-permute-start | bytes 98312 | tf_op jit(solution)/shard_map/ppermute | solution.py:18
  54.0 9.7 %collective-permute-start.2 = (bf16[8,16,256]{2,1,0:T(8,128)(2,1)S(1)}, bf16[8,16,256]{2,1,0:T(8,128)(2,1)S(1)}, u32[]{:S(2)}, u32[]{:S(2)}) collective-permute-start(bf16[8,16,256]{2,1,0:T(8,128)(2,1)S(1)} %pad_maximum_fusion.1), channel_id=1, source_target_pairs={{0,960},{16,976},{32,992},{48,1008},{64,0},{80,16},{96,32},{112,48... | collective-permute-start | bytes 196616 | tf_op jit(solution)/shard_map/ppermute | solution.py:18
  65.7 18.4 %all-to-all-start.2 = ((f32[16,24,128]{2,1,0:T(8,128)}), f32[16,24,128]{2,1,0:T(8,128)S(1)}, u32[]{:S(2)}, u32[]{:S(2)}) async-start(f32[16,24,128]{2,1,0:T(8,128)} %maximum_maximum_fusion), calls=%async_computation.2 | async-start | bytes 393216 | tf_op jit(solution)/shard_map/all_to_all | solution.py:87
  96.9 26.8 %copy-start.1 = (bf16[16,24,128]{2,1,0:T(8,128)(2,1)}, bf16[16,24,128]{2,1,0:T(8,128)(2,1)S(1)}, u32[]{:S(2)}) copy-start(bf16[16,24,128]{2,1,0:T(8,128)(2,1)S(1)} %all_to_all.30) | copy-start | bytes 294916
  97.5 11.1 %collective-permute-start.4 = (bf16[8,16,256]{2,0,1:T(8,128)(2,1)S(1)}, bf16[8,16,256]{2,0,1:T(8,128)(2,1)S(1)}, u32[]{:S(2)}, u32[]{:S(2)}) collective-permute-start(bf16[8,16,256]{2,0,1:T(8,128)(2,1)S(1)} %slice.147), channel_id=1, source_target_pairs={{0,64},{16,80},{32,96},{48,112},{64,128},{80,144},{96,160},{112,17... | collective-permute-start | bytes 196616 | tf_op jit(solution)/shard_map/ppermute | solution.py:18
  100.8 31.2 %all-to-all-start.4 = ((bf16[16,128,256]{2,1,0:T(8,128)(2,1)}), bf16[16,128,256]{2,1,0:T(8,128)(2,1)S(1)}, u32[]{:S(2)}, u32[]{:S(2)}) async-start(bf16[16,128,256]{2,1,0:T(8,128)(2,1)} %bitcast.16), calls=%async_computation.4 | async-start | bytes 2097152 | tf_op jit(solution)/shard_map/all_to_all | solution.py:132
  108.6 9.6 %collective-permute-start.5 = (bf16[4,16,256]{2,0,1:T(4,128)(2,1)S(1)}, bf16[4,16,256]{2,0,1:T(4,128)(2,1)S(1)}, u32[]{:S(2)}, u32[]{:S(2)}) collective-permute-start(bf16[4,16,256]{2,0,1:T(4,128)(2,1)S(1)} %slice.148), channel_id=1, source_target_pairs={{0,32},{16,48},{32,64},{48,80},{64,96},{80,112},{96,128},{112,144}... | collective-permute-start | bytes 98312 | tf_op jit(solution)/shard_map/ppermute | solution.py:18
  118.3 7.9 %collective-permute-start.6 = (bf16[2,16,256]{2,0,1:T(2,128)(2,1)S(1)}, bf16[2,16,256]{2,0,1:T(2,128)(2,1)S(1)}, u32[]{:S(2)}, u32[]{:S(2)}) collective-permute-start(bf16[2,16,256]{2,0,1:T(2,128)(2,1)S(1)} %slice.149), channel_id=1, source_target_pairs={{0,16},{16,32},{32,48},{48,64},{64,80},{80,96},{96,112},{112,128},... | collective-permute-start | bytes 49160 | tf_op jit(solution)/shard_map/ppermute | solution.py:18
  132.7 12.1 %all-to-all-start.5 = ((bf16[16,16,256]{2,1,0:T(8,128)(2,1)}), bf16[16,16,256]{2,1,0:T(8,128)(2,1)S(1)}, u32[]{:S(2)}, u32[]{:S(2)}) async-start(bf16[16,16,256]{2,1,0:T(8,128)(2,1)} %bitcast.22), calls=%async_computation.5 | async-start | bytes 262144 | tf_op jit(solution)/shard_map/all_to_all | solution.py:132

commit v9 on v8

--- a/solution.py
+++ b/solution.py
@@ -32,6 +32,10 @@
     )(value, wanted)
 
 
+def once(there, value):
+    return jnp.where(there == there, value, jnp.zeros_like(value))
+
+
 def halves(value, parts):
     out = []
     for _ in range(parts):
@@ -52,10 +56,6 @@
     q_part = q_rows // tensors
     core, chip = lax.axis_index("core"), lax.axis_index("chip")
 
-    other = lax.ppermute(neighbours, "core", [(0, 1), (1, 0)])
-    lists = jnp.concatenate([neighbours, other], axis=0)
-    lists = jnp.where(core == 0, lists, lists[::-1])
-
     def project(rows):
         part = jnp.dot(rows, out_weight, preferred_element_type=f32).astype(bf16)
         return part.reshape(rows.shape[0], members, feats).transpose(1, 0, 2)
@@ -73,7 +73,12 @@
     reach = 1
     while reach < WINDOW:
         window = jnp.concatenate([window, shift_chips(window, -reach)], axis=0)
+        if reach == 1:
+            mine = once(window[-1, 0, 0], neighbours)
+            other = lax.ppermute(mine, "core", [(0, 1), (1, 0)])
         reach *= 2
+    lists = jnp.concatenate([neighbours, other], axis=0)
+    lists = jnp.where(core == 0, lists, lists[::-1])
     spots = (lists - CORES * chip) % (CORES * lax.axis_size("chip"))
     cand = window[spots].reshape(CORES, slots, feats)
 

time: 150 us -> 152 us (1.013)
  starting transfers between devices: 73.3 us -> 69.8 us
  waiting for transfers between devices: 37.6 us -> 40.3 us
    all_to_all x1, starting transfers between devices: 10.1 us -> 7.69 us  [on_device(): lax.all_to_all(sums.reshape(members, q_part + 8, slots), MEMBERS, 0, 0)]
    ppermute x6, starting transfers between devices: 29.5 us -> 27.1 us  [shift_chips(): lax.ppermute(value, 'chip', [(i, (i + by) % chips) for i in range(chips)])]
  transfers between devices with their start and end apart: 12 -> 12, of which waited for: 9 -> 10; matrix products, arithmetic and copies ran while one was open for 9% -> 9% of each run, Pallas kernels for 1% -> 1%
where the time goes in v9:
time: 152 us; the launch traced here: 150 us
  starting transfers between devices  69.8 us (46%)
  waiting for transfers between devices  40.3 us (27%)
  matrix products  15 us (10%)
  blocking collectives  12.1 us (8%)
  local copies, waits for them, and re-layouts  6.62 us (4%)
  other arithmetic  2.42 us (2%)
  between operations  2.26 us (1%)
    ppermute x6, starting transfers between devices, shift_chips(): lax.ppermute(value, 'chip', [(i, (i + by) % chips) for i in range(chips)])  27.1 us
    all_to_all x2, starting transfers between devices, reduce_over_tensor(): got = lax.all_to_all(part, MEMBERS, 0, 0)  22.2 us
    ppermute x6, waiting for transfers between devices, shift_chips(): lax.ppermute(value, 'chip', [(i, (i + by) % chips) for i in range(chips)])  18.8 us
    all_to_all x1, blocking collectives, on_device(): lax.all_to_all(jnp.broadcast_to(told[None], (members,) + told.shape), MEM...  12.1 us
    all_to_all x2, starting transfers between devices, gather_features(): lax.all_to_all(part.reshape((members,) + part.shape[2:]), MEMBERS, 0, 0)  9.41 us
    all_to_all x2, waiting for transfers between devices, gather_features(): lax.all_to_all(part.reshape((members,) + part.shape[2:]), MEMBERS, 0, 0)  9.13 us
    dot_general x2, matrix products, unproject(): jnp.einsum('mrf,hmf->rh', part, weight, preferred_element_type=f32)  8.36 us
    all_to_all x1, waiting for transfers between devices, on_device(): lax.all_to_all(sums.reshape(members, q_part + 8, slots), MEMBERS, 0, 0)  8.2 us
  transfers between devices with their start and end apart: 12, of which 10 were waited for; matrix products, arithmetic and copies ran while one was open for 9% of the time, Pallas kernels for 1%

profile of v9, /device:TPU:1, one launch (start us, length us, event | category | flops | bytes accessed | tf_op | source)
XLA Modules:
  0.0 149.7 jit_solution(17061677726223474435)
XLA Ops:
  0.6 2.9 %convolution_convert_fusion.1 = bf16[16,4096]{1,0:T(8,128)(2,1)S(1)} fusion(bf16[16,512]{1,0:T(8,128)(2,1)} %param.6, bf16[512,4096]{1,0:T(8,128)(2,1)} %param.7), kind=kOutput, calls=%fused_computation.2 | convolution fusion | flops 67174400 | bytes 4341760 | tf_op jit(solution)/shard_map/dot_general | solution.py:60
  3.5 0.7 copy.70
  4.2 17.5 %all-to-all-start.1 = ((bf16[16,16,256]{2,1,0:T(8,128)(2,1)}), bf16[16,16,256]{2,1,0:T(8,128)(2,1)S(1)}, u32[]{:S(2)}, u32[]{:S(2)}) async-start(bf16[16,16,256]{2,1,0:T(8,128)(2,1)} %bitcast.82), calls=%async_computation.1 | async-start | bytes 262144 | tf_op jit(solution)/shard_map/all_to_all | solution.py:64
  21.7 2.9 %convolution_convert_fusion = bf16[128,4096]{1,0:T(8,128)(2,1)S(1)} fusion(bf16[128,512]{1,0:T(8,128)(2,1)S(1)} %copy-done, bf16[512,4096]{1,0:T(8,128)(2,1)} %param.7), kind=kOutput, calls=%fused_computation.1 | convolution fusion | flops 537395200 | bytes 5373952 | tf_op jit(solution)/shard_map/dot_general | solution.py:60
  24.7 1.1 copy.69
  25.8 3.3 %all-to-all-done.1 = bf16[16,16,256]{2,1,0:T(8,128)(2,1)S(1)} async-done(((bf16[16,16,256]{2,1,0:T(8,128)(2,1)}), bf16[16,16,256]{2,1,0:T(8,128)(2,1)S(1)}, u32[]{:S(2)}, u32[]{:S(2)}) %all-to-all-start.1) | async-done | bytes 131104 | tf_op jit(solution)/shard_map/all_to_all | solution.py:64
  29.1 4.7 %all-to-all-start = ((bf16[16,128,256]{2,1,0:T(8,128)(2,1)}), bf16[16,128,256]{2,1,0:T(8,128)(2,1)S(1)}, u32[]{:S(2)}, u32[]{:S(2)}) async-start(bf16[16,128,256]{2,1,0:T(8,128)(2,1)} %bitcast.80), calls=%async_computation | async-start | bytes 2097152 | tf_op jit(solution)/shard_map/all_to_all | solution.py:64
  33.8 11.2 %collective-permute-start = (bf16[2,16,256]{2,1,0:T(8,128)(2,1)S(1)}, bf16[2,16,256]{2,1,0:T(8,128)(2,1)S(1)}, u32[]{:S(2)}, u32[]{:S(2)}) collective-permute-start(bf16[2,16,256]{2,1,0:T(8,128)(2,1)S(1)} %bitcast_reduce_fusion.1), channel_id=1, source_target_pairs={{0,1008},{16,0},{32,16},{48,32},{64,48},{80,64},{96,80},{112,96},{... | collective-permute-start | bytes 49160 | tf_op jit(solution)/shard_map/ppermute | solution.py:18
  45.2 0.8 collective-permute-done
  45.9 3.8 %collective-permute-start.1 = (bf16[4,16,256]{2,1,0:T(8,128)(2,1)S(1)}, bf16[4,16,256]{2,1,0:T(8,128)(2,1)S(1)}, u32[]{:S(2)}, u32[]{:S(2)}) collective-permute-start(bf16[4,16,256]{2,1,0:T(8,128)(2,1)S(1)} %pad_maximum_fusion.2), channel_id=1, source_target_pairs={{0,992},{16,1008},{32,0},{48,16},{64,32},{80,48},{96,64},{112,80},... | collective-permute-start | bytes 98312 | tf_op jit(solution)/shard_map/ppermute | solution.py:18
  49.7 0.5 slice.85
  51.5 3.3 %collective-permute-start.3 = (s32[1,8]{1,0:T(1,128)S(1)}, s32[1,8]{1,0:T(1,128)S(1)}, u32[]{:S(2)}, u32[]{:S(2)}) collective-permute-start(s32[1,8]{1,0:T(1,128)S(1)} %broadcast_select_fusion), channel_id=1, source_target_pairs={{0,8},{8,0},{1,9},{9,1},{2,10},{10,2},{3,11},{11,3},{4,12},{12,4},... | collective-permute-start | bytes 104 | tf_op jit(solution)/shard_map/ppermute | solution.py:78
  54.9 0.8 collective-permute-done.3
  55.7 0.1 reshape.108
  55.8 3.4 %collective-permute-start.2 = (bf16[8,16,256]{2,1,0:T(8,128)(2,1)S(1)}, bf16[8,16,256]{2,1,0:T(8,128)(2,1)S(1)}, u32[]{:S(2)}, u32[]{:S(2)}) collective-permute-start(bf16[8,16,256]{2,1,0:T(8,128)(2,1)S(1)} %pad_maximum_fusion.1), channel_id=1, source_target_pairs={{0,960},{16,976},{32,992},{48,1008},{64,0},{80,16},{96,32},{112,48... | collective-permute-start | bytes 196616 | tf_op jit(solution)/shard_map/ppermute | solution.py:18
  59.2 7.8 %collective-permute-done.2 = bf16[8,16,256]{2,1,0:T(8,128)(2,1)S(1)} collective-permute-done((bf16[8,16,256]{2,1,0:T(8,128)(2,1)S(1)}, bf16[8,16,256]{2,1,0:T(8,128)(2,1)S(1)}, u32[]{:S(2)}, u32[]{:S(2)}) %collective-permute-start.2) | collective-permute-done | bytes 65568 | tf_op jit(solution)/shard_map/ppermute | solution.py:18
  67.0 0.6 gather_fusion
  67.6 0.1 multiply_reduce_fusion
  67.8 0.1 bitcast_reduce_fusion
  67.9 0.1 fusion.20
  68.0 0.2 fusion.39
  68.3 0.8 maximum_maximum_fusion
  69.1 7.7 %all-to-all-start.2 = ((f32[16,24,128]{2,1,0:T(8,128)}), f32[16,24,128]{2,1,0:T(8,128)S(1)}, u32[]{:S(2)}, u32[]{:S(2)}) async-start(f32[16,24,128]{2,1,0:T(8,128)} %maximum_maximum_fusion), calls=%async_computation.2 | async-start | bytes 393216 | tf_op jit(solution)/shard_map/all_to_all | solution.py:92
  76.8 8.2 %all-to-all-done.2 = f32[16,24,128]{2,1,0:T(8,128)S(1)} async-done(((f32[16,24,128]{2,1,0:T(8,128)}), f32[16,24,128]{2,1,0:T(8,128)S(1)}, u32[]{:S(2)}, u32[]{:S(2)}) %all-to-all-start.2) | async-done | bytes 196640 | tf_op jit(solution)/shard_map/all_to_all | solution.py:92
  85.1 0.2 select_reduce_fusion
  85.3 0.2 fusion.27
  85.5 0.1 concatenate.38
  85.7 12.1 %all_to_all.30 = bf16[16,24,128]{2,1,0:T(8,128)(2,1)S(1)} all-to-all(bf16[16,24,128]{2,1,0:T(8,128)(2,1)S(1)} %broadcast_in_dim.21), channel_id=1, replica_groups=mesh['chip'=64,'core'=2,'tensor'=8] {'core','tensor'}, dimensions={0} | all-to-all | bytes 196608 | tf_op jit(solution)/shard_map/all_to_all | solution.py:113
  97.9 0.2 fusion.10
  98.2 0.3 convolution_bitcast_fusion
  98.5 1.9 %collective-permute-start.4 = (bf16[8,16,256]{2,0,1:T(8,128)(2,1)S(1)}, bf16[8,16,256]{2,0,1:T(8,128)(2,1)S(1)}, u32[]{:S(2)}, u32[]{:S(2)}) collective-permute-start(bf16[8,16,256]{2,0,1:T(8,128)(2,1)S(1)} %slice.152), channel_id=1, source_target_pairs={{0,64},{16,80},{32,96},{48,112},{64,128},{80,144},{96,160},{112,17... | collective-permute-start | bytes 196616 | tf_op jit(solution)/shard_map/ppermute | solution.py:18
  100.5 0.2 fusion.9
  100.7 1.1 broadcast_in_dim.22
  101.8 4.6 %all-to-all-start.4 = ((bf16[16,128,256]{2,1,0:T(8,128)(2,1)}), bf16[16,128,256]{2,1,0:T(8,128)(2,1)S(1)}, u32[]{:S(2)}, u32[]{:S(2)}) async-start(bf16[16,128,256]{2,1,0:T(8,128)(2,1)} %bitcast.17), calls=%async_computation.4 | async-start | bytes 2097152 | tf_op jit(solution)/shard_map/all_to_all | solution.py:137
  106.4 3.2 %collective-permute-done.4 = bf16[8,16,256]{2,0,1:T(8,128)(2,1)S(1)} collective-permute-done((bf16[8,16,256]{2,0,1:T(8,128)(2,1)S(1)}, bf16[8,16,256]{2,0,1:T(8,128)(2,1)S(1)}, u32[]{:S(2)}, u32[]{:S(2)}) %collective-permute-start.4) | collective-permute-done | bytes 65568 | tf_op jit(solution)/shard_map/ppermute | solution.py:18
  109.6 1.9 %collective-permute-start.5 = (bf16[4,16,256]{2,0,1:T(4,128)(2,1)S(1)}, bf16[4,16,256]{2,0,1:T(4,128)(2,1)S(1)}, u32[]{:S(2)}, u32[]{:S(2)}) collective-permute-start(bf16[4,16,256]{2,0,1:T(4,128)(2,1)S(1)} %slice.153), channel_id=1, source_target_pairs={{0,32},{16,48},{32,64},{48,80},{64,96},{80,112},{96,128},{112,144}... | collective-permute-start | bytes 98312 | tf_op jit(solution)/shard_map/ppermute | solution.py:18
  111.5 0.6 fusion.25.value_ref
  112.1 6.8 %collective-permute-done.5 = bf16[4,16,256]{2,0,1:T(4,128)(2,1)S(1)} collective-permute-done((bf16[4,16,256]{2,0,1:T(4,128)(2,1)S(1)}, bf16[4,16,256]{2,0,1:T(4,128)(2,1)S(1)}, u32[]{:S(2)}, u32[]{:S(2)}) %collective-permute-start.5) | collective-permute-done | bytes 32800 | tf_op jit(solution)/shard_map/ppermute | solution.py:18
  118.9 4.9 %collective-permute-start.6 = (bf16[2,16,256]{2,0,1:T(2,128)(2,1)S(1)}, bf16[2,16,256]{2,0,1:T(2,128)(2,1)S(1)}, u32[]{:S(2)}, u32[]{:S(2)}) collective-permute-start(bf16[2,16,256]{2,0,1:T(2,128)(2,1)S(1)} %slice.154), channel_id=1, source_target_pairs={{0,16},{16,32},{32,48},{48,64},{64,80},{80,96},{96,112},{112,128},... | collective-permute-start | bytes 49160 | tf_op jit(solution)/shard_map/ppermute | solution.py:18
  123.9 1.3 shard_map.76
  125.1 1.3 reshape.104
  126.4 0.3 collective-permute-done.6
  126.8 6.2 %all-to-all-done.4 = bf16[16,128,256]{2,1,0:T(8,128)(2,1)S(1)} async-done(((bf16[16,128,256]{2,1,0:T(8,128)(2,1)}), bf16[16,128,256]{2,1,0:T(8,128)(2,1)S(1)}, u32[]{:S(2)}, u32[]{:S(2)}) %all-to-all-start.4) | async-done | bytes 1048608 | tf_op jit(solution)/shard_map/all_to_all | solution.py:137
  133.0 0.6 broadcast_in_dim.23
  133.6 4.8 %all-to-all-start.5 = ((bf16[16,16,256]{2,1,0:T(8,128)(2,1)}), bf16[16,16,256]{2,1,0:T(8,128)(2,1)S(1)}, u32[]{:S(2)}, u32[]{:S(2)}) async-start(bf16[16,16,256]{2,1,0:T(8,128)(2,1)} %bitcast.23), calls=%async_computation.5 | async-start | bytes 262144 | tf_op jit(solution)/shard_map/all_to_all | solution.py:137
  138.5 4.4 %fusion.11 = bf16[128,512]{1,0:T(8,128)(2,1)} fusion(bf16[16,128,256]{2,1,0:T(8,128)(2,1)S(1)} %all-to-all-done.4, bf16[64,16,8,256]{3,2,1,0:T(8,128)(2,1)} %bitcast.83), kind=kOutput, calls=%fused_computation.15 | convolution fusion | flops 536936448 | bytes 5373952 | tf_op jit(solution)/shard_map/mrf,hmf->rh/dot_general | solution.py:141
  142.8 2.9 %all-to-all-done.5 = bf16[16,16,256]{2,1,0:T(8,128)(2,1)S(1)} async-done(((bf16[16,16,256]{2,1,0:T(8,128)(2,1)}), bf16[16,16,256]{2,1,0:T(8,128)(2,1)S(1)}, u32[]{:S(2)}, u32[]{:S(2)}) %all-to-all-start.5) | async-done | bytes 131104 | tf_op jit(solution)/shard_map/all_to_all | solution.py:137
  145.8 4.0 %fusion.17 = bf16[16,512]{1,0:T(8,128)(2,1)} fusion(bf16[16,16,256]{2,1,0:T(8,128)(2,1)S(1)} %all-to-all-done.5, bf16[64,16,8,256]{3,2,1,0:T(8,128)(2,1)} %bitcast.84), kind=kOutput, calls=%fused_computation.17 | convolution fusion | flops 67117056 | bytes 4341760 | tf_op jit(solution)/shard_map/mrf,hmf->rh/dot_general | solution.py:141
  (51 shorter events, 0.9 us)
Async XLA Ops:
  0.6 21.1 %copy-start = (bf16[128,512]{1,0:T(8,128)(2,1)S(1)}, bf16[128,512]{1,0:T(8,128)(2,1)}, u32[]{:S(2)}) copy-start(bf16[128,512]{1,0:T(8,128)(2,1)} %param.5) | copy-start | bytes 393220
  4.2 24.9 %all-to-all-start.1 = ((bf16[16,16,256]{2,1,0:T(8,128)(2,1)}), bf16[16,16,256]{2,1,0:T(8,128)(2,1)S(1)}, u32[]{:S(2)}, u32[]{:S(2)}) async-start(bf16[16,16,256]{2,1,0:T(8,128)(2,1)} %bitcast.82), calls=%async_computation.1 | async-start | bytes 262144 | tf_op jit(solution)/shard_map/all_to_all | solution.py:64
  21.7 29.8 %copy-start.2 = (s32[1,8]{1,0:T(1,128)S(1)}, s32[1,8]{1,0:T(1,128)}, u32[]{:S(2)}) copy-start(s32[1,8]{1,0:T(1,128)} %param.8) | copy-start | bytes 100
  24.7 52.1 %copy-start.3 = (s32[128]{0:T(128)S(1)}, s32[128]{0:T(128)}, u32[]{:S(2)}) copy-start(s32[128]{0:T(128)} %param.9) | copy-start | bytes 1540
  29.1 38.7 %all-to-all-start = ((bf16[16,128,256]{2,1,0:T(8,128)(2,1)}), bf16[16,128,256]{2,1,0:T(8,128)(2,1)S(1)}, u32[]{:S(2)}, u32[]{:S(2)}) async-start(bf16[16,128,256]{2,1,0:T(8,128)(2,1)} %bitcast.80), calls=%async_computation | async-start | bytes 2097152 | tf_op jit(solution)/shard_map/all_to_all | solution.py:64
  33.8 12.1 %collective-permute-start = (bf16[2,16,256]{2,1,0:T(8,128)(2,1)S(1)}, bf16[2,16,256]{2,1,0:T(8,128)(2,1)S(1)}, u32[]{:S(2)}, u32[]{:S(2)}) collective-permute-start(bf16[2,16,256]{2,1,0:T(8,128)(2,1)S(1)} %bitcast_reduce_fusion.1), channel_id=1, source_target_pairs={{0,1008},{16,0},{32,16},{48,32},{64,48},{80,64},{96,80},{112,96},{... | collective-permute-start | bytes 49160 | tf_op jit(solution)/shard_map/ppermute | solution.py:18
  45.9 9.9 %collective-permute-start.1 = (bf16[4,16,256]{2,1,0:T(8,128)(2,1)S(1)}, bf16[4,16,256]{2,1,0:T(8,128)(2,1)S(1)}, u32[]{:S(2)}, u32[]{:S(2)}) collective-permute-start(bf16[4,16,256]{2,1,0:T(8,128)(2,1)S(1)} %pad_maximum_fusion.2), channel_id=1, source_target_pairs={{0,992},{16,1008},{32,0},{48,16},{64,32},{80,48},{96,64},{112,80},... | collective-permute-start | bytes 98312 | tf_op jit(solution)/shard_map/ppermute | solution.py:18
  51.5 4.2 %collective-permute-start.3 = (s32[1,8]{1,0:T(1,128)S(1)}, s32[1,8]{1,0:T(1,128)S(1)}, u32[]{:S(2)}, u32[]{:S(2)}) collective-permute-start(s32[1,8]{1,0:T(1,128)S(1)} %broadcast_select_fusion), channel_id=1, source_target_pairs={{0,8},{8,0},{1,9},{9,1},{2,10},{10,2},{3,11},{11,3},{4,12},{12,4},... | collective-permute-start | bytes 104 | tf_op jit(solution)/shard_map/ppermute | solution.py:78
  55.8 11.1 %collective-permute-start.2 = (bf16[8,16,256]{2,1,0:T(8,128)(2,1)S(1)}, bf16[8,16,256]{2,1,0:T(8,128)(2,1)S(1)}, u32[]{:S(2)}, u32[]{:S(2)}) collective-permute-start(bf16[8,16,256]{2,1,0:T(8,128)(2,1)S(1)} %pad_maximum_fusion.1), channel_id=1, source_target_pairs={{0,960},{16,976},{32,992},{48,1008},{64,0},{80,16},{96,32},{112,48... | collective-permute-start | bytes 196616 | tf_op jit(solution)/shard_map/ppermute | solution.py:18
  69.1 16.0 %all-to-all-start.2 = ((f32[16,24,128]{2,1,0:T(8,128)}), f32[16,24,128]{2,1,0:T(8,128)S(1)}, u32[]{:S(2)}, u32[]{:S(2)}) async-start(f32[16,24,128]{2,1,0:T(8,128)} %maximum_maximum_fusion), calls=%async_computation.2 | async-start | bytes 393216 | tf_op jit(solution)/shard_map/all_to_all | solution.py:92
  97.8 26.0 %copy-start.1 = (bf16[16,24,128]{2,1,0:T(8,128)(2,1)}, bf16[16,24,128]{2,1,0:T(8,128)(2,1)S(1)}, u32[]{:S(2)}) copy-start(bf16[16,24,128]{2,1,0:T(8,128)(2,1)S(1)} %all_to_all.30) | copy-start | bytes 294916
  98.5 11.0 %collective-permute-start.4 = (bf16[8,16,256]{2,0,1:T(8,128)(2,1)S(1)}, bf16[8,16,256]{2,0,1:T(8,128)(2,1)S(1)}, u32[]{:S(2)}, u32[]{:S(2)}) collective-permute-start(bf16[8,16,256]{2,0,1:T(8,128)(2,1)S(1)} %slice.152), channel_id=1, source_target_pairs={{0,64},{16,80},{32,96},{48,112},{64,128},{80,144},{96,160},{112,17... | collective-permute-start | bytes 196616 | tf_op jit(solution)/shard_map/ppermute | solution.py:18
  101.8 31.2 %all-to-all-start.4 = ((bf16[16,128,256]{2,1,0:T(8,128)(2,1)}), bf16[16,128,256]{2,1,0:T(8,128)(2,1)S(1)}, u32[]{:S(2)}, u32[]{:S(2)}) async-start(bf16[16,128,256]{2,1,0:T(8,128)(2,1)} %bitcast.17), calls=%async_computation.4 | async-start | bytes 2097152 | tf_op jit(solution)/shard_map/all_to_all | solution.py:137
  109.6 9.3 %collective-permute-start.5 = (bf16[4,16,256]{2,0,1:T(4,128)(2,1)S(1)}, bf16[4,16,256]{2,0,1:T(4,128)(2,1)S(1)}, u32[]{:S(2)}, u32[]{:S(2)}) collective-permute-start(bf16[4,16,256]{2,0,1:T(4,128)(2,1)S(1)} %slice.153), channel_id=1, source_target_pairs={{0,32},{16,48},{32,64},{48,80},{64,96},{80,112},{96,128},{112,144}... | collective-permute-start | bytes 98312 | tf_op jit(solution)/shard_map/ppermute | solution.py:18
  118.9 7.8 %collective-permute-start.6 = (bf16[2,16,256]{2,0,1:T(2,128)(2,1)S(1)}, bf16[2,16,256]{2,0,1:T(2,128)(2,1)S(1)}, u32[]{:S(2)}, u32[]{:S(2)}) collective-permute-start(bf16[2,16,256]{2,0,1:T(2,128)(2,1)S(1)} %slice.154), channel_id=1, source_target_pairs={{0,16},{16,32},{32,48},{48,64},{64,80},{80,96},{96,112},{112,128},... | collective-permute-start | bytes 49160 | tf_op jit(solution)/shard_map/ppermute | solution.py:18
  133.6 12.1 %all-to-all-start.5 = ((bf16[16,16,256]{2,1,0:T(8,128)(2,1)}), bf16[16,16,256]{2,1,0:T(8,128)(2,1)S(1)}, u32[]{:S(2)}, u32[]{:S(2)}) async-start(bf16[16,16,256]{2,1,0:T(8,128)(2,1)} %bitcast.23), calls=%async_computation.5 | async-start | bytes 262144 | tf_op jit(solution)/shard_map/all_to_all | solution.py:137

commit v10 on v8

--- a/solution.py
+++ b/solution.py
@@ -118,26 +118,29 @@
     dq = (dq - q_inner * q_pre.astype(f32)).astype(bf16)
     dc = jnp.einsum("kqc,kqf->kcf", coef, q_pre, preferred_element_type=f32)
     dc = (dc - c_inner * cand.astype(f32)).astype(bf16)
-    match = (jnp.arange(WINDOW * CORES, dtype=jnp.int32)[:, None, None] == spots[None]).astype(bf16)
+    far = spots // CORES
+    slot = (far % 2 * 4 + far // 2 % 2 * 2 + far // 4) * CORES + spots % CORES
+    match = (jnp.arange(WINDOW * CORES, dtype=jnp.int32)[:, None, None] == slot[None]).astype(bf16)
     dwin = jnp.einsum("wks,kspf->wpf", match, dc.reshape(CORES, listed, p_rows, feats), preferred_element_type=f32)
 
-    while reach > 1:
-        reach //= 2
-        away = shift_chips(dwin[CORES * reach :].astype(bf16), reach)
-        dwin = dwin[: CORES * reach] + away.astype(f32)
+    reach = 1
+    while reach < WINDOW:
+        half = dwin.shape[0] // 2
+        dwin = dwin[:half] + shift_chips(dwin[half:].astype(bf16), reach).astype(f32)
+        reach *= 2
     dp = dwin.astype(bf16)
 
-    def gather_features(part):
+    def copies(part):
         part = jnp.broadcast_to(part[:, None], (CORES, tensors) + part.shape[1:])
-        return lax.all_to_all(part.reshape((members,) + part.shape[2:]), MEMBERS, 0, 0)
+        return part.reshape((members,) + part.shape[2:])
 
     def unproject(part):
         weight = out_weight.reshape(out_weight.shape[0], members, feats)
         return jnp.einsum("mrf,hmf->rh", part, weight, preferred_element_type=f32).astype(bf16)
 
-    q_all = gather_features(dq)
-    q_all, dp = lax.optimization_barrier((q_all, dp))
-    p_grad = unproject(gather_features(dp))
+    q_all = lax.all_to_all(copies(dq), MEMBERS, 0, 0)
+    q_all, dp = lax.optimization_barrier((q_all, copies(dp)))
+    p_grad = unproject(lax.all_to_all(dp, MEMBERS, 0, 0))
     return unproject(q_all), p_grad, losses
 
 

time: 150 us -> 154 us (1.027)
  waiting for transfers between devices: 37.6 us -> 41.8 us
    ppermute x6, waiting for transfers between devices: 17.4 us -> 22.1 us  [shift_chips(): lax.ppermute(value, 'chip', [(i, (i + by) % chips) for i in range(chips)])]
  transfers between devices with their start and end apart: 12 -> 12, of which waited for: 9 -> 11; matrix products, arithmetic and copies ran while one was open for 9% -> 8% of each run, Pallas kernels for 1% -> 1%
where the time goes in v10:
time: 154 us; the launch traced here: 153 us
  starting transfers between devices  73.5 us (48%)
  waiting for transfers between devices  41.8 us (27%)
  matrix products  15.1 us (10%)
  blocking collectives  12.1 us (8%)
  local copies, waits for them, and re-layouts  6.1 us (4%)
  other arithmetic  2.46 us (2%)
    ppermute x6, starting transfers between devices, shift_chips(): lax.ppermute(value, 'chip', [(i, (i + by) % chips) for i in range(chips)])  28 us
    all_to_all x2, starting transfers between devices, reduce_over_tensor(): got = lax.all_to_all(part, MEMBERS, 0, 0)  22.2 us
    ppermute x6, waiting for transfers between devices, shift_chips(): lax.ppermute(value, 'chip', [(i, (i + by) % chips) for i in range(chips)])  22.1 us
    all_to_all x1, blocking collectives, on_device(): lax.all_to_all(jnp.broadcast_to(told[None], (members,) + told.shape), MEM...  12.1 us
    all_to_all x1, starting transfers between devices, on_device(): lax.all_to_all(sums.reshape(members, q_part + 8, slots), MEMBERS, 0, 0)  11.1 us
    dot_general x2, matrix products, unproject(): jnp.einsum('mrf,hmf->rh', part, weight, preferred_element_type=f32)  8.37 us
    all_to_all x1, waiting for transfers between devices, on_device(): lax.all_to_all(sums.reshape(members, q_part + 8, slots), MEMBERS, 0, 0)  8.2 us
    dot_general x2, matrix products, project(): part = jnp.dot(rows, out_weight, preferred_element_type=f32).astype(bf16)  5.81 us
  transfers between devices with their start and end apart: 12, of which 11 were waited for; matrix products, arithmetic and copies ran while one was open for 8% of the time, Pallas kernels for 1%

profile of v10, /device:TPU:1, one launch (start us, length us, event | category | flops | bytes accessed | tf_op | source)
XLA Modules:
  0.0 153.2 jit_solution(918923434209042559)
XLA Ops:
  0.6 2.9 %convolution_convert_fusion.1 = bf16[16,4096]{1,0:T(8,128)(2,1)S(1)} fusion(bf16[16,512]{1,0:T(8,128)(2,1)} %param.6, bf16[512,4096]{1,0:T(8,128)(2,1)} %param.7), kind=kOutput, calls=%fused_computation.2 | convolution fusion | flops 67174400 | bytes 4341760 | tf_op jit(solution)/shard_map/dot_general | solution.py:60
  3.5 0.7 copy.92
  4.2 17.5 %all-to-all-start.1 = ((bf16[16,16,256]{2,1,0:T(8,128)(2,1)}), bf16[16,16,256]{2,1,0:T(8,128)(2,1)S(1)}, u32[]{:S(2)}, u32[]{:S(2)}) async-start(bf16[16,16,256]{2,1,0:T(8,128)(2,1)} %bitcast.81), calls=%async_computation.1 | async-start | bytes 262144 | tf_op jit(solution)/shard_map/all_to_all | solution.py:64
  21.7 2.9 %convolution_convert_fusion = bf16[128,4096]{1,0:T(8,128)(2,1)S(1)} fusion(bf16[128,512]{1,0:T(8,128)(2,1)S(1)} %copy-done, bf16[512,4096]{1,0:T(8,128)(2,1)} %param.7), kind=kOutput, calls=%fused_computation.1 | convolution fusion | flops 537395200 | bytes 5373952 | tf_op jit(solution)/shard_map/dot_general | solution.py:60
  24.7 1.1 copy.91
  25.8 3.3 %all-to-all-done.1 = bf16[16,16,256]{2,1,0:T(8,128)(2,1)S(1)} async-done(((bf16[16,16,256]{2,1,0:T(8,128)(2,1)}), bf16[16,16,256]{2,1,0:T(8,128)(2,1)S(1)}, u32[]{:S(2)}, u32[]{:S(2)}) %all-to-all-start.1) | async-done | bytes 131104 | tf_op jit(solution)/shard_map/all_to_all | solution.py:64
  29.1 4.7 %all-to-all-start = ((bf16[16,128,256]{2,1,0:T(8,128)(2,1)}), bf16[16,128,256]{2,1,0:T(8,128)(2,1)S(1)}, u32[]{:S(2)}, u32[]{:S(2)}) async-start(bf16[16,128,256]{2,1,0:T(8,128)(2,1)} %bitcast.79), calls=%async_computation | async-start | bytes 2097152 | tf_op jit(solution)/shard_map/all_to_all | solution.py:64
  33.8 2.1 %collective-permute-start.3 = (s32[1,8]{1,0:T(1,128)S(1)}, s32[1,8]{1,0:T(1,128)S(1)}, u32[]{:S(2)}, u32[]{:S(2)}) collective-permute-start(s32[1,8]{1,0:T(1,128)S(1)} %copy-done.2), channel_id=1, source_target_pairs={{0,8},{8,0},{1,9},{9,1},{2,10},{10,2},{3,11},{11,3},{4,12},{12,4},... | collective-permute-start | bytes 104 | tf_op jit(solution)/shard_map/ppermute | solution.py:55
  36.0 0.8 collective-permute-done.3
  36.9 11.2 %collective-permute-start = (bf16[2,16,256]{2,1,0:T(8,128)(2,1)S(1)}, bf16[2,16,256]{2,1,0:T(8,128)(2,1)S(1)}, u32[]{:S(2)}, u32[]{:S(2)}) collective-permute-start(bf16[2,16,256]{2,1,0:T(8,128)(2,1)S(1)} %bitcast_reduce_fusion.1), channel_id=1, source_target_pairs={{0,1008},{16,0},{32,16},{48,32},{64,48},{80,64},{96,80},{112,96},{... | collective-permute-start | bytes 49160 | tf_op jit(solution)/shard_map/ppermute | solution.py:18
  48.2 0.8 collective-permute-done
  49.0 3.9 %collective-permute-start.1 = (bf16[4,16,256]{2,1,0:T(8,128)(2,1)S(1)}, bf16[4,16,256]{2,1,0:T(8,128)(2,1)S(1)}, u32[]{:S(2)}, u32[]{:S(2)}) collective-permute-start(bf16[4,16,256]{2,1,0:T(8,128)(2,1)S(1)} %pad_maximum_fusion.2), channel_id=1, source_target_pairs={{0,992},{16,1008},{32,0},{48,16},{64,32},{80,48},{96,64},{112,80},... | collective-permute-start | bytes 98312 | tf_op jit(solution)/shard_map/ppermute | solution.py:18
  52.9 0.1 reshape.107
  53.0 1.5 %collective-permute-done.1 = bf16[4,16,256]{2,1,0:T(8,128)(2,1)S(1)} collective-permute-done((bf16[4,16,256]{2,1,0:T(8,128)(2,1)S(1)}, bf16[4,16,256]{2,1,0:T(8,128)(2,1)S(1)}, u32[]{:S(2)}, u32[]{:S(2)}) %collective-permute-start.1) | collective-permute-done | bytes 32800 | tf_op jit(solution)/shard_map/ppermute | solution.py:18
  54.5 4.2 %collective-permute-start.2 = (bf16[8,16,256]{2,1,0:T(8,128)(2,1)S(1)}, bf16[8,16,256]{2,1,0:T(8,128)(2,1)S(1)}, u32[]{:S(2)}, u32[]{:S(2)}) collective-permute-start(bf16[8,16,256]{2,1,0:T(8,128)(2,1)S(1)} %pad_maximum_fusion.1), channel_id=1, source_target_pairs={{0,960},{16,976},{32,992},{48,1008},{64,0},{80,16},{96,32},{112,48... | collective-permute-start | bytes 196616 | tf_op jit(solution)/shard_map/ppermute | solution.py:18
  58.7 4.7 %collective-permute-done.2 = bf16[8,16,256]{2,1,0:T(8,128)(2,1)S(1)} collective-permute-done((bf16[8,16,256]{2,1,0:T(8,128)(2,1)S(1)}, bf16[8,16,256]{2,1,0:T(8,128)(2,1)S(1)}, u32[]{:S(2)}, u32[]{:S(2)}) %collective-permute-start.2) | collective-permute-done | bytes 65568 | tf_op jit(solution)/shard_map/ppermute | solution.py:18
  63.5 0.6 gather_fusion
  64.0 0.1 multiply_reduce_fusion
  64.2 0.1 bitcast_reduce_fusion
  64.4 0.1 fusion.20
  64.5 0.2 fusion.45
  64.8 0.8 maximum_maximum_fusion
  65.5 11.1 %all-to-all-start.2 = ((f32[16,24,128]{2,1,0:T(8,128)}), f32[16,24,128]{2,1,0:T(8,128)S(1)}, u32[]{:S(2)}, u32[]{:S(2)}) async-start(f32[16,24,128]{2,1,0:T(8,128)} %maximum_maximum_fusion), calls=%async_computation.2 | async-start | bytes 393216 | tf_op jit(solution)/shard_map/all_to_all | solution.py:87
  76.7 8.2 %all-to-all-done.2 = f32[16,24,128]{2,1,0:T(8,128)S(1)} async-done(((f32[16,24,128]{2,1,0:T(8,128)}), f32[16,24,128]{2,1,0:T(8,128)S(1)}, u32[]{:S(2)}, u32[]{:S(2)}) %all-to-all-start.2) | async-done | bytes 196640 | tf_op jit(solution)/shard_map/all_to_all | solution.py:87
  85.0 0.2 select_reduce_fusion
  85.2 0.2 fusion.27
  85.4 0.1 concatenate.38
  85.6 12.1 %all_to_all.30 = bf16[16,24,128]{2,1,0:T(8,128)(2,1)S(1)} all-to-all(bf16[16,24,128]{2,1,0:T(8,128)(2,1)S(1)} %broadcast_in_dim.21), channel_id=1, replica_groups=mesh['chip'=64,'core'=2,'tensor'=8] {'core','tensor'}, dimensions={0} | all-to-all | bytes 196608 | tf_op jit(solution)/shard_map/all_to_all | solution.py:108
  97.8 0.2 fusion.10
  98.1 0.3 convolution_bitcast_fusion
  98.4 4.8 %collective-permute-start.4 = (bf16[8,16,256]{2,1,0:T(8,128)(2,1)S(1)}, bf16[8,16,256]{2,1,0:T(8,128)(2,1)S(1)}, u32[]{:S(2)}, u32[]{:S(2)}) collective-permute-start(bf16[8,16,256]{2,1,0:T(8,128)(2,1)S(1)} %copy.90), channel_id=1, source_target_pairs={{0,16},{16,32},{32,48},{48,64},{64,80},{80,96},{96,112},{112,128},... | collective-permute-start | bytes 196616 | tf_op jit(solution)/shard_map/ppermute | solution.py:18
  103.3 0.2 fusion.9
  103.5 1.1 broadcast_in_dim.22
  104.6 4.9 %all-to-all-start.4 = ((bf16[16,128,256]{2,1,0:T(8,128)(2,1)}), bf16[16,128,256]{2,1,0:T(8,128)(2,1)S(1)}, u32[]{:S(2)}, u32[]{:S(2)}) async-start(bf16[16,128,256]{2,1,0:T(8,128)(2,1)} %bitcast.16), calls=%async_computation.4 | async-start | bytes 2097152 | tf_op jit(solution)/shard_map/all_to_all | solution.py:141
  109.5 2.6 %collective-permute-done.4 = bf16[8,16,256]{2,1,0:T(8,128)(2,1)S(1)} collective-permute-done((bf16[8,16,256]{2,1,0:T(8,128)(2,1)S(1)}, bf16[8,16,256]{2,1,0:T(8,128)(2,1)S(1)}, u32[]{:S(2)}, u32[]{:S(2)}) %collective-permute-start.4) | collective-permute-done | bytes 65568 | tf_op jit(solution)/shard_map/ppermute | solution.py:18
  112.1 1.9 %collective-permute-start.5 = (bf16[4,16,256]{2,1,0:T(8,128)(2,1)S(1)}, bf16[4,16,256]{2,1,0:T(8,128)(2,1)S(1)}, u32[]{:S(2)}, u32[]{:S(2)}) collective-permute-start(bf16[4,16,256]{2,1,0:T(8,128)(2,1)S(1)} %slice.145), channel_id=1, source_target_pairs={{0,32},{16,48},{32,64},{48,80},{64,96},{80,112},{96,128},{112,144}... | collective-permute-start | bytes 98312 | tf_op jit(solution)/shard_map/ppermute | solution.py:18
  114.1 0.6 fusion.25.value_ref
  114.7 6.5 %collective-permute-done.5 = bf16[4,16,256]{2,1,0:T(8,128)(2,1)S(1)} collective-permute-done((bf16[4,16,256]{2,1,0:T(8,128)(2,1)S(1)}, bf16[4,16,256]{2,1,0:T(8,128)(2,1)S(1)}, u32[]{:S(2)}, u32[]{:S(2)}) %collective-permute-start.5) | collective-permute-done | bytes 32800 | tf_op jit(solution)/shard_map/ppermute | solution.py:18
  121.1 1.9 %collective-permute-start.6 = (bf16[2,16,256]{2,1,0:T(8,128)(2,1)S(1)}, bf16[2,16,256]{2,1,0:T(8,128)(2,1)S(1)}, u32[]{:S(2)}, u32[]{:S(2)}) collective-permute-start(bf16[2,16,256]{2,1,0:T(8,128)(2,1)S(1)} %slice.146), channel_id=1, source_target_pairs={{0,64},{16,80},{32,96},{48,112},{64,128},{80,144},{96,160},{112,17... | collective-permute-start | bytes 49160 | tf_op jit(solution)/shard_map/ppermute | solution.py:18
  123.1 1.3 shard_map.76
  124.4 1.3 reshape.103
  125.6 6.0 %collective-permute-done.6 = bf16[2,16,256]{2,1,0:T(8,128)(2,1)S(1)} collective-permute-done((bf16[2,16,256]{2,1,0:T(8,128)(2,1)S(1)}, bf16[2,16,256]{2,1,0:T(8,128)(2,1)S(1)}, u32[]{:S(2)}, u32[]{:S(2)}) %collective-permute-start.6) | collective-permute-done | bytes 16416 | tf_op jit(solution)/shard_map/ppermute | solution.py:18
  131.7 4.4 %all-to-all-done.4 = bf16[16,128,256]{2,1,0:T(8,128)(2,1)S(1)} async-done(((bf16[16,128,256]{2,1,0:T(8,128)(2,1)}), bf16[16,128,256]{2,1,0:T(8,128)(2,1)S(1)}, u32[]{:S(2)}, u32[]{:S(2)}) %all-to-all-start.4) | async-done | bytes 1048608 | tf_op jit(solution)/shard_map/all_to_all | solution.py:141
  136.1 0.6 broadcast_in_dim.23
  136.7 5.2 %all-to-all-start.5 = ((bf16[16,16,256]{2,1,0:T(8,128)(2,1)}), bf16[16,16,256]{2,1,0:T(8,128)(2,1)S(1)}, u32[]{:S(2)}, u32[]{:S(2)}) async-start(bf16[16,16,256]{2,1,0:T(8,128)(2,1)} %bitcast.21), calls=%async_computation.5 | async-start | bytes 262144 | tf_op jit(solution)/shard_map/all_to_all | solution.py:143
  141.9 4.4 %fusion.11 = bf16[128,512]{1,0:T(8,128)(2,1)} fusion(bf16[16,128,256]{2,1,0:T(8,128)(2,1)S(1)} %all-to-all-done.4, bf16[64,16,8,256]{3,2,1,0:T(8,128)(2,1)} %bitcast.82), kind=kOutput, calls=%fused_computation.15 | convolution fusion | flops 536936448 | bytes 5373952 | tf_op jit(solution)/shard_map/mrf,hmf->rh/dot_general | solution.py:139
  146.3 2.9 %all-to-all-done.5 = bf16[16,16,256]{2,1,0:T(8,128)(2,1)S(1)} async-done(((bf16[16,16,256]{2,1,0:T(8,128)(2,1)}), bf16[16,16,256]{2,1,0:T(8,128)(2,1)S(1)}, u32[]{:S(2)}, u32[]{:S(2)}) %all-to-all-start.5) | async-done | bytes 131104 | tf_op jit(solution)/shard_map/all_to_all | solution.py:143
  149.2 4.0 %fusion.17 = bf16[16,512]{1,0:T(8,128)(2,1)} fusion(bf16[16,16,256]{2,1,0:T(8,128)(2,1)S(1)} %all-to-all-done.5, bf16[64,16,8,256]{3,2,1,0:T(8,128)(2,1)} %bitcast.83), kind=kOutput, calls=%fused_computation.17 | convolution fusion | flops 67117056 | bytes 4341760 | tf_op jit(solution)/shard_map/mrf,hmf->rh/dot_general | solution.py:139
  (51 shorter events, 1.0 us)
Async XLA Ops:
  0.6 21.1 %copy-start = (bf16[128,512]{1,0:T(8,128)(2,1)S(1)}, bf16[128,512]{1,0:T(8,128)(2,1)}, u32[]{:S(2)}) copy-start(bf16[128,512]{1,0:T(8,128)(2,1)} %param.5) | copy-start | bytes 393220
  4.2 24.9 %all-to-all-start.1 = ((bf16[16,16,256]{2,1,0:T(8,128)(2,1)}), bf16[16,16,256]{2,1,0:T(8,128)(2,1)S(1)}, u32[]{:S(2)}, u32[]{:S(2)}) async-start(bf16[16,16,256]{2,1,0:T(8,128)(2,1)} %bitcast.81), calls=%async_computation.1 | async-start | bytes 262144 | tf_op jit(solution)/shard_map/all_to_all | solution.py:64
  21.7 12.1 %copy-start.2 = (s32[1,8]{1,0:T(1,128)S(1)}, s32[1,8]{1,0:T(1,128)}, u32[]{:S(2)}) copy-start(s32[1,8]{1,0:T(1,128)} %param.8) | copy-start | bytes 100
  24.7 52.0 %copy-start.3 = (s32[128]{0:T(128)S(1)}, s32[128]{0:T(128)}, u32[]{:S(2)}) copy-start(s32[128]{0:T(128)} %param.9) | copy-start | bytes 1540
  29.1 35.2 %all-to-all-start = ((bf16[16,128,256]{2,1,0:T(8,128)(2,1)}), bf16[16,128,256]{2,1,0:T(8,128)(2,1)S(1)}, u32[]{:S(2)}, u32[]{:S(2)}) async-start(bf16[16,128,256]{2,1,0:T(8,128)(2,1)} %bitcast.79), calls=%async_computation | async-start | bytes 2097152 | tf_op jit(solution)/shard_map/all_to_all | solution.py:64
  33.8 3.0 %collective-permute-start.3 = (s32[1,8]{1,0:T(1,128)S(1)}, s32[1,8]{1,0:T(1,128)S(1)}, u32[]{:S(2)}, u32[]{:S(2)}) collective-permute-start(s32[1,8]{1,0:T(1,128)S(1)} %copy-done.2), channel_id=1, source_target_pairs={{0,8},{8,0},{1,9},{9,1},{2,10},{10,2},{3,11},{11,3},{4,12},{12,4},... | collective-permute-start | bytes 104 | tf_op jit(solution)/shard_map/ppermute | solution.py:55
  36.9 12.1 %collective-permute-start = (bf16[2,16,256]{2,1,0:T(8,128)(2,1)S(1)}, bf16[2,16,256]{2,1,0:T(8,128)(2,1)S(1)}, u32[]{:S(2)}, u32[]{:S(2)}) collective-permute-start(bf16[2,16,256]{2,1,0:T(8,128)(2,1)S(1)} %bitcast_reduce_fusion.1), channel_id=1, source_target_pairs={{0,1008},{16,0},{32,16},{48,32},{64,48},{80,64},{96,80},{112,96},{... | collective-permute-start | bytes 49160 | tf_op jit(solution)/shard_map/ppermute | solution.py:18
  49.0 5.5 %collective-permute-start.1 = (bf16[4,16,256]{2,1,0:T(8,128)(2,1)S(1)}, bf16[4,16,256]{2,1,0:T(8,128)(2,1)S(1)}, u32[]{:S(2)}, u32[]{:S(2)}) collective-permute-start(bf16[4,16,256]{2,1,0:T(8,128)(2,1)S(1)} %pad_maximum_fusion.2), channel_id=1, source_target_pairs={{0,992},{16,1008},{32,0},{48,16},{64,32},{80,48},{96,64},{112,80},... | collective-permute-start | bytes 98312 | tf_op jit(solution)/shard_map/ppermute | solution.py:18
  54.5 8.9 %collective-permute-start.2 = (bf16[8,16,256]{2,1,0:T(8,128)(2,1)S(1)}, bf16[8,16,256]{2,1,0:T(8,128)(2,1)S(1)}, u32[]{:S(2)}, u32[]{:S(2)}) collective-permute-start(bf16[8,16,256]{2,1,0:T(8,128)(2,1)S(1)} %pad_maximum_fusion.1), channel_id=1, source_target_pairs={{0,960},{16,976},{32,992},{48,1008},{64,0},{80,16},{96,32},{112,48... | collective-permute-start | bytes 196616 | tf_op jit(solution)/shard_map/ppermute | solution.py:18
  65.5 19.4 %all-to-all-start.2 = ((f32[16,24,128]{2,1,0:T(8,128)}), f32[16,24,128]{2,1,0:T(8,128)S(1)}, u32[]{:S(2)}, u32[]{:S(2)}) async-start(f32[16,24,128]{2,1,0:T(8,128)} %maximum_maximum_fusion), calls=%async_computation.2 | async-start | bytes 393216 | tf_op jit(solution)/shard_map/all_to_all | solution.py:87
  97.7 25.4 %copy-start.1 = (bf16[16,24,128]{2,1,0:T(8,128)(2,1)}, bf16[16,24,128]{2,1,0:T(8,128)(2,1)S(1)}, u32[]{:S(2)}) copy-start(bf16[16,24,128]{2,1,0:T(8,128)(2,1)S(1)} %all_to_all.30) | copy-start | bytes 294916
  98.4 13.7 %collective-permute-start.4 = (bf16[8,16,256]{2,1,0:T(8,128)(2,1)S(1)}, bf16[8,16,256]{2,1,0:T(8,128)(2,1)S(1)}, u32[]{:S(2)}, u32[]{:S(2)}) collective-permute-start(bf16[8,16,256]{2,1,0:T(8,128)(2,1)S(1)} %copy.90), channel_id=1, source_target_pairs={{0,16},{16,32},{32,48},{48,64},{64,80},{80,96},{96,112},{112,128},... | collective-permute-start | bytes 196616 | tf_op jit(solution)/shard_map/ppermute | solution.py:18
  104.6 31.5 %all-to-all-start.4 = ((bf16[16,128,256]{2,1,0:T(8,128)(2,1)}), bf16[16,128,256]{2,1,0:T(8,128)(2,1)S(1)}, u32[]{:S(2)}, u32[]{:S(2)}) async-start(bf16[16,128,256]{2,1,0:T(8,128)(2,1)} %bitcast.16), calls=%async_computation.4 | async-start | bytes 2097152 | tf_op jit(solution)/shard_map/all_to_all | solution.py:141
  112.1 9.0 %collective-permute-start.5 = (bf16[4,16,256]{2,1,0:T(8,128)(2,1)S(1)}, bf16[4,16,256]{2,1,0:T(8,128)(2,1)S(1)}, u32[]{:S(2)}, u32[]{:S(2)}) collective-permute-start(bf16[4,16,256]{2,1,0:T(8,128)(2,1)S(1)} %slice.145), channel_id=1, source_target_pairs={{0,32},{16,48},{32,64},{48,80},{64,96},{80,112},{96,128},{112,144}... | collective-permute-start | bytes 98312 | tf_op jit(solution)/shard_map/ppermute | solution.py:18
  121.1 10.5 %collective-permute-start.6 = (bf16[2,16,256]{2,1,0:T(8,128)(2,1)S(1)}, bf16[2,16,256]{2,1,0:T(8,128)(2,1)S(1)}, u32[]{:S(2)}, u32[]{:S(2)}) collective-permute-start(bf16[2,16,256]{2,1,0:T(8,128)(2,1)S(1)} %slice.146), channel_id=1, source_target_pairs={{0,64},{16,80},{32,96},{48,112},{64,128},{80,144},{96,160},{112,17... | collective-permute-start | bytes 49160 | tf_op jit(solution)/shard_map/ppermute | solution.py:18
  136.7 12.5 %all-to-all-start.5 = ((bf16[16,16,256]{2,1,0:T(8,128)(2,1)}), bf16[16,16,256]{2,1,0:T(8,128)(2,1)S(1)}, u32[]{:S(2)}, u32[]{:S(2)}) async-start(bf16[16,16,256]{2,1,0:T(8,128)(2,1)} %bitcast.21), calls=%async_computation.5 | async-start | bytes 262144 | tf_op jit(solution)/shard_map/all_to_all | solution.py:143

commit v11 on v8

--- a/solution.py
+++ b/solution.py
@@ -39,6 +39,48 @@
         out.append(top.astype(jnp.bfloat16))
         value = value - top
     return out
+
+
+def unproject_kernel(x_ref, w_ref, out_ref, sum_ref):
+    step = pl.program_id(0)
+    per, _, feats = x_ref.shape
+
+    @pl.when(step == 0)
+    def _():
+        sum_ref[...] = jnp.zeros_like(sum_ref)
+
+    total = sum_ref[...]
+    for j in range(per):
+        total += lax.dot_general(
+            w_ref[:, j * feats : (j + 1) * feats],
+            x_ref[j],
+            (((1,), (1,)), ((), ())),
+            preferred_element_type=jnp.float32,
+        )
+    sum_ref[...] = total
+
+    @pl.when(step == pl.num_programs(0) - 1)
+    def _():
+        out_ref[...] = total.T.astype(out_ref.dtype)
+
+
+def unproject_few(part, weight, steps=4):
+    members, rows, feats = part.shape
+    depth, width = weight.shape
+    return pl.pallas_call(
+        unproject_kernel,
+        grid=(steps,),
+        in_specs=[
+            pl.BlockSpec((members // steps, rows, feats), lambda g: (g, 0, 0)),
+            pl.BlockSpec((depth, width // steps), lambda g: (0, g)),
+        ],
+        out_specs=pl.BlockSpec((rows, depth), lambda g: (0, 0)),
+        out_shape=jax.ShapeDtypeStruct((rows, depth), jnp.bfloat16),
+        scratch_shapes=[pltpu.VMEM((depth, rows), jnp.float32)],
+        cost_estimate=pl.CostEstimate(
+            flops=2 * rows * depth * width, bytes_accessed=2 * depth * width, transcendentals=0
+        ),
+    )(part, weight)
 
 
 def on_device(q_ctx, p_ctx, out_weight, neighbours, positive):
@@ -137,7 +179,7 @@
 
     q_all = gather_features(dq)
     q_all, dp = lax.optimization_barrier((q_all, dp))
-    p_grad = unproject(gather_features(dp))
+    p_grad = unproject_few(gather_features(dp), out_weight)
     return unproject(q_all), p_grad, losses
 
 

time: 150 us -> 152 us (1.013)
  Pallas kernels: 1.28 us -> 5.8 us
  matrix products: 15 us -> 11.1 us
    pallas_call x0 -> x1, Pallas kernels: none -> 4.52 us  [unproject_few(): pl.pallas_call(unproject_kernel, grid=(steps,), in_specs=[pl.BlockSpec((m...]
    dot_general x2 -> x1, matrix products: 8.36 us -> 4.37 us  [unproject(): jnp.einsum('mrf,hmf->rh', part, weight, preferred_element_type=f32)]
where the time goes in v11:
time: 152 us; the launch traced here: 150 us
  starting transfers between devices  73.3 us (48%)
  waiting for transfers between devices  37.6 us (25%)
  blocking collectives  12.1 us (8%)
  matrix products  11.1 us (7%)
  local copies, waits for them, and re-layouts  6.74 us (4%)
  Pallas kernels  5.8 us (4%)
  other arithmetic  2.42 us (2%)
    ppermute x6, starting transfers between devices, shift_chips(): lax.ppermute(value, 'chip', [(i, (i + by) % chips) for i in range(chips)])  29.5 us
    all_to_all x2, starting transfers between devices, reduce_over_tensor(): got = lax.all_to_all(part, MEMBERS, 0, 0)  22.2 us
    ppermute x6, waiting for transfers between devices, shift_chips(): lax.ppermute(value, 'chip', [(i, (i + by) % chips) for i in range(chips)])  17.4 us
    all_to_all x1, blocking collectives, on_device(): lax.all_to_all(jnp.broadcast_to(told[None], (members,) + told.shape), MEM...  12.1 us
    all_to_all x1, starting transfers between devices, on_device(): lax.all_to_all(sums.reshape(members, q_part + 8, slots), MEMBERS, 0, 0)  10.1 us
    all_to_all x2, starting transfers between devices, gather_features(): lax.all_to_all(part.reshape((members,) + part.shape[2:]), MEMBERS, 0, 0)  9.41 us
    all_to_all x2, waiting for transfers between devices, gather_features(): lax.all_to_all(part.reshape((members,) + part.shape[2:]), MEMBERS, 0, 0)  8.71 us
    all_to_all x1, waiting for transfers between devices, on_device(): lax.all_to_all(sums.reshape(members, q_part + 8, slots), MEMBERS, 0, 0)  8.2 us
  transfers between devices with their start and end apart: 12, of which 9 were waited for; matrix products, arithmetic and copies ran while one was open for 9% of the time, Pallas kernels for 1%

profile of v11, /device:TPU:1, one launch (start us, length us, event | category | flops | bytes accessed | tf_op | source)
XLA Modules:
  0.0 150.0 jit_solution(10099147078722339529)
XLA Ops:
  0.6 2.9 %convolution_convert_fusion.1 = bf16[16,4096]{1,0:T(8,128)(2,1)S(1)} fusion(bf16[16,512]{1,0:T(8,128)(2,1)} %param.6, bf16[512,4096]{1,0:T(8,128)(2,1)} %w_ref.1), kind=kOutput, calls=%fused_computation.2 | convolution fusion | flops 67174400 | bytes 4341760 | tf_op jit(solution)/shard_map/dot_general | solution.py:102
  3.5 0.7 copy.59
  4.2 17.5 %all-to-all-start.1 = ((bf16[16,16,256]{2,1,0:T(8,128)(2,1)}), bf16[16,16,256]{2,1,0:T(8,128)(2,1)S(1)}, u32[]{:S(2)}, u32[]{:S(2)}) async-start(bf16[16,16,256]{2,1,0:T(8,128)(2,1)} %bitcast.70), calls=%async_computation.1 | async-start | bytes 262144 | tf_op jit(solution)/shard_map/all_to_all | solution.py:106
  21.7 2.9 %convolution_convert_fusion = bf16[128,4096]{1,0:T(8,128)(2,1)S(1)} fusion(bf16[128,512]{1,0:T(8,128)(2,1)S(1)} %copy-done, bf16[512,4096]{1,0:T(8,128)(2,1)} %w_ref.1), kind=kOutput, calls=%fused_computation.1 | convolution fusion | flops 537395200 | bytes 5373952 | tf_op jit(solution)/shard_map/dot_general | solution.py:102
  24.7 1.1 copy.58
  25.8 3.3 %all-to-all-done.1 = bf16[16,16,256]{2,1,0:T(8,128)(2,1)S(1)} async-done(((bf16[16,16,256]{2,1,0:T(8,128)(2,1)}), bf16[16,16,256]{2,1,0:T(8,128)(2,1)S(1)}, u32[]{:S(2)}, u32[]{:S(2)}) %all-to-all-start.1) | async-done | bytes 131104 | tf_op jit(solution)/shard_map/all_to_all | solution.py:106
  29.1 4.7 %all-to-all-start = ((bf16[16,128,256]{2,1,0:T(8,128)(2,1)}), bf16[16,128,256]{2,1,0:T(8,128)(2,1)S(1)}, u32[]{:S(2)}, u32[]{:S(2)}) async-start(bf16[16,128,256]{2,1,0:T(8,128)(2,1)} %bitcast.68), calls=%async_computation | async-start | bytes 2097152 | tf_op jit(solution)/shard_map/all_to_all | solution.py:106
  33.8 2.1 %collective-permute-start.3 = (s32[1,8]{1,0:T(1,128)S(1)}, s32[1,8]{1,0:T(1,128)S(1)}, u32[]{:S(2)}, u32[]{:S(2)}) collective-permute-start(s32[1,8]{1,0:T(1,128)S(1)} %copy-done.3), channel_id=1, source_target_pairs={{0,8},{8,0},{1,9},{9,1},{2,10},{10,2},{3,11},{11,3},{4,12},{12,4},... | collective-permute-start | bytes 104 | tf_op jit(solution)/shard_map/ppermute | solution.py:97
  36.0 11.2 %collective-permute-start = (bf16[2,16,256]{2,1,0:T(8,128)(2,1)S(1)}, bf16[2,16,256]{2,1,0:T(8,128)(2,1)S(1)}, u32[]{:S(2)}, u32[]{:S(2)}) collective-permute-start(bf16[2,16,256]{2,1,0:T(8,128)(2,1)S(1)} %bitcast_reduce_fusion.1), channel_id=1, source_target_pairs={{0,1008},{16,0},{32,16},{48,32},{64,48},{80,64},{96,80},{112,96},{... | collective-permute-start | bytes 49160 | tf_op jit(solution)/shard_map/ppermute | solution.py:18
  47.3 0.8 collective-permute-done
  48.1 3.9 %collective-permute-start.1 = (bf16[4,16,256]{2,1,0:T(8,128)(2,1)S(1)}, bf16[4,16,256]{2,1,0:T(8,128)(2,1)S(1)}, u32[]{:S(2)}, u32[]{:S(2)}) collective-permute-start(bf16[4,16,256]{2,1,0:T(8,128)(2,1)S(1)} %pad_maximum_fusion.2), channel_id=1, source_target_pairs={{0,992},{16,1008},{32,0},{48,16},{64,32},{80,48},{96,64},{112,80},... | collective-permute-start | bytes 98312 | tf_op jit(solution)/shard_map/ppermute | solution.py:18
  52.0 0.1 reshape.106
  52.1 1.8 %collective-permute-done.1 = bf16[4,16,256]{2,1,0:T(8,128)(2,1)S(1)} collective-permute-done((bf16[4,16,256]{2,1,0:T(8,128)(2,1)S(1)}, bf16[4,16,256]{2,1,0:T(8,128)(2,1)S(1)}, u32[]{:S(2)}, u32[]{:S(2)}) %collective-permute-start.1) | collective-permute-done | bytes 32800 | tf_op jit(solution)/shard_map/ppermute | solution.py:18
  54.0 3.9 %collective-permute-start.2 = (bf16[8,16,256]{2,1,0:T(8,128)(2,1)S(1)}, bf16[8,16,256]{2,1,0:T(8,128)(2,1)S(1)}, u32[]{:S(2)}, u32[]{:S(2)}) collective-permute-start(bf16[8,16,256]{2,1,0:T(8,128)(2,1)S(1)} %pad_maximum_fusion.1), channel_id=1, source_target_pairs={{0,960},{16,976},{32,992},{48,1008},{64,0},{80,16},{96,32},{112,48... | collective-permute-start | bytes 196616 | tf_op jit(solution)/shard_map/ppermute | solution.py:18
  57.9 5.8 %collective-permute-done.2 = bf16[8,16,256]{2,1,0:T(8,128)(2,1)S(1)} collective-permute-done((bf16[8,16,256]{2,1,0:T(8,128)(2,1)S(1)}, bf16[8,16,256]{2,1,0:T(8,128)(2,1)S(1)}, u32[]{:S(2)}, u32[]{:S(2)}) %collective-permute-start.2) | collective-permute-done | bytes 65568 | tf_op jit(solution)/shard_map/ppermute | solution.py:18
  63.7 0.6 gather_fusion
  64.2 0.1 multiply_reduce_fusion
  64.3 0.1 broadcast_in_dim.17
  64.4 0.1 bitcast_reduce_fusion
  64.6 0.1 fusion.11
  64.7 0.2 fusion.30
  65.0 0.8 maximum_maximum_fusion
  65.7 10.1 %all-to-all-start.2 = ((f32[16,24,128]{2,1,0:T(8,128)}), f32[16,24,128]{2,1,0:T(8,128)S(1)}, u32[]{:S(2)}, u32[]{:S(2)}) async-start(f32[16,24,128]{2,1,0:T(8,128)} %maximum_maximum_fusion), calls=%async_computation.2 | async-start | bytes 393216 | tf_op jit(solution)/shard_map/all_to_all | solution.py:129
  75.9 8.2 %all-to-all-done.2 = f32[16,24,128]{2,1,0:T(8,128)S(1)} async-done(((f32[16,24,128]{2,1,0:T(8,128)}), f32[16,24,128]{2,1,0:T(8,128)S(1)}, u32[]{:S(2)}, u32[]{:S(2)}) %all-to-all-start.2) | async-done | bytes 196640 | tf_op jit(solution)/shard_map/all_to_all | solution.py:129
  84.1 0.2 select_reduce_fusion
  84.3 0.2 fusion.18
  84.6 0.1 concatenate.38
  84.8 12.1 %all_to_all.30 = bf16[16,24,128]{2,1,0:T(8,128)(2,1)S(1)} all-to-all(bf16[16,24,128]{2,1,0:T(8,128)(2,1)S(1)} %broadcast_in_dim.21), channel_id=1, replica_groups=mesh['chip'=64,'core'=2,'tensor'=8] {'core','tensor'}, dimensions={0} | all-to-all | bytes 196608 | tf_op jit(solution)/shard_map/all_to_all | solution.py:150
  97.0 0.2 fusion.7
  97.2 0.3 convolution_bitcast_fusion
  97.5 1.9 %collective-permute-start.4 = (bf16[8,16,256]{2,0,1:T(8,128)(2,1)S(1)}, bf16[8,16,256]{2,0,1:T(8,128)(2,1)S(1)}, u32[]{:S(2)}, u32[]{:S(2)}) collective-permute-start(bf16[8,16,256]{2,0,1:T(8,128)(2,1)S(1)} %slice.147), channel_id=1, source_target_pairs={{0,64},{16,80},{32,96},{48,112},{64,128},{80,144},{96,160},{112,17... | collective-permute-start | bytes 196616 | tf_op jit(solution)/shard_map/ppermute | solution.py:18
  99.5 0.2 fusion.6
  99.7 1.1 broadcast_in_dim.22
  100.8 4.6 %all-to-all-start.4 = ((bf16[16,128,256]{2,1,0:T(8,128)(2,1)}), bf16[16,128,256]{2,1,0:T(8,128)(2,1)S(1)}, u32[]{:S(2)}, u32[]{:S(2)}) async-start(bf16[16,128,256]{2,1,0:T(8,128)(2,1)} %bitcast.16), calls=%async_computation.4 | async-start | bytes 2097152 | tf_op jit(solution)/shard_map/all_to_all | solution.py:174
  105.4 3.2 %collective-permute-done.4 = bf16[8,16,256]{2,0,1:T(8,128)(2,1)S(1)} collective-permute-done((bf16[8,16,256]{2,0,1:T(8,128)(2,1)S(1)}, bf16[8,16,256]{2,0,1:T(8,128)(2,1)S(1)}, u32[]{:S(2)}, u32[]{:S(2)}) %collective-permute-start.4) | collective-permute-done | bytes 65568 | tf_op jit(solution)/shard_map/ppermute | solution.py:18
  108.6 3.1 %collective-permute-start.5 = (bf16[4,16,256]{2,0,1:T(4,128)(2,1)S(1)}, bf16[4,16,256]{2,0,1:T(4,128)(2,1)S(1)}, u32[]{:S(2)}, u32[]{:S(2)}) collective-permute-start(bf16[4,16,256]{2,0,1:T(4,128)(2,1)S(1)} %slice.148), channel_id=1, source_target_pairs={{0,32},{16,48},{32,64},{48,80},{64,96},{80,112},{96,128},{112,144}... | collective-permute-start | bytes 98312 | tf_op jit(solution)/shard_map/ppermute | solution.py:18
  111.8 0.6 fusion.16.value_ref
  112.4 5.8 %collective-permute-done.5 = bf16[4,16,256]{2,0,1:T(4,128)(2,1)S(1)} collective-permute-done((bf16[4,16,256]{2,0,1:T(4,128)(2,1)S(1)}, bf16[4,16,256]{2,0,1:T(4,128)(2,1)S(1)}, u32[]{:S(2)}, u32[]{:S(2)}) %collective-permute-start.5) | collective-permute-done | bytes 32800 | tf_op jit(solution)/shard_map/ppermute | solution.py:18
  118.3 5.4 %collective-permute-start.6 = (bf16[2,16,256]{2,0,1:T(2,128)(2,1)S(1)}, bf16[2,16,256]{2,0,1:T(2,128)(2,1)S(1)}, u32[]{:S(2)}, u32[]{:S(2)}) collective-permute-start(bf16[2,16,256]{2,0,1:T(2,128)(2,1)S(1)} %slice.149), channel_id=1, source_target_pairs={{0,16},{16,32},{32,48},{48,64},{64,80},{80,96},{96,112},{112,128},... | collective-permute-start | bytes 49160 | tf_op jit(solution)/shard_map/ppermute | solution.py:18
  123.7 1.3 shard_map.77
  124.9 1.3 reshape.102
  126.2 5.8 %all-to-all-done.4 = bf16[16,128,256]{2,1,0:T(8,128)(2,1)S(1)} async-done(((bf16[16,128,256]{2,1,0:T(8,128)(2,1)}), bf16[16,128,256]{2,1,0:T(8,128)(2,1)S(1)}, u32[]{:S(2)}, u32[]{:S(2)}) %all-to-all-start.4) | async-done | bytes 1048608 | tf_op jit(solution)/shard_map/all_to_all | solution.py:174
  132.0 0.6 broadcast_in_dim.23
  132.7 4.8 %all-to-all-start.5 = ((bf16[16,16,256]{2,1,0:T(8,128)(2,1)}), bf16[16,16,256]{2,1,0:T(8,128)(2,1)S(1)}, u32[]{:S(2)}, u32[]{:S(2)}) async-start(bf16[16,16,256]{2,1,0:T(8,128)(2,1)} %bitcast.22), calls=%async_computation.5 | async-start | bytes 262144 | tf_op jit(solution)/shard_map/all_to_all | solution.py:174
  137.5 4.4 %fusion.8 = bf16[128,512]{1,0:T(8,128)(2,1)} fusion(bf16[16,128,256]{2,1,0:T(8,128)(2,1)S(1)} %all-to-all-done.4, bf16[64,16,8,256]{3,2,1,0:T(8,128)(2,1)} %bitcast.71), kind=kOutput, calls=%fused_computation.12 | convolution fusion | flops 536936448 | bytes 5373952 | tf_op jit(solution)/shard_map/mrf,hmf->rh/dot_general | solution.py:178
  141.9 2.9 %all-to-all-done.5.x_ref = bf16[16,16,256]{2,1,0:T(8,128)(2,1)S(1)} async-done(((bf16[16,16,256]{2,1,0:T(8,128)(2,1)}), bf16[16,16,256]{2,1,0:T(8,128)(2,1)S(1)}, u32[]{:S(2)}, u32[]{:S(2)}) %all-to-all-start.5) | async-done | bytes 131104 | tf_op jit(solution)/shard_map/all_to_all | solution.py:174
  144.8 0.6 copy-done.1
  145.4 4.5 %shard_map.76 = bf16[16,512]{1,0:T(8,128)(2,1)} custom-call(bf16[16,16,256]{2,1,0:T(8,128)(2,1)} %copy-done.1, bf16[512,4096]{1,0:T(8,128)(2,1)} %w_ref.1), custom_call_target="tpu_custom_call" | custom-call | flops 67108864 | bytes 4194304 | tf_op jit(solution)/shard_map/pallas_call | solution.py:70
  (51 shorter events, 0.8 us)
Async XLA Ops:
  0.6 21.1 %copy-start = (bf16[128,512]{1,0:T(8,128)(2,1)S(1)}, bf16[128,512]{1,0:T(8,128)(2,1)}, u32[]{:S(2)}) copy-start(bf16[128,512]{1,0:T(8,128)(2,1)} %param.5) | copy-start | bytes 393220
  4.2 24.9 %all-to-all-start.1 = ((bf16[16,16,256]{2,1,0:T(8,128)(2,1)}), bf16[16,16,256]{2,1,0:T(8,128)(2,1)S(1)}, u32[]{:S(2)}, u32[]{:S(2)}) async-start(bf16[16,16,256]{2,1,0:T(8,128)(2,1)} %bitcast.70), calls=%async_computation.1 | async-start | bytes 262144 | tf_op jit(solution)/shard_map/all_to_all | solution.py:106
  21.7 12.1 %copy-start.3 = (s32[1,8]{1,0:T(1,128)S(1)}, s32[1,8]{1,0:T(1,128)}, u32[]{:S(2)}) copy-start(s32[1,8]{1,0:T(1,128)} %param.8) | copy-start | bytes 100
  24.7 51.2 %copy-start.4 = (s32[128]{0:T(128)S(1)}, s32[128]{0:T(128)}, u32[]{:S(2)}) copy-start(s32[128]{0:T(128)} %param.9) | copy-start | bytes 1540
  29.1 35.4 %all-to-all-start = ((bf16[16,128,256]{2,1,0:T(8,128)(2,1)}), bf16[16,128,256]{2,1,0:T(8,128)(2,1)S(1)}, u32[]{:S(2)}, u32[]{:S(2)}) async-start(bf16[16,128,256]{2,1,0:T(8,128)(2,1)} %bitcast.68), calls=%async_computation | async-start | bytes 2097152 | tf_op jit(solution)/shard_map/all_to_all | solution.py:106
  33.8 13.4 %collective-permute-start.3 = (s32[1,8]{1,0:T(1,128)S(1)}, s32[1,8]{1,0:T(1,128)S(1)}, u32[]{:S(2)}, u32[]{:S(2)}) collective-permute-start(s32[1,8]{1,0:T(1,128)S(1)} %copy-done.3), channel_id=1, source_target_pairs={{0,8},{8,0},{1,9},{9,1},{2,10},{10,2},{3,11},{11,3},{4,12},{12,4},... | collective-permute-start | bytes 104 | tf_op jit(solution)/shard_map/ppermute | solution.py:97
  36.0 12.1 %collective-permute-start = (bf16[2,16,256]{2,1,0:T(8,128)(2,1)S(1)}, bf16[2,16,256]{2,1,0:T(8,128)(2,1)S(1)}, u32[]{:S(2)}, u32[]{:S(2)}) collective-permute-start(bf16[2,16,256]{2,1,0:T(8,128)(2,1)S(1)} %bitcast_reduce_fusion.1), channel_id=1, source_target_pairs={{0,1008},{16,0},{32,16},{48,32},{64,48},{80,64},{96,80},{112,96},{... | collective-permute-start | bytes 49160 | tf_op jit(solution)/shard_map/ppermute | solution.py:18
  48.1 5.8 %collective-permute-start.1 = (bf16[4,16,256]{2,1,0:T(8,128)(2,1)S(1)}, bf16[4,16,256]{2,1,0:T(8,128)(2,1)S(1)}, u32[]{:S(2)}, u32[]{:S(2)}) collective-permute-start(bf16[4,16,256]{2,1,0:T(8,128)(2,1)S(1)} %pad_maximum_fusion.2), channel_id=1, source_target_pairs={{0,992},{16,1008},{32,0},{48,16},{64,32},{80,48},{96,64},{112,80},... | collective-permute-start | bytes 98312 | tf_op jit(solution)/shard_map/ppermute | solution.py:18
  54.0 9.7 %collective-permute-start.2 = (bf16[8,16,256]{2,1,0:T(8,128)(2,1)S(1)}, bf16[8,16,256]{2,1,0:T(8,128)(2,1)S(1)}, u32[]{:S(2)}, u32[]{:S(2)}) collective-permute-start(bf16[8,16,256]{2,1,0:T(8,128)(2,1)S(1)} %pad_maximum_fusion.1), channel_id=1, source_target_pairs={{0,960},{16,976},{32,992},{48,1008},{64,0},{80,16},{96,32},{112,48... | collective-permute-start | bytes 196616 | tf_op jit(solution)/shard_map/ppermute | solution.py:18
  65.7 18.4 %all-to-all-start.2 = ((f32[16,24,128]{2,1,0:T(8,128)}), f32[16,24,128]{2,1,0:T(8,128)S(1)}, u32[]{:S(2)}, u32[]{:S(2)}) async-start(f32[16,24,128]{2,1,0:T(8,128)} %maximum_maximum_fusion), calls=%async_computation.2 | async-start | bytes 393216 | tf_op jit(solution)/shard_map/all_to_all | solution.py:129
  96.9 26.8 %copy-start.2 = (bf16[16,24,128]{2,1,0:T(8,128)(2,1)}, bf16[16,24,128]{2,1,0:T(8,128)(2,1)S(1)}, u32[]{:S(2)}) copy-start(bf16[16,24,128]{2,1,0:T(8,128)(2,1)S(1)} %all_to_all.30) | copy-start | bytes 294916
  97.5 11.1 %collective-permute-start.4 = (bf16[8,16,256]{2,0,1:T(8,128)(2,1)S(1)}, bf16[8,16,256]{2,0,1:T(8,128)(2,1)S(1)}, u32[]{:S(2)}, u32[]{:S(2)}) collective-permute-start(bf16[8,16,256]{2,0,1:T(8,128)(2,1)S(1)} %slice.147), channel_id=1, source_target_pairs={{0,64},{16,80},{32,96},{48,112},{64,128},{80,144},{96,160},{112,17... | collective-permute-start | bytes 196616 | tf_op jit(solution)/shard_map/ppermute | solution.py:18
  100.8 31.2 %all-to-all-start.4 = ((bf16[16,128,256]{2,1,0:T(8,128)(2,1)}), bf16[16,128,256]{2,1,0:T(8,128)(2,1)S(1)}, u32[]{:S(2)}, u32[]{:S(2)}) async-start(bf16[16,128,256]{2,1,0:T(8,128)(2,1)} %bitcast.16), calls=%async_computation.4 | async-start | bytes 2097152 | tf_op jit(solution)/shard_map/all_to_all | solution.py:174
  108.6 9.6 %collective-permute-start.5 = (bf16[4,16,256]{2,0,1:T(4,128)(2,1)S(1)}, bf16[4,16,256]{2,0,1:T(4,128)(2,1)S(1)}, u32[]{:S(2)}, u32[]{:S(2)}) collective-permute-start(bf16[4,16,256]{2,0,1:T(4,128)(2,1)S(1)} %slice.148), channel_id=1, source_target_pairs={{0,32},{16,48},{32,64},{48,80},{64,96},{80,112},{96,128},{112,144}... | collective-permute-start | bytes 98312 | tf_op jit(solution)/shard_map/ppermute | solution.py:18
  118.3 7.9 %collective-permute-start.6 = (bf16[2,16,256]{2,0,1:T(2,128)(2,1)S(1)}, bf16[2,16,256]{2,0,1:T(2,128)(2,1)S(1)}, u32[]{:S(2)}, u32[]{:S(2)}) collective-permute-start(bf16[2,16,256]{2,0,1:T(2,128)(2,1)S(1)} %slice.149), channel_id=1, source_target_pairs={{0,16},{16,32},{32,48},{48,64},{64,80},{80,96},{96,112},{112,128},... | collective-permute-start | bytes 49160 | tf_op jit(solution)/shard_map/ppermute | solution.py:18
  132.7 12.1 %all-to-all-start.5 = ((bf16[16,16,256]{2,1,0:T(8,128)(2,1)}), bf16[16,16,256]{2,1,0:T(8,128)(2,1)S(1)}, u32[]{:S(2)}, u32[]{:S(2)}) async-start(bf16[16,16,256]{2,1,0:T(8,128)(2,1)} %bitcast.22), calls=%async_computation.5 | async-start | bytes 262144 | tf_op jit(solution)/shard_map/all_to_all | solution.py:174
  144.8 0.6 copy-start.1

commit v12 on v8

--- a/solution.py
+++ b/solution.py
@@ -118,13 +118,14 @@
     dq = (dq - q_inner * q_pre.astype(f32)).astype(bf16)
     dc = jnp.einsum("kqc,kqf->kcf", coef, q_pre, preferred_element_type=f32)
     dc = (dc - c_inner * cand.astype(f32)).astype(bf16)
-    match = (jnp.arange(WINDOW * CORES, dtype=jnp.int32)[:, None, None] == spots[None]).astype(bf16)
+    far = spots // CORES
+    slot = (far // 4 * 4 + far % 2 * 2 + far // 2 % 2) * CORES + spots % CORES
+    match = (jnp.arange(WINDOW * CORES, dtype=jnp.int32)[:, None, None] == slot[None]).astype(bf16)
     dwin = jnp.einsum("wks,kspf->wpf", match, dc.reshape(CORES, listed, p_rows, feats), preferred_element_type=f32)
 
-    while reach > 1:
-        reach //= 2
-        away = shift_chips(dwin[CORES * reach :].astype(bf16), reach)
-        dwin = dwin[: CORES * reach] + away.astype(f32)
+    for by in (4, 1, 2):
+        half = dwin.shape[0] // 2
+        dwin = dwin[:half] + shift_chips(dwin[half:].astype(bf16), by).astype(f32)
     dp = dwin.astype(bf16)
 
     def gather_features(part):

time: 150 us -> 151 us (level)
    ppermute x6, waiting for transfers between devices: 17.4 us -> 20.6 us  [shift_chips(): lax.ppermute(value, 'chip', [(i, (i + by) % chips) for i in range(chips)])]
    all_to_all x2, waiting for transfers between devices: 8.71 us -> 5.71 us  [gather_features(): lax.all_to_all(part.reshape((members,) + part.shape[2:]), MEMBERS, 0, 0)]
  transfers between devices with their start and end apart: 12 -> 12, of which waited for: 9 -> 11; matrix products, arithmetic and copies ran while one was open for 9% -> 9% of each run, Pallas kernels for 1% -> 1%
where the time goes in v12:
time: 151 us; the launch traced here: 150 us
  starting transfers between devices  73 us (48%)
  waiting for transfers between devices  38.7 us (26%)
  matrix products  15 us (10%)
  blocking collectives  12.1 us (8%)
  local copies, waits for them, and re-layouts  6.11 us (4%)
  other arithmetic  2.45 us (2%)
    ppermute x6, starting transfers between devices, shift_chips(): lax.ppermute(value, 'chip', [(i, (i + by) % chips) for i in range(chips)])  28.5 us
    all_to_all x2, starting transfers between devices, reduce_over_tensor(): got = lax.all_to_all(part, MEMBERS, 0, 0)  22.2 us
    ppermute x6, waiting for transfers between devices, shift_chips(): lax.ppermute(value, 'chip', [(i, (i + by) % chips) for i in range(chips)])  20.6 us
    all_to_all x1, blocking collectives, on_device(): lax.all_to_all(jnp.broadcast_to(told[None], (members,) + told.shape), MEM...  12.1 us
    all_to_all x1, starting transfers between devices, on_device(): lax.all_to_all(sums.reshape(members, q_part + 8, slots), MEMBERS, 0, 0)  11.1 us
    all_to_all x2, starting transfers between devices, gather_features(): lax.all_to_all(part.reshape((members,) + part.shape[2:]), MEMBERS, 0, 0)  9.12 us
    dot_general x2, matrix products, unproject(): jnp.einsum('mrf,hmf->rh', part, weight, preferred_element_type=f32)  8.36 us
    all_to_all x1, waiting for transfers between devices, on_device(): lax.all_to_all(sums.reshape(members, q_part + 8, slots), MEMBERS, 0, 0)  8.2 us
  transfers between devices with their start and end apart: 12, of which 11 were waited for; matrix products, arithmetic and copies ran while one was open for 9% of the time, Pallas kernels for 1%

profile of v12, /device:TPU:1, one launch (start us, length us, event | category | flops | bytes accessed | tf_op | source)
XLA Modules:
  0.0 149.6 jit_solution(11265771449474111717)
XLA Ops:
  0.6 2.9 %convolution_convert_fusion.1 = bf16[16,4096]{1,0:T(8,128)(2,1)S(1)} fusion(bf16[16,512]{1,0:T(8,128)(2,1)} %param.6, bf16[512,4096]{1,0:T(8,128)(2,1)} %param.7), kind=kOutput, calls=%fused_computation.2 | convolution fusion | flops 67174400 | bytes 4341760 | tf_op jit(solution)/shard_map/dot_general | solution.py:60
  3.5 0.7 copy.70
  4.2 17.5 %all-to-all-start.1 = ((bf16[16,16,256]{2,1,0:T(8,128)(2,1)}), bf16[16,16,256]{2,1,0:T(8,128)(2,1)S(1)}, u32[]{:S(2)}, u32[]{:S(2)}) async-start(bf16[16,16,256]{2,1,0:T(8,128)(2,1)} %bitcast.81), calls=%async_computation.1 | async-start | bytes 262144 | tf_op jit(solution)/shard_map/all_to_all | solution.py:64
  21.7 2.9 %convolution_convert_fusion = bf16[128,4096]{1,0:T(8,128)(2,1)S(1)} fusion(bf16[128,512]{1,0:T(8,128)(2,1)S(1)} %copy-done, bf16[512,4096]{1,0:T(8,128)(2,1)} %param.7), kind=kOutput, calls=%fused_computation.1 | convolution fusion | flops 537395200 | bytes 5373952 | tf_op jit(solution)/shard_map/dot_general | solution.py:60
  24.7 1.1 copy.69
  25.8 3.3 %all-to-all-done.1 = bf16[16,16,256]{2,1,0:T(8,128)(2,1)S(1)} async-done(((bf16[16,16,256]{2,1,0:T(8,128)(2,1)}), bf16[16,16,256]{2,1,0:T(8,128)(2,1)S(1)}, u32[]{:S(2)}, u32[]{:S(2)}) %all-to-all-start.1) | async-done | bytes 131104 | tf_op jit(solution)/shard_map/all_to_all | solution.py:64
  29.1 4.7 %all-to-all-start = ((bf16[16,128,256]{2,1,0:T(8,128)(2,1)}), bf16[16,128,256]{2,1,0:T(8,128)(2,1)S(1)}, u32[]{:S(2)}, u32[]{:S(2)}) async-start(bf16[16,128,256]{2,1,0:T(8,128)(2,1)} %bitcast.79), calls=%async_computation | async-start | bytes 2097152 | tf_op jit(solution)/shard_map/all_to_all | solution.py:64
  33.8 2.1 %collective-permute-start.3 = (s32[1,8]{1,0:T(1,128)S(1)}, s32[1,8]{1,0:T(1,128)S(1)}, u32[]{:S(2)}, u32[]{:S(2)}) collective-permute-start(s32[1,8]{1,0:T(1,128)S(1)} %copy-done.2), channel_id=1, source_target_pairs={{0,8},{8,0},{1,9},{9,1},{2,10},{10,2},{3,11},{11,3},{4,12},{12,4},... | collective-permute-start | bytes 104 | tf_op jit(solution)/shard_map/ppermute | solution.py:55
  36.0 0.8 collective-permute-done.3
  36.9 11.2 %collective-permute-start = (bf16[2,16,256]{2,1,0:T(8,128)(2,1)S(1)}, bf16[2,16,256]{2,1,0:T(8,128)(2,1)S(1)}, u32[]{:S(2)}, u32[]{:S(2)}) collective-permute-start(bf16[2,16,256]{2,1,0:T(8,128)(2,1)S(1)} %bitcast_reduce_fusion.1), channel_id=1, source_target_pairs={{0,1008},{16,0},{32,16},{48,32},{64,48},{80,64},{96,80},{112,96},{... | collective-permute-start | bytes 49160 | tf_op jit(solution)/shard_map/ppermute | solution.py:18
  48.2 0.8 collective-permute-done
  49.0 3.9 %collective-permute-start.1 = (bf16[4,16,256]{2,1,0:T(8,128)(2,1)S(1)}, bf16[4,16,256]{2,1,0:T(8,128)(2,1)S(1)}, u32[]{:S(2)}, u32[]{:S(2)}) collective-permute-start(bf16[4,16,256]{2,1,0:T(8,128)(2,1)S(1)} %pad_maximum_fusion.2), channel_id=1, source_target_pairs={{0,992},{16,1008},{32,0},{48,16},{64,32},{80,48},{96,64},{112,80},... | collective-permute-start | bytes 98312 | tf_op jit(solution)/shard_map/ppermute | solution.py:18
  52.9 0.1 reshape.107
  53.0 1.5 %collective-permute-done.1 = bf16[4,16,256]{2,1,0:T(8,128)(2,1)S(1)} collective-permute-done((bf16[4,16,256]{2,1,0:T(8,128)(2,1)S(1)}, bf16[4,16,256]{2,1,0:T(8,128)(2,1)S(1)}, u32[]{:S(2)}, u32[]{:S(2)}) %collective-permute-start.1) | collective-permute-done | bytes 32800 | tf_op jit(solution)/shard_map/ppermute | solution.py:18
  54.5 4.2 %collective-permute-start.2 = (bf16[8,16,256]{2,1,0:T(8,128)(2,1)S(1)}, bf16[8,16,256]{2,1,0:T(8,128)(2,1)S(1)}, u32[]{:S(2)}, u32[]{:S(2)}) collective-permute-start(bf16[8,16,256]{2,1,0:T(8,128)(2,1)S(1)} %pad_maximum_fusion.1), channel_id=1, source_target_pairs={{0,960},{16,976},{32,992},{48,1008},{64,0},{80,16},{96,32},{112,48... | collective-permute-start | bytes 196616 | tf_op jit(solution)/shard_map/ppermute | solution.py:18
  58.7 4.7 %collective-permute-done.2 = bf16[8,16,256]{2,1,0:T(8,128)(2,1)S(1)} collective-permute-done((bf16[8,16,256]{2,1,0:T(8,128)(2,1)S(1)}, bf16[8,16,256]{2,1,0:T(8,128)(2,1)S(1)}, u32[]{:S(2)}, u32[]{:S(2)}) %collective-permute-start.2) | collective-permute-done | bytes 65568 | tf_op jit(solution)/shard_map/ppermute | solution.py:18
  63.5 0.6 gather_fusion
  64.0 0.1 multiply_reduce_fusion
  64.2 0.1 bitcast_reduce_fusion
  64.4 0.1 fusion.20
  64.5 0.2 fusion.44
  64.8 0.8 maximum_maximum_fusion
  65.5 11.1 %all-to-all-start.2 = ((f32[16,24,128]{2,1,0:T(8,128)}), f32[16,24,128]{2,1,0:T(8,128)S(1)}, u32[]{:S(2)}, u32[]{:S(2)}) async-start(f32[16,24,128]{2,1,0:T(8,128)} %maximum_maximum_fusion), calls=%async_computation.2 | async-start | bytes 393216 | tf_op jit(solution)/shard_map/all_to_all | solution.py:87
  76.7 8.2 %all-to-all-done.2 = f32[16,24,128]{2,1,0:T(8,128)S(1)} async-done(((f32[16,24,128]{2,1,0:T(8,128)}), f32[16,24,128]{2,1,0:T(8,128)S(1)}, u32[]{:S(2)}, u32[]{:S(2)}) %all-to-all-start.2) | async-done | bytes 196640 | tf_op jit(solution)/shard_map/all_to_all | solution.py:87
  85.0 0.2 select_reduce_fusion
  85.2 0.2 fusion.27
  85.4 0.1 concatenate.38
  85.6 12.1 %all_to_all.30 = bf16[16,24,128]{2,1,0:T(8,128)(2,1)S(1)} all-to-all(bf16[16,24,128]{2,1,0:T(8,128)(2,1)S(1)} %broadcast_in_dim.21), channel_id=1, replica_groups=mesh['chip'=64,'core'=2,'tensor'=8] {'core','tensor'}, dimensions={0} | all-to-all | bytes 196608 | tf_op jit(solution)/shard_map/all_to_all | solution.py:108
  97.8 0.2 fusion.10
  98.1 0.3 convolution_bitcast_fusion
  98.4 1.9 %collective-permute-start.4 = (bf16[8,16,256]{2,0,1:T(8,128)(2,1)S(1)}, bf16[8,16,256]{2,0,1:T(8,128)(2,1)S(1)}, u32[]{:S(2)}, u32[]{:S(2)}) collective-permute-start(bf16[8,16,256]{2,0,1:T(8,128)(2,1)S(1)} %slice.147), channel_id=1, source_target_pairs={{0,64},{16,80},{32,96},{48,112},{64,128},{80,144},{96,160},{112,17... | collective-permute-start | bytes 196616 | tf_op jit(solution)/shard_map/ppermute | solution.py:18
  100.4 0.2 fusion.9
  100.6 1.1 broadcast_in_dim.22
  101.7 4.6 %all-to-all-start.4 = ((bf16[16,128,256]{2,1,0:T(8,128)(2,1)}), bf16[16,128,256]{2,1,0:T(8,128)(2,1)S(1)}, u32[]{:S(2)}, u32[]{:S(2)}) async-start(bf16[16,128,256]{2,1,0:T(8,128)(2,1)} %bitcast.16), calls=%async_computation.4 | async-start | bytes 2097152 | tf_op jit(solution)/shard_map/all_to_all | solution.py:133
  106.2 3.2 %collective-permute-done.4 = bf16[8,16,256]{2,0,1:T(8,128)(2,1)S(1)} collective-permute-done((bf16[8,16,256]{2,0,1:T(8,128)(2,1)S(1)}, bf16[8,16,256]{2,0,1:T(8,128)(2,1)S(1)}, u32[]{:S(2)}, u32[]{:S(2)}) %collective-permute-start.4) | collective-permute-done | bytes 65568 | tf_op jit(solution)/shard_map/ppermute | solution.py:18
  109.5 5.3 %collective-permute-start.5 = (bf16[4,16,256]{2,0,1:T(4,128)(2,1)S(1)}, bf16[4,16,256]{2,0,1:T(4,128)(2,1)S(1)}, u32[]{:S(2)}, u32[]{:S(2)}) collective-permute-start(bf16[4,16,256]{2,0,1:T(4,128)(2,1)S(1)} %slice.148), channel_id=1, source_target_pairs={{0,16},{16,32},{32,48},{48,64},{64,80},{80,96},{96,112},{112,128},... | collective-permute-start | bytes 98312 | tf_op jit(solution)/shard_map/ppermute | solution.py:18
  114.8 0.6 fusion.25.value_ref
  115.4 6.2 %collective-permute-done.5 = bf16[4,16,256]{2,0,1:T(4,128)(2,1)S(1)} collective-permute-done((bf16[4,16,256]{2,0,1:T(4,128)(2,1)S(1)}, bf16[4,16,256]{2,0,1:T(4,128)(2,1)S(1)}, u32[]{:S(2)}, u32[]{:S(2)}) %collective-permute-start.5) | collective-permute-done | bytes 32800 | tf_op jit(solution)/shard_map/ppermute | solution.py:18
  121.6 1.9 %collective-permute-start.6 = (bf16[2,16,256]{2,0,1:T(2,128)(2,1)S(1)}, bf16[2,16,256]{2,0,1:T(2,128)(2,1)S(1)}, u32[]{:S(2)}, u32[]{:S(2)}) collective-permute-start(bf16[2,16,256]{2,0,1:T(2,128)(2,1)S(1)} %slice.149), channel_id=1, source_target_pairs={{0,32},{16,48},{32,64},{48,80},{64,96},{80,112},{96,128},{112,144}... | collective-permute-start | bytes 49160 | tf_op jit(solution)/shard_map/ppermute | solution.py:18
  123.6 1.3 shard_map.76
  124.8 1.3 reshape.103
  126.1 4.2 %collective-permute-done.6 = bf16[2,16,256]{2,0,1:T(2,128)(2,1)S(1)} collective-permute-done((bf16[2,16,256]{2,0,1:T(2,128)(2,1)S(1)}, bf16[2,16,256]{2,0,1:T(2,128)(2,1)S(1)}, u32[]{:S(2)}, u32[]{:S(2)}) %collective-permute-start.6) | collective-permute-done | bytes 16416 | tf_op jit(solution)/shard_map/ppermute | solution.py:18
  130.4 2.8 %all-to-all-done.4 = bf16[16,128,256]{2,1,0:T(8,128)(2,1)S(1)} async-done(((bf16[16,128,256]{2,1,0:T(8,128)(2,1)}), bf16[16,128,256]{2,1,0:T(8,128)(2,1)S(1)}, u32[]{:S(2)}, u32[]{:S(2)}) %all-to-all-start.4) | async-done | bytes 1048608 | tf_op jit(solution)/shard_map/all_to_all | solution.py:133
  133.2 0.6 broadcast_in_dim.23
  133.8 4.5 %all-to-all-start.5 = ((bf16[16,16,256]{2,1,0:T(8,128)(2,1)}), bf16[16,16,256]{2,1,0:T(8,128)(2,1)S(1)}, u32[]{:S(2)}, u32[]{:S(2)}) async-start(bf16[16,16,256]{2,1,0:T(8,128)(2,1)} %bitcast.22), calls=%async_computation.5 | async-start | bytes 262144 | tf_op jit(solution)/shard_map/all_to_all | solution.py:133
  138.3 4.4 %fusion.11 = bf16[128,512]{1,0:T(8,128)(2,1)} fusion(bf16[16,128,256]{2,1,0:T(8,128)(2,1)S(1)} %all-to-all-done.4, bf16[64,16,8,256]{3,2,1,0:T(8,128)(2,1)} %bitcast.82), kind=kOutput, calls=%fused_computation.15 | convolution fusion | flops 536936448 | bytes 5373952 | tf_op jit(solution)/shard_map/mrf,hmf->rh/dot_general | solution.py:137
  142.7 2.9 %all-to-all-done.5 = bf16[16,16,256]{2,1,0:T(8,128)(2,1)S(1)} async-done(((bf16[16,16,256]{2,1,0:T(8,128)(2,1)}), bf16[16,16,256]{2,1,0:T(8,128)(2,1)S(1)}, u32[]{:S(2)}, u32[]{:S(2)}) %all-to-all-start.5) | async-done | bytes 131104 | tf_op jit(solution)/shard_map/all_to_all | solution.py:133
  145.6 4.0 %fusion.17 = bf16[16,512]{1,0:T(8,128)(2,1)} fusion(bf16[16,16,256]{2,1,0:T(8,128)(2,1)S(1)} %all-to-all-done.5, bf16[64,16,8,256]{3,2,1,0:T(8,128)(2,1)} %bitcast.83), kind=kOutput, calls=%fused_computation.17 | convolution fusion | flops 67117056 | bytes 4341760 | tf_op jit(solution)/shard_map/mrf,hmf->rh/dot_general | solution.py:137
  (50 shorter events, 1.0 us)
Async XLA Ops:
  0.6 21.1 %copy-start = (bf16[128,512]{1,0:T(8,128)(2,1)S(1)}, bf16[128,512]{1,0:T(8,128)(2,1)}, u32[]{:S(2)}) copy-start(bf16[128,512]{1,0:T(8,128)(2,1)} %param.5) | copy-start | bytes 393220
  4.2 24.9 %all-to-all-start.1 = ((bf16[16,16,256]{2,1,0:T(8,128)(2,1)}), bf16[16,16,256]{2,1,0:T(8,128)(2,1)S(1)}, u32[]{:S(2)}, u32[]{:S(2)}) async-start(bf16[16,16,256]{2,1,0:T(8,128)(2,1)} %bitcast.81), calls=%async_computation.1 | async-start | bytes 262144 | tf_op jit(solution)/shard_map/all_to_all | solution.py:64
  21.7 12.1 %copy-start.2 = (s32[1,8]{1,0:T(1,128)S(1)}, s32[1,8]{1,0:T(1,128)}, u32[]{:S(2)}) copy-start(s32[1,8]{1,0:T(1,128)} %param.8) | copy-start | bytes 100
  24.7 52.0 %copy-start.3 = (s32[128]{0:T(128)S(1)}, s32[128]{0:T(128)}, u32[]{:S(2)}) copy-start(s32[128]{0:T(128)} %param.9) | copy-start | bytes 1540
  29.1 35.2 %all-to-all-start = ((bf16[16,128,256]{2,1,0:T(8,128)(2,1)}), bf16[16,128,256]{2,1,0:T(8,128)(2,1)S(1)}, u32[]{:S(2)}, u32[]{:S(2)}) async-start(bf16[16,128,256]{2,1,0:T(8,128)(2,1)} %bitcast.79), calls=%async_computation | async-start | bytes 2097152 | tf_op jit(solution)/shard_map/all_to_all | solution.py:64
  33.8 3.0 %collective-permute-start.3 = (s32[1,8]{1,0:T(1,128)S(1)}, s32[1,8]{1,0:T(1,128)S(1)}, u32[]{:S(2)}, u32[]{:S(2)}) collective-permute-start(s32[1,8]{1,0:T(1,128)S(1)} %copy-done.2), channel_id=1, source_target_pairs={{0,8},{8,0},{1,9},{9,1},{2,10},{10,2},{3,11},{11,3},{4,12},{12,4},... | collective-permute-start | bytes 104 | tf_op jit(solution)/shard_map/ppermute | solution.py:55
  36.9 12.1 %collective-permute-start = (bf16[2,16,256]{2,1,0:T(8,128)(2,1)S(1)}, bf16[2,16,256]{2,1,0:T(8,128)(2,1)S(1)}, u32[]{:S(2)}, u32[]{:S(2)}) collective-permute-start(bf16[2,16,256]{2,1,0:T(8,128)(2,1)S(1)} %bitcast_reduce_fusion.1), channel_id=1, source_target_pairs={{0,1008},{16,0},{32,16},{48,32},{64,48},{80,64},{96,80},{112,96},{... | collective-permute-start | bytes 49160 | tf_op jit(solution)/shard_map/ppermute | solution.py:18
  49.0 5.5 %collective-permute-start.1 = (bf16[4,16,256]{2,1,0:T(8,128)(2,1)S(1)}, bf16[4,16,256]{2,1,0:T(8,128)(2,1)S(1)}, u32[]{:S(2)}, u32[]{:S(2)}) collective-permute-start(bf16[4,16,256]{2,1,0:T(8,128)(2,1)S(1)} %pad_maximum_fusion.2), channel_id=1, source_target_pairs={{0,992},{16,1008},{32,0},{48,16},{64,32},{80,48},{96,64},{112,80},... | collective-permute-start | bytes 98312 | tf_op jit(solution)/shard_map/ppermute | solution.py:18
  54.5 8.9 %collective-permute-start.2 = (bf16[8,16,256]{2,1,0:T(8,128)(2,1)S(1)}, bf16[8,16,256]{2,1,0:T(8,128)(2,1)S(1)}, u32[]{:S(2)}, u32[]{:S(2)}) collective-permute-start(bf16[8,16,256]{2,1,0:T(8,128)(2,1)S(1)} %pad_maximum_fusion.1), channel_id=1, source_target_pairs={{0,960},{16,976},{32,992},{48,1008},{64,0},{80,16},{96,32},{112,48... | collective-permute-start | bytes 196616 | tf_op jit(solution)/shard_map/ppermute | solution.py:18
  65.5 19.4 %all-to-all-start.2 = ((f32[16,24,128]{2,1,0:T(8,128)}), f32[16,24,128]{2,1,0:T(8,128)S(1)}, u32[]{:S(2)}, u32[]{:S(2)}) async-start(f32[16,24,128]{2,1,0:T(8,128)} %maximum_maximum_fusion), calls=%async_computation.2 | async-start | bytes 393216 | tf_op jit(solution)/shard_map/all_to_all | solution.py:87
  97.7 25.9 %copy-start.1 = (bf16[16,24,128]{2,1,0:T(8,128)(2,1)}, bf16[16,24,128]{2,1,0:T(8,128)(2,1)S(1)}, u32[]{:S(2)}) copy-start(bf16[16,24,128]{2,1,0:T(8,128)(2,1)S(1)} %all_to_all.30) | copy-start | bytes 294916
  98.4 11.0 %collective-permute-start.4 = (bf16[8,16,256]{2,0,1:T(8,128)(2,1)S(1)}, bf16[8,16,256]{2,0,1:T(8,128)(2,1)S(1)}, u32[]{:S(2)}, u32[]{:S(2)}) collective-permute-start(bf16[8,16,256]{2,0,1:T(8,128)(2,1)S(1)} %slice.147), channel_id=1, source_target_pairs={{0,64},{16,80},{32,96},{48,112},{64,128},{80,144},{96,160},{112,17... | collective-permute-start | bytes 196616 | tf_op jit(solution)/shard_map/ppermute | solution.py:18
  101.7 31.5 %all-to-all-start.4 = ((bf16[16,128,256]{2,1,0:T(8,128)(2,1)}), bf16[16,128,256]{2,1,0:T(8,128)(2,1)S(1)}, u32[]{:S(2)}, u32[]{:S(2)}) async-start(bf16[16,128,256]{2,1,0:T(8,128)(2,1)} %bitcast.16), calls=%async_computation.4 | async-start | bytes 2097152 | tf_op jit(solution)/shard_map/all_to_all | solution.py:133
  109.5 12.1 %collective-permute-start.5 = (bf16[4,16,256]{2,0,1:T(4,128)(2,1)S(1)}, bf16[4,16,256]{2,0,1:T(4,128)(2,1)S(1)}, u32[]{:S(2)}, u32[]{:S(2)}) collective-permute-start(bf16[4,16,256]{2,0,1:T(4,128)(2,1)S(1)} %slice.148), channel_id=1, source_target_pairs={{0,16},{16,32},{32,48},{48,64},{64,80},{80,96},{96,112},{112,128},... | collective-permute-start | bytes 98312 | tf_op jit(solution)/shard_map/ppermute | solution.py:18
  121.6 8.7 %collective-permute-start.6 = (bf16[2,16,256]{2,0,1:T(2,128)(2,1)S(1)}, bf16[2,16,256]{2,0,1:T(2,128)(2,1)S(1)}, u32[]{:S(2)}, u32[]{:S(2)}) collective-permute-start(bf16[2,16,256]{2,0,1:T(2,128)(2,1)S(1)} %slice.149), channel_id=1, source_target_pairs={{0,32},{16,48},{32,64},{48,80},{64,96},{80,112},{96,128},{112,144}... | collective-permute-start | bytes 49160 | tf_op jit(solution)/shard_map/ppermute | solution.py:18
  133.8 11.8 %all-to-all-start.5 = ((bf16[16,16,256]{2,1,0:T(8,128)(2,1)}), bf16[16,16,256]{2,1,0:T(8,128)(2,1)S(1)}, u32[]{:S(2)}, u32[]{:S(2)}) async-start(bf16[16,16,256]{2,1,0:T(8,128)(2,1)} %bitcast.22), calls=%async_computation.5 | async-start | bytes 262144 | tf_op jit(solution)/shard_map/all_to_all | solution.py:133
